TPU v7x, 128 devices: a whole 4x4x4 slice. The times are simulated.
128 devices in a mesh: ch: 4 (over x_hi, core), tile: 32 (over y, x_lo, z).
Axes of the slice: x: 4 (x_hi: 2, x_lo: 2; x = x_hi * 2 + x_lo), y: 4, z: 4, core: 2. Of those that a mesh axis runs over, the one named last changes fastest.
Arguments:
- latent: bfloat16 [2, 8, 32, 8, 30, 512], P(None, None, 'tile', None, None, 'ch'), may hold values from -6 to 6
- expand_weight: bfloat16 [512, 2, 2048], P('tile', None, 'ch'), may hold values from -0.25 to 0.25
- depth_kernel: float32 [3, 3, 3, 2, 2048], P(None, None, None, None, 'ch'), may hold values from -1.25 to 1.25
- project_weight: bfloat16 [2048, 512], P('ch', 'tile'), may hold values from -0.125 to 0.125
Outputs:
- decoded: bfloat16 [2, 8, 32, 8, 30, 512], P(None, 'ch', 'tile')
All inputs are finite; a program needn't handle non-finite values.
Results may differ from a plain program's by a relative error of at most 0.009.
Values may be sent and summed in bfloat16 or wider, within the bound.
No kernel may reach another device: no remote copies, remote signals or barrier semaphores. Data moves between devices by JAX's collectives and lax.ppermute only.
A program may use at most 192 MiB of HBM per device.

v0:
```python
import jax
import jax.numpy as jnp
from jax import lax
from jax.sharding import PartitionSpec as P

GC = 4


def shifted(shard, axis, by):
    size = lax.axis_size(axis)
    pairs = [(i, i + by) for i in range(size) if 0 <= i + by < size]
    return lax.ppermute(shard, axis, pairs)


def depthwise(padded_space, kernel):
    padded_all = jnp.pad(padded_space, ((0, 0), (1, 1), (0, 0), (0, 0), (0, 0), (0, 0)))
    frame_count = padded_all.shape[1] - 2
    row_count = padded_all.shape[2] - 2
    column_count = padded_all.shape[3] - 2
    accumulated = jnp.zeros(
        padded_all.shape[:1] + (frame_count, row_count, column_count) + padded_all.shape[4:],
        jnp.float32,
    )
    for i in range(3):
        for j in range(3):
            for l in range(3):
                window = padded_all[:, i : i + frame_count, j : j + row_count, l : l + column_count]
                accumulated = accumulated + window.astype(jnp.float32) * kernel[i, j, l]
    return accumulated


def grid_rim(field, move_columns, move_rows):
    position = lax.axis_index("tile") % GC
    from_left = move_columns(field[:, :, :, -1:], 1)
    from_right = move_columns(field[:, :, :, :1], -1)
    from_left = jnp.where(position > 0, from_left, jnp.zeros_like(from_left))
    from_right = jnp.where(position < GC - 1, from_right, jnp.zeros_like(from_right))
    widened = jnp.concatenate([from_left, field, from_right], axis=3)
    from_above = move_rows(widened[:, :, -1:], GC)
    from_below = move_rows(widened[:, :, :1], -GC)
    return jnp.concatenate([from_above, widened, from_below], axis=2)


def expand_block(source, expand_weight):
    before = jnp.einsum(
        "bfhwc,cgk->bfhwgk",
        source,
        lax.all_gather(expand_weight, "tile", axis=0, tiled=True),
        preferred_element_type=jnp.float32,
    )
    return jax.nn.silu(before).astype(jnp.bfloat16)


def on_device(latent, expand_weight, depth_kernel, project_weight):
    gathered = lax.all_gather(latent, "ch", axis=5, tiled=True)[:, :, 0]
    expanded = expand_block(gathered, expand_weight)
    padded = grid_rim(
        expanded,
        lambda piece, by: shifted(piece, "tile", by),
        lambda piece, by: shifted(piece, "tile", by),
    )
    filtered = depthwise(padded, depth_kernel)
    hidden = (filtered[..., 0, :] * jax.nn.silu(filtered[..., 1, :])).astype(jnp.bfloat16)
    partial_value = jnp.dot(
        hidden,
        lax.all_gather(project_weight, "tile", axis=1, tiled=True),
        preferred_element_type=jnp.float32,
    )
    groups = lax.axis_size("ch")
    frame_share = gathered.shape[1] // groups
    own_latent = lax.dynamic_slice_in_dim(
        gathered, lax.axis_index("ch") * frame_share, frame_share, 1
    )
    channel_sums = lax.psum_scatter(
        partial_value.astype(jnp.bfloat16), "ch", scatter_dimension=4, tiled=True
    ).astype(jnp.float32)
    summed = lax.all_to_all(
        channel_sums.astype(jnp.bfloat16), "ch", split_axis=1, concat_axis=4, tiled=True
    ).astype(channel_sums.dtype)
    result = (own_latent.astype(jnp.float32) + summed).astype(jnp.bfloat16)
    return result[:, :, None]


def solution(mesh):
    return jax.shard_map(
        on_device,
        mesh=mesh,
        in_specs=(
            P(None, None, "tile", None, None, "ch"),
            P("tile", None, "ch"),
            P(None, None, None, None, "ch"),
            P("ch", "tile"),
        ),
        out_specs=P(None, "ch", "tile", None, None, None),
        check_vma=False,
    )
```

profile of v0, /device:TPU:1, one launch (start us, length us, event | category | flops | bytes accessed | tf_op | source)
XLA Modules:
  0.0 627.6 jit_solution(2927116330658585380)
XLA Ops:
  6.5 0.0 all-gather.5.cloned.1.call-start
  6.5 1.4 copy.30
  7.9 0.0 all-gather.5.cloned.1.call-update
  7.9 0.0 all-gather.3.cloned.1.call-start
  8.0 0.7 all-gather.3.cloned.1.call-update
  8.7 0.0 reduce-scatter.4.cloned.1.call-start
  8.7 133.3 %all-gather.5.cloned.1.call-done = bf16[512,2,512]{2,0,1:T(8,128)(2,1)} async-done(((bf16[16,2,512]{2,0,1:T(8,128)(2,1)}), bf16[512,2,512]{2,0,1:T(8,128)(2,1)}) %all-gather.5.cloned.1.call-update) | async-done | bytes 1048592 | tf_op jit(solution)/shard_map/all_gather | solution.py:48
  142.0 61.1 %all-gather.3.cloned.1.call-done = bf16[2,8,1,8,30,512]{5,3,4,2,1,0:T(8,128)(2,1)} async-done(((bf16[2,8,1,8,30,128]{5,3,4,2,1,0:T(8,128)(2,1)}), bf16[2,8,1,8,30,512]{5,3,4,2,1,0:T(8,128)(2,1)}) %all-gather.3.cloned.1.call-update) | async-done | bytes 3932176 | tf_op jit(solution)/shard_map/all_gather | solution.py:55
  203.1 0.0 copy-start.2
  203.1 0.0 copy-start.3
  203.1 8.9 %multiply_convert_fusion = bf16[2,8,8,30,2,512]{5,3,4,2,1,0:T(8,128)(2,1)S(1)} fusion(bf16[2,8,8,30,512,1]{4,2,3,1,0,5:T(8,128)(2,1)} %bitcast.101, bf16[512,2,512]{2,0,1:T(8,128)(2,1)} %all-gather.5.cloned.1.call-done), kind=kOutput, calls=%fused_computation.4 | convolution fusion | flops 4046192640 | bytes 12845056 | tf_op jit(solution)/shard_map/bfhwc,cgk->bfhwgk/dot_general | solution.py:45
  212.0 0.0 copy-start
  212.0 3.2 copy-done
  215.3 1.2 fusion.18
  216.4 3.2 collective-permute-start
  219.7 1.3 collective-permute-start.1
  221.0 0.0 copy-start.1
  221.0 9.7 %collective-permute-done = bf16[2,8,8,1,2,512]{5,3,4,2,1,0:T(2,128)(2,1)S(1)} collective-permute-done((bf16[2,8,8,1,2,512]{5,3,4,2,1,0:T(2,128)(2,1)S(1)}, bf16[2,8,8,1,2,512]{5,3,4,2,1,0:T(2,128)(2,1)S(1)}, u32[]{:S(2)}, u32[]{:S(2)}) %collective-permute-start) | collective-permute-done | bytes 262176 | tf_op jit(solution)/shard_map/ppermute | solution.py:12
  230.7 0.6 broadcast_select_fusion.1
  231.2 3.3 collective-permute-done.1
  234.5 0.6 broadcast_select_fusion
  235.1 2.9 pad_maximum_fusion.5
  238.0 2.3 collective-permute-start.2
  240.3 1.3 collective-permute-start.3
  241.6 0.0 copy-done.2
  241.7 0.0 copy-done.3
  241.7 100.1 %all_gather.11 = bf16[512,512]{0,1:T(8,128)(2,1)S(1)} all-gather(bf16[512,16]{0,1:T(8,128)(2,1)S(1)} %copy-done.3), channel_id=1, replica_groups=mesh['ch'=4,'tile'=32] {'tile'}, dimensions={1}, use_global_device_ids=true | all-gather | bytes 540672 | tf_op jit(solution)/shard_map/all_gather | solution.py:66
  341.8 0.0 collective-permute-done.2
  341.8 0.0 collective-permute-done.3
  341.8 0.0 copy-done.1
  341.8 18.9 %maximum_maximum_fusion = (bf16[2,8,9,32,2,512]{5,3,4,2,1,0:T(8,128)(2,1)}, bf16[2,8,9,32,2,512]{5,3,4,2,1,0:T(8,128)(2,1)}) fusion(bf16[2,8,8,1,2,512]{5,3,4,2,1,0:T(2,128)(2,1)S(1)} %broadcast_select_fusion, bf16[2,8,8,30,2,512]{5,3,4,2,1,0:T(8,128)(2,1)S(1)} %copy-done.1, bf16[2,8,8,1,2,512]{5,3,4,2,1,0:T(2,128)(2,1)S(1)} %broadcast_select_fusion.1, ...), kind=kLoop, calls=%fused_computation.12 | loop fusion | flops 75497472 | bytes 29360128 | tf_op jit(solution)/shard_map/concatenate | solution.py:41
  360.7 7.6 %select_maximum_fusion = bf16[2,10,10,32,2,512]{5,3,4,2,1,0:T(8,128)(2,1)} fusion(bf16[2,8,1,32,2,512]{5,3,4,2,1,0:T(8,128)(2,1)S(1)} %collective-permute-done.3, bf16[2,8,1,32,2,512]{5,3,4,2,1,0:T(8,128)(2,1)S(1)} %collective-permute-done.2, bf16[2,8,8,1,2,512]{5,3,4,2,1,0:T(2,128)(2,1)S(1)} %broadcast_select_fusion, ...), kind=kLoop, calls=%fused_computation.5 | loop fusion | flops 117964800 | bytes 23592960 | tf_op jit(solution)/shard_map/concatenate | solution.py:41
  368.3 91.4 %multiply_add_fusion = f32[2,8,8,30,2,512]{5,3,4,2,1,0:T(8,128)} fusion(bf16[2,8,8,30,2,512]{5,3,4,2,1,0:T(8,128)(2,1)} %copy-done, bf16[2,10,10,32,2,512]{5,3,4,2,1,0:T(8,128)(2,1)} %select_maximum_fusion, bf16[2,8,9,32,2,512]{5,3,4,2,1,0:T(8,128)(2,1)} %get-tuple-element.6, bf16[2,8,8,1,2,512]{5,3,4,2,1,0:T(2,128)(2,1)S(1)} %broadcast_select_fusion, ...), kind=kLoop, calls=%fused_computation.3 | loop fusion | flops 338165760 | bytes 212971520 | tf_op jit(solution)/shard_map/add | solution.py:28
  459.7 10.4 %fusion.11 = bf16[2,8,8,30,512]{4,3,2,1,0:T(8,128)(2,1)} fusion(f32[2,8,8,30,2,512]{5,3,4,2,1,0:T(8,128)} %multiply_add_fusion, bf16[512,512]{0,1:T(8,128)(2,1)S(1)} %all_gather.11), kind=kOutput, calls=%fused_computation.22 | convolution fusion | flops 2027028480 | bytes 20185088 | tf_op jit(solution)/shard_map/dot_general | solution.py:64
  470.0 24.9 %copy.41 = bf16[2,8,8,30,512]{3,2,1,0,4:T(8,128)(2,1)} copy(bf16[2,8,8,30,512]{4,3,2,1,0:T(8,128)(2,1)} %fusion.11) | data formatting | bytes 7864320
  495.0 24.7 %reshape.47 = bf16[512,3840]{1,0:T(8,128)(2,1)} reshape(bf16[512,2,8,8,30]{4,3,2,1,0:T(8,128)(2,1)} %bitcast.98) | data formatting | bytes 7864320
  519.7 0.0 reduce-scatter.4.cloned.1.call-update
  519.7 60.3 %reduce-scatter.4.cloned.1.call-done = bf16[128,3840]{1,0:T(8,128)(2,1)} async-done(((bf16[512,3840]{1,0:T(8,128)(2,1)}), bf16[128,3840]{1,0:T(8,128)(2,1)}) %reduce-scatter.4.cloned.1.call-update) | async-done | bytes 983056
  580.0 12.7 %reshape.48 = bf16[128,2,8,8,30]{4,3,2,1,0:T(8,128)(2,1)} reshape(bf16[128,3840]{1,0:T(8,128)(2,1)} %reduce-scatter.4.cloned.1.call-done) | data formatting | bytes 1966080
  592.8 7.3 %copy.33 = bf16[2,8,8,30,128]{4,2,3,0,1:T(8,128)(2,1)} copy(bf16[2,8,8,30,128]{3,2,1,0,4:T(8,128)(2,1)} %bitcast.99) | data formatting | bytes 1966080 | tf_op jit(solution)/shard_map/reduce_scatter | solution.py:74
  600.0 4.2 all-to-all-start
  604.2 14.4 %all-to-all-done = bf16[2,8,8,30,128]{4,2,3,0,1:T(8,128)(2,1)S(1)} async-done(((bf16[2,8,8,30,128]{4,2,3,0,1:T(8,128)(2,1)}), bf16[2,8,8,30,128]{4,2,3,0,1:T(8,128)(2,1)S(1)}, u32[]{:S(2)}, u32[]{:S(2)}) %all-to-all-start) | async-done | bytes 983072 | tf_op jit(solution)/shard_map/all_to_all | solution.py:77
  618.6 0.1 copy.34
  618.7 2.4 fusion.14
  (2 shorter events, 0.0 us)
Async XLA Ops:
  6.5 135.5 %all-gather.5.cloned.1.call-start = ((), (), s32[]{:S(2)}) async-start(), calls=%async_computation.3 | async-start | bytes 1081344 | tf_op jit(solution)/shard_map/all_gather | solution.py:48
  7.9 195.2 %all-gather.3.cloned.1.call-start = ((), (), s32[]{:S(2)}) async-start(), calls=%async_computation.2 | async-start | bytes 4915200 | tf_op jit(solution)/shard_map/all_gather | solution.py:55
  8.7 571.3 %reduce-scatter.4.cloned.1.call-start = ((), (), s32[]{:S(2)}) async-start(), calls=%async_computation.4 | async-start | bytes 4915200
  203.1 38.5 %copy-start.2 = (f32[3,3,3,2,512]{4,3,2,1,0:T(2,128)S(1)}, f32[3,3,3,2,512]{4,3,2,1,0:T(2,128)}, u32[]{:S(2)}) copy-start(f32[3,3,3,2,512]{4,3,2,1,0:T(2,128)} %param.6) | copy-start | bytes 331780
  203.1 38.6 %copy-start.3 = (bf16[512,16]{0,1:T(8,128)(2,1)S(1)}, bf16[512,16]{0,1:T(8,128)(2,1)}, u32[]{:S(2)}) copy-start(bf16[512,16]{0,1:T(8,128)(2,1)} %param.7) | copy-start | bytes 49156
  212.0 3.2 copy-start
  216.4 14.2 %collective-permute-start = (bf16[2,8,8,1,2,512]{5,3,4,2,1,0:T(2,128)(2,1)S(1)}, bf16[2,8,8,1,2,512]{5,3,4,2,1,0:T(2,128)(2,1)S(1)}, u32[]{:S(2)}, u32[]{:S(2)}) collective-permute-start(bf16[2,8,8,1,2,512]{5,3,4,2,1,0:T(2,128)(2,1)S(1)} %get-tuple-element.9), channel_id=1, source_target_pairs={{0,1},{1,2},{2,3},{3,4},{4,5},{5,6},{6,7},{7,8},{8,9},{9,10},{10,1... | collective-permute-start | bytes 786440 | tf_op jit(solution)/shard_map/ppermute | solution.py:12
  219.7 14.9 %collective-permute-start.1 = (bf16[2,8,8,1,2,512]{5,3,4,2,1,0:T(2,128)(2,1)S(1)}, bf16[2,8,8,1,2,512]{5,3,4,2,1,0:T(2,128)(2,1)S(1)}, u32[]{:S(2)}, u32[]{:S(2)}) collective-permute-start(bf16[2,8,8,1,2,512]{5,3,4,2,1,0:T(2,128)(2,1)S(1)} %get-tuple-element.10), channel_id=1, source_target_pairs={{1,0},{2,1},{3,2},{4,3},{5,4},{6,5},{7,6},{8,7},{9,8},{10,9},{11,1... | collective-permute-start | bytes 786440 | tf_op jit(solution)/shard_map/ppermute | solution.py:12
  221.0 120.9 %copy-start.1 = (bf16[2,8,8,30,2,512]{5,3,4,2,1,0:T(8,128)(2,1)S(1)}, bf16[2,8,8,30,2,512]{5,3,4,2,1,0:T(8,128)(2,1)}, u32[]{:S(2)}) copy-start(bf16[2,8,8,30,2,512]{5,3,4,2,1,0:T(8,128)(2,1)} %copy-done) | copy-start | bytes 23592964
  238.0 103.8 %collective-permute-start.2 = (bf16[2,8,1,32,2,512]{5,3,4,2,1,0:T(8,128)(2,1)S(1)}, bf16[2,8,1,32,2,512]{5,3,4,2,1,0:T(8,128)(2,1)S(1)}, u32[]{:S(2)}, u32[]{:S(2)}) collective-permute-start(bf16[2,8,1,32,2,512]{5,3,4,2,1,0:T(8,128)(2,1)S(1)} %get-tuple-element.7), channel_id=1, source_target_pairs={{0,4},{1,5},{2,6},{3,7},{4,8},{5,9},{6,10},{7,11},{8,12},{9,13},{1... | collective-permute-start | bytes 3145736 | tf_op jit(solution)/shard_map/ppermute | solution.py:12
  240.3 101.5 %collective-permute-start.3 = (bf16[2,8,1,32,2,512]{5,3,4,2,1,0:T(8,128)(2,1)S(1)}, bf16[2,8,1,32,2,512]{5,3,4,2,1,0:T(8,128)(2,1)S(1)}, u32[]{:S(2)}, u32[]{:S(2)}) collective-permute-start(bf16[2,8,1,32,2,512]{5,3,4,2,1,0:T(8,128)(2,1)S(1)} %get-tuple-element.8), channel_id=1, source_target_pairs={{4,0},{5,1},{6,2},{7,3},{8,4},{9,5},{10,6},{11,7},{12,8},{13,9},{1... | collective-permute-start | bytes 3145736 | tf_op jit(solution)/shard_map/ppermute | solution.py:12
  600.0 18.6 %all-to-all-start = ((bf16[2,8,8,30,128]{4,2,3,0,1:T(8,128)(2,1)}), bf16[2,8,8,30,128]{4,2,3,0,1:T(8,128)(2,1)S(1)}, u32[]{:S(2)}, u32[]{:S(2)}) async-start(bf16[2,8,8,30,128]{4,2,3,0,1:T(8,128)(2,1)} %copy.33), calls=%async_computation | async-start | bytes 1966080 | tf_op jit(solution)/shard_map/all_to_all | solution.py:77
Sparse Core Ops, SparseCore 0:
  9.0 132.9 all-gather.4
  143.7 59.3 all-gather.2
  519.8 60.1 reduce-scatter.3
where the time goes:
time: 628 us
  waiting for transfers between devices  283 us (45%)
  other arithmetic  124 us (20%)
  blocking collectives  100 us (16%)
  local copies, waits for them, and re-layouts  75.6 us (12%)
  matrix products  19.3 us (3%)
  between operations  13.2 us (2%)
  starting transfers between devices  12.4 us (2%)
    all_gather x1, waiting for transfers between devices, expand_block(): lax.all_gather(expand_weight, 'tile', axis=0, tiled=True)  133 us
    all_gather x1, blocking collectives, on_device(): lax.all_gather(project_weight, 'tile', axis=1, tiled=True)  100 us
    add x1, other arithmetic, depthwise(): accumulated = accumulated + window.astype(jnp.float32) * kernel[i, j, l]  91.4 us
    unnamed x12, local copies, waits for them, and re-layouts  67 us
    all_gather x1, waiting for transfers between devices, on_device(): gathered = lax.all_gather(latent, 'ch', axis=5, tiled=True)[:, :, 0]  61.1 us
    unnamed x4, waiting for transfers between devices  61 us
    concatenate x2, other arithmetic, grid_rim(): return jnp.concatenate([from_above, widened, from_below], axis=2)  26.5 us
    all_to_all x1, waiting for transfers between devices, on_device(): lax.all_to_all(channel_sums.astype(jnp.bfloat16), 'ch', split_axis=1, con...  14.4 us
  transfers between devices with their start and end apart: 8, of which 6 were waited for; matrix products, arithmetic and copies ran while one was open for 0% of the time, Pallas kernels for 0%

commit v1 on v0

v1 whole, which is shorter than its diff:
```python
import functools

import jax
import jax.numpy as jnp
from jax import lax
from jax.experimental import pallas as pl
from jax.experimental.pallas import tpu as pltpu
from jax.sharding import PartitionSpec as P

F32 = jnp.float32
BF16 = jnp.bfloat16
BOTH = ("ch", "tile")


def device_pairs(move):
    pairs = []
    for ch in range(4):
        for tile in range(32):
            x, core = (ch // 2) * 2 + (tile // 4) % 2, ch % 2
            y, z = tile // 8, tile % 4
            to = move(x, y, z, core)
            if to is not None:
                tx, ty, tz, tc = to
                target = ((tx // 2) * 2 + tc) * 32 + (ty * 2 + tx % 2) * 4 + tz
                pairs.append((ch * 32 + tile, target))
    return pairs


def around(axis, by):
    def move(x, y, z, core):
        at = [x, y, z]
        at[axis] = (at[axis] + by) % 4
        return (*at, core)

    return device_pairs(move)


def column_step(by):
    def move(x, y, z, core):
        return (x, y, z + by, core) if 0 <= z + by < 4 else None

    return device_pairs(move)


def row_step(by):
    def move(x, y, z, core):
        row = y * 2 + x % 2 + by
        return ((x // 2) * 2 + row % 2, row // 2, z, core) if 0 <= row < 8 else None

    return device_pairs(move)


ACROSS = around(0, 2)
CORES = device_pairs(lambda x, y, z, core: (x, y, z, 1 - core))


def send(value, pairs):
    return lax.ppermute(value, BOTH, pairs)


def conv_taps(window, k_ref, gate, group):
    sums = [[None] * 3 for _ in range(4)]
    for j in range(3):
        taps = [[k_ref[(i * 3 + j) * 3 + l, gate, group] for l in range(3)] for i in range(3)]
        taps = [[jnp.concatenate([t, t], axis=0) for t in row] for row in taps]
        for slot in range(6):
            x = window(slot, j)
            for i in range(3):
                f = slot - i
                if 0 <= f < 4:
                    for l in range(3):
                        p = x * taps[i][l]
                        sums[f][l] = p if sums[f][l] is None else sums[f][l] + p
    out = []
    for f in range(4):
        left, centre, right = [s.astype(F32) for s in sums[f]]
        out.append(centre + pltpu.roll(left, 1, 0) + pltpu.roll(right, 31, 0))
    return out


ROWS = 1664
CHUNK = 416


def block_kernel(pos_ref, x0, x1, x2, x3, a0, a1, a2, a3, b0, b1, b2, b3, k_ref, out_ref,
                 x_scr, w_scr, e_scr, acc):
    xhi, core, y, z = pos_ref[0], pos_ref[1], pos_ref[2], pos_ref[3]
    base = 1 - xhi
    ch = xhi * 2 + core
    for r, ref in enumerate((x0, x1, x2, x3)):
        m = ch ^ r
        for b in range(2):
            x_scr[m, b, 0:1600, :] = ref[b]
            x_scr[m, b, 1600:ROWS, :] = jnp.zeros((ROWS - 1600, 128), BF16)
    for r, (a, b) in enumerate(((a0, b0), (a1, b1), (a2, b2), (a3, b3))):
        py, pz = (y + r) % 4, (z + r) % 4
        for o in range(4):
            for xlo in range(2):
                at_a = pl.ds(pl.multiple_of(((py * 2 + xlo) * 4 + o) * 16, 16), 16)
                at_b = pl.ds(pl.multiple_of(((o * 2 + xlo) * 4 + pz) * 16, 16), 16)
                for g in range(3):
                    w_scr[g, 0, at_a, :] = a[o, xlo, g]
                    w_scr[g, 1, at_b, :] = b[o, xlo, g]
    empty = jnp.where(base == 0, 5, 0)
    for buf in range(2):
        for g in range(4):
            e_scr[buf, g, pl.ds(pl.multiple_of(empty * 320, 64), 320), :] = jnp.zeros((320, 128), BF16)

    def expand(s, it, buf):
        b, c = s // 4, s % 4
        at = pl.ds(pl.multiple_of(it * CHUNK, 16), CHUNK)
        rows = jnp.concatenate([x_scr[m, b, at, :] for m in range(4)], axis=1)
        for g in range(2):
            w = w_scr[g, c // 2, :, pl.ds(pl.multiple_of((c % 2) * 256, 256), 256)]
            half = jnp.dot(rows, w, preferred_element_type=F32)
            e = (half * jnp.tanh(half) + half).astype(BF16)
            for q in range(2):
                to = pl.ds(pl.multiple_of(base * 320 + it * CHUNK, 16), CHUNK)
                e_scr[buf, g * 2 + q, to, :] = e[:, q * 128:(q + 1) * 128]

    def filter_rows(s, it, buf):
        b, c = s // 4, s % 4
        hidden, kept = [], []
        for r in range(2):
            h = it * 2 + r
            cols = []
            for q in range(2):
                parts = []
                for g in range(2):
                    def window(slot, j):
                        at = pl.multiple_of(slot * 320 + (h + j) * 32, 32)
                        return e_scr[buf, g * 2 + q, pl.ds(at, 32), :]

                    parts.append(conv_taps(window, k_ref, g, c * 2 + q))
                gated = []
                for f in range(4):
                    u = parts[1][f] * 0.5
                    gated.append((parts[0][f] * (u * jnp.tanh(u) + u)).astype(BF16))
                cols.append(jnp.concatenate(gated, axis=0))
            hidden.append(jnp.concatenate(cols, axis=1))
            for f in range(4):
                at = pl.ds(pl.multiple_of((f + xhi) * 320 + (h + 1) * 32, 32), 32)
                cells = jnp.concatenate([x_scr[m, b, at, :] for m in range(4)], axis=1)
                kept.append(jnp.where(core == f // 2, cells.astype(F32), 0.0))
        hidden = jnp.concatenate(hidden, axis=0)
        w = w_scr[2, c // 2, :, pl.ds(pl.multiple_of((c % 2) * 256, 256), 256)]
        y_new = lax.dot_general(hidden, w, (((1,), (1,)), ((), ())), preferred_element_type=F32)
        at = pl.ds(pl.multiple_of(it * 256, 256), 256)
        total = y_new + jnp.where(c == 0, jnp.concatenate(kept, axis=0), acc[at, :])
        acc[at, :] = total
        for r in range(2):
            for f in range(4):
                out_ref[f // 2 ^ core, b, f % 2, it * 2 + r] = total[(r * 4 + f) * 32:(r * 4 + f + 1) * 32]

    lax.fori_loop(0, 4, lambda it, _: (expand(0, it, 0), 0)[1], 0)

    def step(s, _):
        def inner(it, _):
            expand(jnp.minimum(s + 1, 7), it, 1 - s % 2)
            filter_rows(s, it, s % 2)
            return 0

        return lax.fori_loop(0, 4, inner, 0)

    lax.fori_loop(0, 8, step, 0)


def run_block(position, pieces, weights_a, weights_b, taps):
    vmem = pl.BlockSpec(memory_space=pltpu.VMEM)
    return pl.pallas_call(
        block_kernel,
        out_shape=jax.ShapeDtypeStruct((2, 2, 2, 8, 32, 512), F32),
        in_specs=[pl.BlockSpec(memory_space=pltpu.SMEM)] + [vmem] * 13,
        out_specs=vmem,
        scratch_shapes=[
            pltpu.VMEM((4, 2, ROWS, 128), BF16),
            pltpu.VMEM((3, 2, 512, 512), BF16),
            pltpu.VMEM((2, 4, 2048, 128), BF16),
            pltpu.VMEM((1024, 512), F32),
        ],
        compiler_params=pltpu.CompilerParams(vmem_limit_bytes=52 * 2**20),
        name="gated_block",
    )(position, *pieces, *weights_a, *weights_b, taps)


def gather_axis(piece, axis):
    return [piece] + [send(piece, around(axis, -by)) for by in (1, 2, 3)]


def in_order(pieces, own):
    return jnp.stack(pieces)[(jnp.arange(4) - own) % 4]


def on_device(latent, expand_weight, depth_kernel, project_weight):
    ch, tile = lax.axis_index("ch"), lax.axis_index("tile")
    xhi, core = ch // 2, ch % 2
    y, xlo, z = tile // 8, (tile // 4) % 2, tile % 4
    x = xhi * 2 + xlo

    cells = latent[:, :, 0]
    left = send(cells[:, :, :, -1:], column_step(1))
    right = send(cells[:, :, :, :1], column_step(-1))
    wide = jnp.concatenate([cells, right, left], axis=3)
    above = send(wide[:, :, -1:], row_step(1))
    below = send(wide[:, :, :1], row_step(-1))
    tall = jnp.concatenate([above, wide, below], axis=2)
    own = lax.dynamic_slice_in_dim(tall, 3 * xhi, 5, 1).reshape(2, 1600, 128)
    other = lax.dynamic_slice_in_dim(tall, 3 * (1 - xhi), 5, 1).reshape(2, 1600, 128)
    across = send(other, ACROSS)
    pieces = [own, send(own, CORES), across, send(across, CORES)]

    half = expand_weight * jnp.asarray(0.5, BF16)
    shard = jnp.stack([half[:, 0], half[:, 1], project_weight.T])
    by_x = in_order(gather_axis(shard, 0), x)
    half_a = in_order(gather_axis(by_x[:2], 2), z)
    half_b = in_order(gather_axis(by_x[2:], 1), y)
    weights_a = gather_axis(half_a, 1)
    weights_b = gather_axis(half_b, 2)

    taps = depth_kernel.reshape(27, 2, 4, 128)
    far = send(taps, ACROSS)
    taps = jnp.where(xhi == 0, jnp.concatenate([taps, far], axis=2), jnp.concatenate([far, taps], axis=2))
    taps = jnp.broadcast_to(taps.astype(BF16)[:, :, :, None], (27, 2, 8, 16, 128))

    position = jnp.stack([xhi, core, y, z]).astype(jnp.int32)
    partial = run_block(position, pieces, weights_a, weights_b, taps)
    received = send(partial[1].astype(BF16), CORES)
    total = (partial[0] + received.astype(F32)).astype(BF16)
    return total[:, :, None, :, :30]


def solution(mesh):
    return jax.shard_map(
        on_device,
        mesh=mesh,
        in_specs=(
            P(None, None, "tile", None, None, "ch"),
            P("tile", None, "ch"),
            P(None, None, None, None, "ch"),
            P("ch", "tile"),
        ),
        out_specs=P(None, "ch", "tile", None, None, None),
        check_vma=False,
    )
```

time: 628 us -> 177 us (0.28)
  waiting for transfers between devices: 283 us -> 57.2 us
  other arithmetic: 124 us -> 5.01 us
  blocking collectives: 100 us -> 0 us
  local copies, waits for them, and re-layouts: 75.6 us -> 11 us
  Pallas kernels: 0 us -> 62 us
  starting transfers between devices: 12.4 us -> 41 us
  matrix products: 19.3 us -> 0 us
  between operations: 13.2 us -> 0.23 us
    all_gather x2 -> x0, waiting for transfers between devices: 194 us -> none  [the longest x1 133 us: expand_block(): lax.all_gather(expand_weight, 'tile', axis=0, tiled=True)]
    all_gather x1 -> x0, blocking collectives: 100 us -> none  [on_device(): lax.all_gather(project_weight, 'tile', axis=1, tiled=True)]
    add x1 -> x0, other arithmetic: 91.4 us -> none  [depthwise(): accumulated = accumulated + window.astype(jnp.float32) * kernel[i, j, l]]
    unnamed x12 -> x10, local copies, waits for them, and re-layouts: 67 us -> 0.03 us
    pallas_call x0 -> x1, Pallas kernels: none -> 62 us  [run_block(): pl.pallas_call(block_kernel, out_shape=jax.ShapeDtypeStruct((2, 2, 2, 8,...]
    unnamed x4 -> x0, waiting for transfers between devices: 61 us -> none
    ppermute x4 -> x24, waiting for transfers between devices: 13 us -> 57.2 us  [send(): return lax.ppermute(value, BOTH, pairs)]
    ppermute x4 -> x24, starting transfers between devices: 8.12 us -> 41 us  [send(): return lax.ppermute(value, BOTH, pairs)]
  transfers between devices with their start and end apart: 8 -> 24, of which waited for: 6 -> 11; matrix products, arithmetic and copies ran while one was open for 0% -> 3% of each run, Pallas kernels for 0% -> 0%
where the time goes in v1:
time: 177 us; the launch traced here: 176 us
  Pallas kernels  62 us (35%)
  waiting for transfers between devices  57.2 us (32%)
  starting transfers between devices  41 us (23%)
  local copies, waits for them, and re-layouts  11 us (6%)
  other arithmetic  5.01 us (3%)
    pallas_call x1, Pallas kernels, run_block(): pl.pallas_call(block_kernel, out_shape=jax.ShapeDtypeStruct((2, 2, 2, 8,...  62 us
    ppermute x24, waiting for transfers between devices, send(): return lax.ppermute(value, BOTH, pairs)  57.2 us
    ppermute x24, starting transfers between devices, send(): return lax.ppermute(value, BOTH, pairs)  41 us
  transfers between devices with their start and end apart: 24, of which 11 were waited for; matrix products, arithmetic and copies ran while one was open for 3% of the time, Pallas kernels for 0%

profile of v1, /device:TPU:1, one launch (start us, length us, event | category | flops | bytes accessed | tf_op | source)
XLA Modules:
  0.0 176.4 jit_solution(11964835532700736489)
XLA Ops:
  0.0 0.9 fusion.11
  0.9 1.3 collective-permute-start
  2.2 5.0 %collective-permute-start.1 = (bf16[2,8,8,1,128]{4,2,3,1,0:T(8,128)(2,1)S(1)}, bf16[2,8,8,1,128]{4,2,3,1,0:T(8,128)(2,1)S(1)}, u32[]{:S(2)}, u32[]{:S(2)}) collective-permute-start(bf16[2,8,8,1,128]{4,2,3,1,0:T(8,128)(2,1)S(1)} %get-tuple-element.10), channel_id=1, source_target_pairs={{0,1},{1,2},{2,3},{4,5},{5,6},{6,7},{8,9},{9,10},{10,11},{12,13},{... | collective-permute-start | bytes 98312 | tf_op jit(solution)/shard_map/ppermute | solution.py:58
  7.2 0.8 copy_multiply_fusion
  7.9 0.2 collective-permute-done.1
  8.2 2.1 %pad_maximum_fusion.5 = (bf16[2,8,1,32,128]{4,2,3,1,0:T(2,128)(2,1)S(1)}, bf16[2,8,1,32,128]{4,2,3,1,0:T(2,128)(2,1)S(1)}) fusion(bf16[2,8,8,1,128]{4,2,3,1,0:T(8,128)(2,1)S(1)} %collective-permute-done.1, bf16[2,8,8,1,128]{4,2,3,1,0:T(8,128)(2,1)S(1)} %collective-permute-done, bf16[2,8,8,30,128]{4,2,3,1,0:T(8,128)(2,1)} %bitcast.42), kind=kLoop, calls=%fused_computation.14 | loop fusion | flops 786432 | bytes 1310720 | tf_op jit(solution)/shard_map/slice | solution.py:204
  10.2 3.1 %collective-permute-start.2 = (bf16[2,8,1,32,128]{4,2,3,1,0:T(2,128)(2,1)S(1)}, bf16[2,8,1,32,128]{4,2,3,1,0:T(2,128)(2,1)S(1)}, u32[]{:S(2)}, u32[]{:S(2)}) collective-permute-start(bf16[2,8,1,32,128]{4,2,3,1,0:T(2,128)(2,1)S(1)} %get-tuple-element.7), channel_id=1, source_target_pairs={{0,4},{1,5},{2,6},{3,7},{4,8},{5,9},{6,10},{7,11},{8,12},{9,13},{1... | collective-permute-start | bytes 393224 | tf_op jit(solution)/shard_map/ppermute | solution.py:58
  13.4 1.3 collective-permute-start.3
  14.7 2.6 %collective-permute-done.2 = bf16[2,8,1,32,128]{4,2,3,1,0:T(2,128)(2,1)S(1)} collective-permute-done((bf16[2,8,1,32,128]{4,2,3,1,0:T(2,128)(2,1)S(1)}, bf16[2,8,1,32,128]{4,2,3,1,0:T(2,128)(2,1)S(1)}, u32[]{:S(2)}, u32[]{:S(2)}) %collective-permute-start.2) | collective-permute-done | bytes 131104 | tf_op jit(solution)/shard_map/ppermute | solution.py:58
  17.3 7.6 %collective-permute-done.3 = bf16[2,8,1,32,128]{4,2,3,1,0:T(2,128)(2,1)S(1)} collective-permute-done((bf16[2,8,1,32,128]{4,2,3,1,0:T(2,128)(2,1)S(1)}, bf16[2,8,1,32,128]{4,2,3,1,0:T(2,128)(2,1)S(1)}, u32[]{:S(2)}, u32[]{:S(2)}) %collective-permute-start.3) | collective-permute-done | bytes 131104 | tf_op jit(solution)/shard_map/ppermute | solution.py:58
  24.9 1.4 pad_maximum_fusion
  26.4 0.5 constant_dynamic-slice_fusion
  26.8 0.0 copy-start.4
  26.8 0.0 copy-start.3
  26.8 1.1 copy.6
  28.0 2.7 %collective-permute-start.5 = (bf16[2,1600,128]{2,1,0:T(8,128)(2,1)}, bf16[2,1600,128]{2,1,0:T(8,128)(2,1)}, u32[]{:S(2)}, u32[]{:S(2)}) collective-permute-start(bf16[2,1600,128]{2,1,0:T(8,128)(2,1)} %bitcast.6), channel_id=1, source_target_pairs={{0,64},{1,65},{2,66},{3,67},{4,68},{5,69},{6,70},{7,71},{8,72},{9,... | collective-permute-start | bytes 2457608 | tf_op jit(solution)/shard_map/ppermute | solution.py:58
  30.7 0.3 collective-permute-start.8
  31.0 2.5 %collective-permute-start.7 = (bf16[3,16,512]{2,1,0:T(8,128)(2,1)S(1)}, bf16[3,16,512]{2,1,0:T(8,128)(2,1)S(1)}, u32[]{:S(2)}, u32[]{:S(2)}) collective-permute-start(bf16[3,16,512]{2,1,0:T(8,128)(2,1)S(1)} %get-tuple-element.16), channel_id=1, source_target_pairs={{0,68},{1,69},{2,70},{3,71},{4,0},{5,1},{6,2},{7,3},{8,76},{9,77},... | collective-permute-start | bytes 147464 | tf_op jit(solution)/shard_map/ppermute | solution.py:58
  33.5 0.1 concatenate.24
  33.6 1.8 %collective-permute-start.22 = (bf16[27,2,4,128]{3,2,1,0:T(4,128)(2,1)S(1)}, bf16[27,2,4,128]{3,2,1,0:T(4,128)(2,1)S(1)}, u32[]{:S(2)}, u32[]{:S(2)}) collective-permute-start(bf16[27,2,4,128]{3,2,1,0:T(4,128)(2,1)S(1)} %concatenate.24), channel_id=1, source_target_pairs={{0,64},{1,65},{2,66},{3,67},{4,68},{5,69},{6,70},{7,71},{8,72},{9,... | collective-permute-start | bytes 165896 | tf_op jit(solution)/shard_map/ppermute | solution.py:58
  35.5 12.6 %collective-permute-done.8 = bf16[3,16,512]{2,1,0:T(8,128)(2,1)S(1)} collective-permute-done((bf16[3,16,512]{2,1,0:T(8,128)(2,1)S(1)}, bf16[3,16,512]{2,1,0:T(8,128)(2,1)S(1)}, u32[]{:S(2)}, u32[]{:S(2)}) %collective-permute-start.8) | collective-permute-done | bytes 49184 | tf_op jit(solution)/shard_map/ppermute | solution.py:58
  48.1 1.1 collective-permute-done.7
  49.2 3.3 %collective-permute-done.9 = bf16[3,16,512]{2,1,0:T(8,128)(2,1)S(1)} collective-permute-done((bf16[3,16,512]{2,1,0:T(8,128)(2,1)S(1)}, bf16[3,16,512]{2,1,0:T(8,128)(2,1)S(1)}, u32[]{:S(2)}, u32[]{:S(2)}) %collective-permute-start.9) | collective-permute-done | bytes 49184 | tf_op jit(solution)/shard_map/ppermute | solution.py:58
  52.6 0.6 gather_fusion
  53.2 2.7 %collective-permute-start.17 = (bf16[2,3,16,512]{3,2,1,0:T(8,128)(2,1)S(1)}, bf16[2,3,16,512]{3,2,1,0:T(8,128)(2,1)S(1)}, u32[]{:S(2)}, u32[]{:S(2)}) collective-permute-start(bf16[2,3,16,512]{3,2,1,0:T(8,128)(2,1)S(1)} %get-tuple-element.14), channel_id=1, source_target_pairs={{0,16},{1,17},{2,18},{3,19},{4,20},{5,21},{6,22},{7,23},{8,24},{9,... | collective-permute-start | bytes 294920 | tf_op jit(solution)/shard_map/ppermute | solution.py:58
  55.9 1.1 collective-permute-start.16
  57.0 0.4 collective-permute-start.18
  57.4 0.2 copy.5
  57.6 0.0 copy-start.1
  57.6 0.0 collective-permute-done.22
  57.6 3.5 %collective-permute-start.11 = (bf16[2,3,16,512]{3,2,1,0:T(8,128)(2,1)S(1)}, bf16[2,3,16,512]{3,2,1,0:T(8,128)(2,1)S(1)}, u32[]{:S(2)}, u32[]{:S(2)}) collective-permute-start(bf16[2,3,16,512]{3,2,1,0:T(8,128)(2,1)S(1)} %get-tuple-element.13), channel_id=1, source_target_pairs={{0,2},{1,3},{2,0},{3,1},{4,6},{5,7},{6,4},{7,5},{8,10},{9,11},{10,... | collective-permute-start | bytes 294920 | tf_op jit(solution)/shard_map/ppermute | solution.py:58
  61.1 0.0 collective-permute-done.17
  61.1 0.6 collective-permute-start.10
  61.7 0.8 collective-permute-start.12
  62.6 2.5 %collective-permute-start.4 = (bf16[2,1600,128]{2,1,0:T(8,128)(2,1)S(1)}, bf16[2,1600,128]{2,1,0:T(8,128)(2,1)}, u32[]{:S(2)}, u32[]{:S(2)}) collective-permute-start(bf16[2,1600,128]{2,1,0:T(8,128)(2,1)S(1)} %bitcast.44), channel_id=1, source_target_pairs={{0,32},{1,33},{2,34},{3,35},{4,36},{5,37},{6,38},{7,39},{8,40},{9,... | collective-permute-start | bytes 2457608 | tf_op jit(solution)/shard_map/ppermute | solution.py:58
  65.1 0.0 collective-permute-done.5.x2
  65.1 0.1 collective-permute-start.6
  65.1 0.1 pad_maximum_fusion.2
  65.2 0.6 gather_fusion.2
  65.8 0.0 collective-permute-done.11
  65.8 0.9 collective-permute-start.21
  66.7 3.1 %collective-permute-start.20 = (bf16[4,2,3,16,512]{4,3,2,1,0:T(8,128)(2,1)S(1)}, bf16[4,2,3,16,512]{4,3,2,1,0:T(8,128)(2,1)}, u32[]{:S(2)}, u32[]{:S(2)}) collective-permute-start(bf16[4,2,3,16,512]{4,3,2,1,0:T(8,128)(2,1)S(1)} %gather_fusion.2), channel_id=1, source_target_pairs={{0,2},{1,3},{2,0},{3,1},{4,6},{5,7},{6,4},{7,5},{8,10},{9,11},{10,... | collective-permute-start | bytes 1179656 | tf_op jit(solution)/shard_map/ppermute | solution.py:58
  69.8 0.0 collective-permute-done.12
  69.8 0.6 collective-permute-start.19
  70.4 0.1 pad_maximum_fusion.1
  70.5 0.6 gather_fusion.1
  71.0 7.2 %collective-permute-done.21.b3 = bf16[4,2,3,16,512]{4,3,2,1,0:T(8,128)(2,1)S(1)} collective-permute-done((bf16[4,2,3,16,512]{4,3,2,1,0:T(8,128)(2,1)S(1)}, bf16[4,2,3,16,512]{4,3,2,1,0:T(8,128)(2,1)S(1)}, u32[]{:S(2)}, u32[]{:S(2)}) %collective-permute-start.21) | collective-permute-done | bytes 393248 | tf_op jit(solution)/shard_map/ppermute | solution.py:58
  78.2 1.3 collective-permute-start.15
  79.5 7.5 %collective-permute-done.20.b2 = bf16[4,2,3,16,512]{4,3,2,1,0:T(8,128)(2,1)} collective-permute-done((bf16[4,2,3,16,512]{4,3,2,1,0:T(8,128)(2,1)S(1)}, bf16[4,2,3,16,512]{4,3,2,1,0:T(8,128)(2,1)}, u32[]{:S(2)}, u32[]{:S(2)}) %collective-permute-start.20) | collective-permute-done | bytes 393248 | tf_op jit(solution)/shard_map/ppermute | solution.py:58
  87.0 3.1 %collective-permute-start.14 = (bf16[4,2,3,16,512]{4,3,2,1,0:T(8,128)(2,1)S(1)}, bf16[4,2,3,16,512]{4,3,2,1,0:T(8,128)(2,1)S(1)}, u32[]{:S(2)}, u32[]{:S(2)}) collective-permute-start(bf16[4,2,3,16,512]{4,3,2,1,0:T(8,128)(2,1)S(1)} %gather_fusion.1), channel_id=1, source_target_pairs={{0,16},{1,17},{2,18},{3,19},{4,20},{5,21},{6,22},{7,23},{8,24},{9,... | collective-permute-start | bytes 1179656 | tf_op jit(solution)/shard_map/ppermute | solution.py:58
  90.0 0.7 collective-permute-start.13
  90.8 0.1 pad_add_fusion.pos_ref
  90.9 0.1 fusion.3
  91.0 0.0 collective-permute-done.15.a3
  91.0 7.7 %collective-permute-done.14.a2 = bf16[4,2,3,16,512]{4,3,2,1,0:T(8,128)(2,1)S(1)} collective-permute-done((bf16[4,2,3,16,512]{4,3,2,1,0:T(8,128)(2,1)S(1)}, bf16[4,2,3,16,512]{4,3,2,1,0:T(8,128)(2,1)S(1)}, u32[]{:S(2)}, u32[]{:S(2)}) %collective-permute-start.14) | collective-permute-done | bytes 393248 | tf_op jit(solution)/shard_map/ppermute | solution.py:58
  98.6 6.7 %collective-permute-done.13.a1 = bf16[4,2,3,16,512]{4,3,2,1,0:T(8,128)(2,1)S(1)} collective-permute-done((bf16[4,2,3,16,512]{4,3,2,1,0:T(8,128)(2,1)S(1)}, bf16[4,2,3,16,512]{4,3,2,1,0:T(8,128)(2,1)S(1)}, u32[]{:S(2)}, u32[]{:S(2)}) %collective-permute-start.13) | collective-permute-done | bytes 393248 | tf_op jit(solution)/shard_map/ppermute | solution.py:58
  105.4 1.5 broadcast_in_dim.4.k_ref
  106.9 62.0 %gated_block.1 = f32[2,2,2,8,32,512]{5,4,3,2,1,0:T(8,128)} custom-call(s32[4]{0:T(128)S(1)} %pad_add_fusion.pos_ref, bf16[2,1600,128]{2,1,0:T(8,128)(2,1)} %bitcast.45, bf16[2,1600,128]{2,1,0:T(8,128)(2,1)} %collective-permute-done.4.x1, bf16[2,1600,128]{2,1,0:T(8,128)(2,1)} %collective-permute-done.5.x2, bf16[2,1600,128]{2,1,0:T(8,128)(2,1)} %collective-permute-done.6.x3, ...), custom_call_target="tpu_custom_call" | custom-call | tf_op jit(solution)/shard_map/gated_block/pallas_call | solution.py:170
  168.9 1.7 fusion.1
  170.6 1.6 collective-permute-start.23
  172.2 1.8 slice_bitcast_fusion
  174.0 0.5 collective-permute-done.23
  174.5 0.4 fusion.2
  174.9 1.5 copy.8
  (25 shorter events, 0.2 us)
Async XLA Ops:
  0.0 24.9 %copy-start = (bf16[2,8,1,8,30,128]{5,3,4,2,1,0:T(8,128)(2,1)S(1)}, bf16[2,8,1,8,30,128]{5,3,4,2,1,0:T(8,128)(2,1)}, u32[]{:S(2)}) copy-start(bf16[2,8,1,8,30,128]{5,3,4,2,1,0:T(8,128)(2,1)} %param.4) | copy-start | bytes 2949124
  0.9 7.1 %collective-permute-start = (bf16[2,8,8,1,128]{4,2,3,1,0:T(8,128)(2,1)S(1)}, bf16[2,8,8,1,128]{4,2,3,1,0:T(8,128)(2,1)S(1)}, u32[]{:S(2)}, u32[]{:S(2)}) collective-permute-start(bf16[2,8,8,1,128]{4,2,3,1,0:T(8,128)(2,1)S(1)} %get-tuple-element.9), channel_id=1, source_target_pairs={{1,0},{2,1},{3,2},{5,4},{6,5},{7,6},{9,8},{10,9},{11,10},{13,12},{... | collective-permute-start | bytes 98312 | tf_op jit(solution)/shard_map/ppermute | solution.py:58
  2.2 6.0 %collective-permute-start.1 = (bf16[2,8,8,1,128]{4,2,3,1,0:T(8,128)(2,1)S(1)}, bf16[2,8,8,1,128]{4,2,3,1,0:T(8,128)(2,1)S(1)}, u32[]{:S(2)}, u32[]{:S(2)}) collective-permute-start(bf16[2,8,8,1,128]{4,2,3,1,0:T(8,128)(2,1)S(1)} %get-tuple-element.10), channel_id=1, source_target_pairs={{0,1},{1,2},{2,3},{4,5},{5,6},{6,7},{8,9},{9,10},{10,11},{12,13},{... | collective-permute-start | bytes 98312 | tf_op jit(solution)/shard_map/ppermute | solution.py:58
  10.2 7.1 %collective-permute-start.2 = (bf16[2,8,1,32,128]{4,2,3,1,0:T(2,128)(2,1)S(1)}, bf16[2,8,1,32,128]{4,2,3,1,0:T(2,128)(2,1)S(1)}, u32[]{:S(2)}, u32[]{:S(2)}) collective-permute-start(bf16[2,8,1,32,128]{4,2,3,1,0:T(2,128)(2,1)S(1)} %get-tuple-element.7), channel_id=1, source_target_pairs={{0,4},{1,5},{2,6},{3,7},{4,8},{5,9},{6,10},{7,11},{8,12},{9,13},{1... | collective-permute-start | bytes 393224 | tf_op jit(solution)/shard_map/ppermute | solution.py:58
  13.4 11.6 %collective-permute-start.3 = (bf16[2,8,1,32,128]{4,2,3,1,0:T(2,128)(2,1)S(1)}, bf16[2,8,1,32,128]{4,2,3,1,0:T(2,128)(2,1)S(1)}, u32[]{:S(2)}, u32[]{:S(2)}) collective-permute-start(bf16[2,8,1,32,128]{4,2,3,1,0:T(2,128)(2,1)S(1)} %get-tuple-element.8), channel_id=1, source_target_pairs={{4,0},{5,1},{6,2},{7,3},{8,4},{9,5},{10,6},{11,7},{12,8},{13,9},{1... | collective-permute-start | bytes 393224 | tf_op jit(solution)/shard_map/ppermute | solution.py:58
  26.8 3.9 %copy-start.4 = (bf16[512,16]{0,1:T(8,128)(2,1)S(1)}, bf16[512,16]{0,1:T(8,128)(2,1)}, u32[]{:S(2)}) copy-start(bf16[512,16]{0,1:T(8,128)(2,1)} %param.7) | copy-start | bytes 49156
  26.8 6.7 %copy-start.3 = (f32[3,3,3,2,512]{4,3,2,1,0:T(2,128)S(1)}, f32[3,3,3,2,512]{4,3,2,1,0:T(2,128)}, u32[]{:S(2)}) copy-start(f32[3,3,3,2,512]{4,3,2,1,0:T(2,128)} %param.6) | copy-start | bytes 331780
  28.0 37.1 %collective-permute-start.5 = (bf16[2,1600,128]{2,1,0:T(8,128)(2,1)}, bf16[2,1600,128]{2,1,0:T(8,128)(2,1)}, u32[]{:S(2)}, u32[]{:S(2)}) collective-permute-start(bf16[2,1600,128]{2,1,0:T(8,128)(2,1)} %bitcast.6), channel_id=1, source_target_pairs={{0,64},{1,65},{2,66},{3,67},{4,68},{5,69},{6,70},{7,71},{8,72},{9,... | collective-permute-start | bytes 2457608 | tf_op jit(solution)/shard_map/ppermute | solution.py:58
  30.7 17.3 %collective-permute-start.8 = (bf16[3,16,512]{2,1,0:T(8,128)(2,1)S(1)}, bf16[3,16,512]{2,1,0:T(8,128)(2,1)S(1)}, u32[]{:S(2)}, u32[]{:S(2)}) collective-permute-start(bf16[3,16,512]{2,1,0:T(8,128)(2,1)S(1)} %get-tuple-element.16), channel_id=1, source_target_pairs={{0,64},{1,65},{2,66},{3,67},{4,68},{5,69},{6,70},{7,71},{8,72},{9,... | collective-permute-start | bytes 147464 | tf_op jit(solution)/shard_map/ppermute | solution.py:58
  31.0 18.2 %collective-permute-start.7 = (bf16[3,16,512]{2,1,0:T(8,128)(2,1)S(1)}, bf16[3,16,512]{2,1,0:T(8,128)(2,1)S(1)}, u32[]{:S(2)}, u32[]{:S(2)}) collective-permute-start(bf16[3,16,512]{2,1,0:T(8,128)(2,1)S(1)} %get-tuple-element.16), channel_id=1, source_target_pairs={{0,68},{1,69},{2,70},{3,71},{4,0},{5,1},{6,2},{7,3},{8,76},{9,77},... | collective-permute-start | bytes 147464 | tf_op jit(solution)/shard_map/ppermute | solution.py:58
  33.5 19.0 %collective-permute-start.9 = (bf16[3,16,512]{2,1,0:T(8,128)(2,1)S(1)}, bf16[3,16,512]{2,1,0:T(8,128)(2,1)S(1)}, u32[]{:S(2)}, u32[]{:S(2)}) collective-permute-start(bf16[3,16,512]{2,1,0:T(8,128)(2,1)S(1)} %get-tuple-element.16), channel_id=1, source_target_pairs={{0,4},{1,5},{2,6},{3,7},{4,64},{5,65},{6,66},{7,67},{8,12},{9,13},... | collective-permute-start | bytes 147464 | tf_op jit(solution)/shard_map/ppermute | solution.py:58
  33.6 24.0 %collective-permute-start.22 = (bf16[27,2,4,128]{3,2,1,0:T(4,128)(2,1)S(1)}, bf16[27,2,4,128]{3,2,1,0:T(4,128)(2,1)S(1)}, u32[]{:S(2)}, u32[]{:S(2)}) collective-permute-start(bf16[27,2,4,128]{3,2,1,0:T(4,128)(2,1)S(1)} %concatenate.24), channel_id=1, source_target_pairs={{0,64},{1,65},{2,66},{3,67},{4,68},{5,69},{6,70},{7,71},{8,72},{9,... | collective-permute-start | bytes 165896 | tf_op jit(solution)/shard_map/ppermute | solution.py:58
  53.2 7.9 %collective-permute-start.17 = (bf16[2,3,16,512]{3,2,1,0:T(8,128)(2,1)S(1)}, bf16[2,3,16,512]{3,2,1,0:T(8,128)(2,1)S(1)}, u32[]{:S(2)}, u32[]{:S(2)}) collective-permute-start(bf16[2,3,16,512]{3,2,1,0:T(8,128)(2,1)S(1)} %get-tuple-element.14), channel_id=1, source_target_pairs={{0,16},{1,17},{2,18},{3,19},{4,20},{5,21},{6,22},{7,23},{8,24},{9,... | collective-permute-start | bytes 294920 | tf_op jit(solution)/shard_map/ppermute | solution.py:58
  55.9 5.8 %collective-permute-start.16 = (bf16[2,3,16,512]{3,2,1,0:T(8,128)(2,1)S(1)}, bf16[2,3,16,512]{3,2,1,0:T(8,128)(2,1)S(1)}, u32[]{:S(2)}, u32[]{:S(2)}) collective-permute-start(bf16[2,3,16,512]{3,2,1,0:T(8,128)(2,1)S(1)} %get-tuple-element.14), channel_id=1, source_target_pairs={{0,24},{1,25},{2,26},{3,27},{4,28},{5,29},{6,30},{7,31},{8,0},{9,1... | collective-permute-start | bytes 294920 | tf_op jit(solution)/shard_map/ppermute | solution.py:58
  57.0 5.6 %collective-permute-start.18 = (bf16[2,3,16,512]{3,2,1,0:T(8,128)(2,1)S(1)}, bf16[2,3,16,512]{3,2,1,0:T(8,128)(2,1)S(1)}, u32[]{:S(2)}, u32[]{:S(2)}) collective-permute-start(bf16[2,3,16,512]{3,2,1,0:T(8,128)(2,1)S(1)} %get-tuple-element.14), channel_id=1, source_target_pairs={{0,8},{1,9},{2,10},{3,11},{4,12},{5,13},{6,14},{7,15},{8,16},{9,17... | collective-permute-start | bytes 294920 | tf_op jit(solution)/shard_map/ppermute | solution.py:58
  57.6 49.3 %copy-start.1 = (bf16[2,5,10,32,128]{4,3,2,1,0:T(8,128)(2,1)}, bf16[2,5,10,32,128]{4,3,2,1,0:T(8,128)(2,1)S(1)}, u32[]{:S(2)}) copy-start(bf16[2,5,10,32,128]{4,3,2,1,0:T(8,128)(2,1)S(1)} %copy.5) | copy-start | bytes 2457604
  57.6 8.2 %collective-permute-start.11 = (bf16[2,3,16,512]{3,2,1,0:T(8,128)(2,1)S(1)}, bf16[2,3,16,512]{3,2,1,0:T(8,128)(2,1)S(1)}, u32[]{:S(2)}, u32[]{:S(2)}) collective-permute-start(bf16[2,3,16,512]{3,2,1,0:T(8,128)(2,1)S(1)} %get-tuple-element.13), channel_id=1, source_target_pairs={{0,2},{1,3},{2,0},{3,1},{4,6},{5,7},{6,4},{7,5},{8,10},{9,11},{10,... | collective-permute-start | bytes 294920 | tf_op jit(solution)/shard_map/ppermute | solution.py:58
  61.1 5.6 %collective-permute-start.10 = (bf16[2,3,16,512]{3,2,1,0:T(8,128)(2,1)S(1)}, bf16[2,3,16,512]{3,2,1,0:T(8,128)(2,1)S(1)}, u32[]{:S(2)}, u32[]{:S(2)}) collective-permute-start(bf16[2,3,16,512]{3,2,1,0:T(8,128)(2,1)S(1)} %get-tuple-element.13), channel_id=1, source_target_pairs={{0,3},{1,0},{2,1},{3,2},{4,7},{5,4},{6,5},{7,6},{8,11},{9,8},{10,9... | collective-permute-start | bytes 294920 | tf_op jit(solution)/shard_map/ppermute | solution.py:58
  61.7 8.0 %collective-permute-start.12 = (bf16[2,3,16,512]{3,2,1,0:T(8,128)(2,1)S(1)}, bf16[2,3,16,512]{3,2,1,0:T(8,128)(2,1)S(1)}, u32[]{:S(2)}, u32[]{:S(2)}) collective-permute-start(bf16[2,3,16,512]{3,2,1,0:T(8,128)(2,1)S(1)} %get-tuple-element.13), channel_id=1, source_target_pairs={{0,1},{1,2},{2,3},{3,0},{4,5},{5,6},{6,7},{7,4},{8,9},{9,10},{10,1... | collective-permute-start | bytes 294920 | tf_op jit(solution)/shard_map/ppermute | solution.py:58
  62.6 42.8 %collective-permute-start.4 = (bf16[2,1600,128]{2,1,0:T(8,128)(2,1)S(1)}, bf16[2,1600,128]{2,1,0:T(8,128)(2,1)}, u32[]{:S(2)}, u32[]{:S(2)}) collective-permute-start(bf16[2,1600,128]{2,1,0:T(8,128)(2,1)S(1)} %bitcast.44), channel_id=1, source_target_pairs={{0,32},{1,33},{2,34},{3,35},{4,36},{5,37},{6,38},{7,39},{8,40},{9,... | collective-permute-start | bytes 2457608 | tf_op jit(solution)/shard_map/ppermute | solution.py:58
  65.1 40.3 %collective-permute-start.6 = (bf16[2,1600,128]{2,1,0:T(8,128)(2,1)}, bf16[2,1600,128]{2,1,0:T(8,128)(2,1)}, u32[]{:S(2)}, u32[]{:S(2)}) collective-permute-start(bf16[2,1600,128]{2,1,0:T(8,128)(2,1)} %collective-permute-done.5.x2), channel_id=1, source_target_pairs={{0,32},{1,33},{2,34},{3,35},{4,36},{5,37},{6,38},{7,39},{8,40},{9,... | collective-permute-start | bytes 2457608 | tf_op jit(solution)/shard_map/ppermute | solution.py:58
  65.8 12.4 %collective-permute-start.21 = (bf16[4,2,3,16,512]{4,3,2,1,0:T(8,128)(2,1)S(1)}, bf16[4,2,3,16,512]{4,3,2,1,0:T(8,128)(2,1)S(1)}, u32[]{:S(2)}, u32[]{:S(2)}) collective-permute-start(bf16[4,2,3,16,512]{4,3,2,1,0:T(8,128)(2,1)S(1)} %gather_fusion.2), channel_id=1, source_target_pairs={{0,1},{1,2},{2,3},{3,0},{4,5},{5,6},{6,7},{7,4},{8,9},{9,10},{10,1... | collective-permute-start | bytes 1179656 | tf_op jit(solution)/shard_map/ppermute | solution.py:58
  66.7 20.3 %collective-permute-start.20 = (bf16[4,2,3,16,512]{4,3,2,1,0:T(8,128)(2,1)S(1)}, bf16[4,2,3,16,512]{4,3,2,1,0:T(8,128)(2,1)}, u32[]{:S(2)}, u32[]{:S(2)}) collective-permute-start(bf16[4,2,3,16,512]{4,3,2,1,0:T(8,128)(2,1)S(1)} %gather_fusion.2), channel_id=1, source_target_pairs={{0,2},{1,3},{2,0},{3,1},{4,6},{5,7},{6,4},{7,5},{8,10},{9,11},{10,... | collective-permute-start | bytes 1179656 | tf_op jit(solution)/shard_map/ppermute | solution.py:58
  69.8 20.3 %collective-permute-start.19 = (bf16[4,2,3,16,512]{4,3,2,1,0:T(8,128)(2,1)S(1)}, bf16[4,2,3,16,512]{4,3,2,1,0:T(8,128)(2,1)}, u32[]{:S(2)}, u32[]{:S(2)}) collective-permute-start(bf16[4,2,3,16,512]{4,3,2,1,0:T(8,128)(2,1)S(1)} %gather_fusion.2), channel_id=1, source_target_pairs={{0,3},{1,0},{2,1},{3,2},{4,7},{5,4},{6,5},{7,6},{8,11},{9,8},{10,9... | collective-permute-start | bytes 1179656 | tf_op jit(solution)/shard_map/ppermute | solution.py:58
  78.2 28.7 %copy-start.2 = (bf16[4,2,3,16,512]{4,3,2,1,0:T(8,128)(2,1)}, bf16[4,2,3,16,512]{4,3,2,1,0:T(8,128)(2,1)S(1)}, u32[]{:S(2)}) copy-start(bf16[4,2,3,16,512]{4,3,2,1,0:T(8,128)(2,1)S(1)} %collective-permute-done.21.b3) | copy-start | bytes 1179652
  78.2 12.7 %collective-permute-start.15 = (bf16[4,2,3,16,512]{4,3,2,1,0:T(8,128)(2,1)S(1)}, bf16[4,2,3,16,512]{4,3,2,1,0:T(8,128)(2,1)S(1)}, u32[]{:S(2)}, u32[]{:S(2)}) collective-permute-start(bf16[4,2,3,16,512]{4,3,2,1,0:T(8,128)(2,1)S(1)} %gather_fusion.1), channel_id=1, source_target_pairs={{0,8},{1,9},{2,10},{3,11},{4,12},{5,13},{6,14},{7,15},{8,16},{9,17... | collective-permute-start | bytes 1179656 | tf_op jit(solution)/shard_map/ppermute | solution.py:58
  87.0 11.7 %collective-permute-start.14 = (bf16[4,2,3,16,512]{4,3,2,1,0:T(8,128)(2,1)S(1)}, bf16[4,2,3,16,512]{4,3,2,1,0:T(8,128)(2,1)S(1)}, u32[]{:S(2)}, u32[]{:S(2)}) collective-permute-start(bf16[4,2,3,16,512]{4,3,2,1,0:T(8,128)(2,1)S(1)} %gather_fusion.1), channel_id=1, source_target_pairs={{0,16},{1,17},{2,18},{3,19},{4,20},{5,21},{6,22},{7,23},{8,24},{9,... | collective-permute-start | bytes 1179656 | tf_op jit(solution)/shard_map/ppermute | solution.py:58
  90.0 15.3 %collective-permute-start.13 = (bf16[4,2,3,16,512]{4,3,2,1,0:T(8,128)(2,1)S(1)}, bf16[4,2,3,16,512]{4,3,2,1,0:T(8,128)(2,1)S(1)}, u32[]{:S(2)}, u32[]{:S(2)}) collective-permute-start(bf16[4,2,3,16,512]{4,3,2,1,0:T(8,128)(2,1)S(1)} %gather_fusion.1), channel_id=1, source_target_pairs={{0,24},{1,25},{2,26},{3,27},{4,28},{5,29},{6,30},{7,31},{8,0},{9,1... | collective-permute-start | bytes 1179656 | tf_op jit(solution)/shard_map/ppermute | solution.py:58
  170.6 3.9 %collective-permute-start.23 = (bf16[2,2,8,32,512]{4,3,2,1,0:T(8,128)(2,1)S(1)}, bf16[2,2,8,32,512]{4,3,2,1,0:T(8,128)(2,1)S(1)}, u32[]{:S(2)}, u32[]{:S(2)}) collective-permute-start(bf16[2,2,8,32,512]{4,3,2,1,0:T(8,128)(2,1)S(1)} %fusion.1), channel_id=1, source_target_pairs={{0,32},{1,33},{2,34},{3,35},{4,36},{5,37},{6,38},{7,39},{8,40},{9,... | collective-permute-start | bytes 3145736 | tf_op jit(solution)/shard_map/ppermute | solution.py:58

commit v2 on v0

v2 whole, which is shorter than its diff:
```python
import functools

import jax
import jax.numpy as jnp
from jax import lax
from jax.experimental import pallas as pl
from jax.experimental.pallas import tpu as pltpu
from jax.sharding import PartitionSpec as P

F32 = jnp.float32
BF16 = jnp.bfloat16
BOTH = ("ch", "tile")


def device_pairs(move):
    pairs = []
    for ch in range(4):
        for tile in range(32):
            x, core = (ch // 2) * 2 + (tile // 4) % 2, ch % 2
            y, z = tile // 8, tile % 4
            to = move(x, y, z, core)
            if to is not None:
                tx, ty, tz, tc = to
                target = ((tx // 2) * 2 + tc) * 32 + (ty * 2 + tx % 2) * 4 + tz
                pairs.append((ch * 32 + tile, target))
    return pairs


def around(axis, by):
    def move(x, y, z, core):
        at = [x, y, z]
        at[axis] = (at[axis] + by) % 4
        return (*at, core)

    return device_pairs(move)


def around_by_core(first, by):
    def move(x, y, z, core):
        at = [x, y, z]
        at[first if core == 0 else 3 - first] = (at[first if core == 0 else 3 - first] + by) % 4
        return (*at, core)

    return device_pairs(move)


def column_step(by):
    def move(x, y, z, core):
        return (x, y, z + by, core) if 0 <= z + by < 4 else None

    return device_pairs(move)


def row_step(by):
    def move(x, y, z, core):
        row = y * 2 + x % 2 + by
        return ((x // 2) * 2 + row % 2, row // 2, z, core) if 0 <= row < 8 else None

    return device_pairs(move)


ACROSS = around(0, 2)
BESIDE = device_pairs(lambda x, y, z, core: (x ^ 1, y, z, core))
DIAGONAL = device_pairs(lambda x, y, z, core: (x ^ 3, y, z, core))
CORES = device_pairs(lambda x, y, z, core: (x, y, z, 1 - core))


def send(value, pairs):
    return lax.ppermute(value, BOTH, pairs)


def forward(frames):
    d1, d2, d3, d4, d5 = frames
    a, b = d4 - 4.0 * d2, d3 - 4.0 * d1
    c, e = d4 - d2, d3 - d1
    e = e + e
    return a - d2, a + b, a - b, c + e, c - e, d5 - d3 - (e + e)


def backward(m):
    p, q, r, s = m[1] + m[2], m[1] - m[2], m[3] + m[4], m[3] - m[4]
    s = s + s
    return m[0] + p + r, q + s, p + 4.0 * r, q + 4.0 * s + m[5]


TAPS = (
    (1 / 4, 0, 0),
    (-1 / 6, -1 / 6, -1 / 6),
    (-1 / 6, 1 / 6, -1 / 6),
    (1 / 24, 1 / 12, 1 / 6),
    (1 / 24, -1 / 12, 1 / 6),
    (0, 0, 1),
)


def from_left(x):
    return jnp.concatenate([pltpu.roll(x[24:32], 1, 0), x[0:24]], axis=0)


def from_right(x):
    return jnp.concatenate([x[8:32], pltpu.roll(x[0:8], 7, 0)], axis=0)


def pack_kernel(pos_ref, c0, c1, c2, c3, x_ref, rows):
    xhi, core = pos_ref[0], pos_ref[1]
    ch = xhi * 2 + core

    def one(i, _):
        b, f = i // 5, i % 5
        to = jnp.where(xhi == 1, 4 - f, f)
        for r, cells in enumerate((c0, c1, c2, c3)):
            rows[r] = cells[pl.ds(pl.multiple_of(i * 320, 32), 320), :].astype(F32)
            for h in range(10):
                tile = jnp.concatenate([rows[r, pl.ds(h * 32 + q, 8, stride=4), :] for q in range(4)], axis=0)
                x_ref[ch ^ r, b, pl.ds(pl.multiple_of((h * 5 + to) * 32, 32), 32), :] = tile.astype(BF16)
        return 0

    lax.fori_loop(0, 10, one, 0)


def pack_cells(position, pieces):
    vmem = pl.BlockSpec(memory_space=pltpu.VMEM)
    return pl.pallas_call(
        pack_kernel,
        out_shape=jax.ShapeDtypeStruct((4, 2, 1600, 128), BF16),
        in_specs=[pl.BlockSpec(memory_space=pltpu.SMEM)] + [vmem] * 4,
        out_specs=vmem,
        scratch_shapes=[pltpu.VMEM((4, 320, 128), F32)],
        compiler_params=pltpu.CompilerParams(vmem_limit_bytes=32 * 2**20),
        name="pack_cells",
    )(position, *pieces)


def block_kernel(pos_ref, x_ref, p0, p1, p2, p3, k_ref, kept_ref, sent_ref, w_scr, t0, t1, acc, out_ref):
    xhi, core, y, z, xlo = (pos_ref[i] for i in range(5))
    for r, piece in enumerate((p0, p1, p2, p3)):
        for o in range(4):
            py = jnp.where(core == 0, y + r, y + o) % 4
            pz = jnp.where(core == 0, z + o, z + r) % 4
            for p in range(2):
                row = pl.multiple_of(((py * 2 + (xlo ^ p)) * 4 + pz) * 16, 16)
                for half in range(2):
                    for g in range(3):
                        w_scr[g, half, pl.ds(row, 16), :] = piece[o, half, p, g]

    def weights(g, c):
        return w_scr[g, c // 2, :, pl.ds(pl.multiple_of((c % 2) * 256, 256), 256)]

    def expand(s, row, g, t):
        b, c = s // 4, s % 4
        at = pl.ds(pl.multiple_of(row * 160, 32), 160)
        cells = jnp.concatenate([x_ref[m, b, at, :] for m in range(4)], axis=1)
        half = jnp.dot(cells, weights(g, c), preferred_element_type=F32)
        half = half * jnp.tanh(half) + half
        for q in range(2):
            frames = [half[f * 32:(f + 1) * 32, q * 128:(q + 1) * 128] for f in range(5)]
            for m, v in enumerate(forward(frames)):
                t[g * 2 + q, m, row] = v

    def filtered(t, group, g, tap, h):
        terms = []
        for m in range(6):
            sums = [None] * 3
            for j in range(3):
                x = t[group, m, h + j]
                for l in range(3):
                    p = x * k_ref[m, j * 3 + l, g, pl.ds(tap, 1), :]
                    sums[l] = p if sums[l] is None else sums[l] + p
            terms.append(sums[1] + from_left(sums[0]) + from_right(sums[2]))
        return backward(terms)

    def gated(t, c, h):
        cols = []
        for q in range(2):
            value = filtered(t, q, 0, c * 2 + q, h)
            gate = filtered(t, 2 + q, 1, c * 2 + q, h)
            cols.append(jnp.concatenate(
                [(v * (u * jnp.tanh(u) + u)).astype(BF16) for v, u in zip(value, gate)], axis=0))
        return jnp.concatenate(cols, axis=1)

    def project(s, it, hidden):
        b, c = s // 4, s % 4
        new = lax.dot_general(
            jnp.concatenate(hidden, axis=0), weights(2, c), (((1,), (1,)), ((), ())),
            preferred_element_type=F32)
        at = pl.ds(pl.multiple_of(it * 512, 512), 512)
        kept = []
        for r in range(4):
            for f in range(4):
                true = jnp.where(xhi == 1, 3 - f, f)
                cells_at = pl.ds(pl.multiple_of(((it * 4 + r + 1) * 5 + f) * 32, 32), 32)
                cells = jnp.concatenate([x_ref[m, b, cells_at, :] for m in range(4)], axis=1)
                kept.append(jnp.where(core == true // 2, cells.astype(F32), 0.0))
        total = new + jnp.where(c == 0, jnp.concatenate(kept, axis=0), acc[at, :])
        acc[at, :] = total
        for r in range(4):
            for f in range(4):
                true = jnp.where(xhi == 1, 3 - f, f)
                out_ref[true // 2 ^ core, b, true % 2, it * 4 + r] = total[(r * 4 + f) * 32:(r * 4 + f + 1) * 32]

    def first(row, _):
        for g in range(2):
            expand(0, row, g, t0)
        return 0

    lax.fori_loop(0, 10, first, 0)

    def step(s, now, later):
        def half(it, _):
            hidden = []
            for r in range(4):
                if later is not None:
                    for u in range(*((0, 3), (3, 6), (6, 8), (8, 10))[r]):
                        expand(s + 1, it * 5 + u % 5, u // 5, later)
                hidden.append(gated(now, s % 4, it * 4 + r))
            project(s, it, hidden)
            return 0

        lax.fori_loop(0, 2, half, 0)

    def pair(i, _):
        step(2 * i, t0, t1)
        step(2 * i + 1, t1, t0)
        return 0

    lax.fori_loop(0, 3, pair, 0)
    step(6, t0, t1)
    step(7, t1, None)

    def move(i, _):
        b, f, h = i // 16, i // 8 % 2, i % 8
        kept_ref[b, f, h] = out_ref[0, b, f, h]
        sent_ref[b, f, h] = out_ref[1, b, f, h].astype(BF16)
        return 0

    lax.fori_loop(0, 32, move, 0, unroll=2)


def run_block(position, cells, weights, taps):
    vmem = pl.BlockSpec(memory_space=pltpu.VMEM)
    return pl.pallas_call(
        block_kernel,
        out_shape=[jax.ShapeDtypeStruct((2, 2, 8, 32, 512), t) for t in (F32, BF16)],
        in_specs=[pl.BlockSpec(memory_space=pltpu.SMEM)] + [vmem] * 6,
        out_specs=[vmem] * 2,
        scratch_shapes=[
            pltpu.VMEM((3, 2, 512, 512), BF16),
            pltpu.VMEM((4, 6, 10, 32, 128), F32),
            pltpu.VMEM((4, 6, 10, 32, 128), F32),
            pltpu.VMEM((1024, 512), F32),
            pltpu.VMEM((2, 2, 2, 8, 32, 512), F32),
        ],
        compiler_params=pltpu.CompilerParams(vmem_limit_bytes=52 * 2**20),
        name="gated_block",
    )(position, cells, *weights, taps)


def finish_kernel(kept, received, out_ref, rows):
    def one(i, _):
        b, f, h = i // 16, i // 8 % 2, i % 8
        total = kept[b, f, h] + received[b, f, h].astype(F32)
        for v in range(4):
            for q in range(4):
                rows[v, pl.ds(q, 8, stride=4), :] = total[q * 8:(q + 1) * 8, v * 128:(v + 1) * 128]
        for v in range(4):
            out_ref[b, f, h, :, v * 128:(v + 1) * 128] = rows[v, 0:30, :].astype(BF16)
        return 0

    lax.fori_loop(0, 32, one, 0)


def finish(kept, received):
    vmem = pl.BlockSpec(memory_space=pltpu.VMEM)
    return pl.pallas_call(
        finish_kernel,
        out_shape=jax.ShapeDtypeStruct((2, 2, 8, 30, 512), BF16),
        in_specs=[vmem] * 2,
        out_specs=vmem,
        scratch_shapes=[pltpu.VMEM((4, 32, 128), F32)],
        compiler_params=pltpu.CompilerParams(vmem_limit_bytes=32 * 2**20),
        name="finish",
    )(kept, received)


def on_device(latent, expand_weight, depth_kernel, project_weight):
    ch, tile = lax.axis_index("ch"), lax.axis_index("tile")
    xhi, core = ch // 2, ch % 2
    y, xlo, z = tile // 8, (tile // 4) % 2, tile % 4
    position = jnp.stack([xhi, core, y, z, xlo]).astype(jnp.int32)
    cells = latent[:, :, 0]

    half = expand_weight * jnp.asarray(0.5, BF16)
    shard = jnp.stack([half[:, 0], half[:, 1], project_weight.T])
    shard = jnp.stack([shard, send(shard, BESIDE), send(shard, ACROSS), send(shard, DIAGONAL)])
    shard = shard.reshape(2, 2, 3, 16, 512)
    above = send(cells[:, :, 7], row_step(1))
    below = send(cells[:, :, 0], row_step(-1))

    def edge(column):
        return jnp.concatenate([above[:, :, None, column], cells[:, :, :, column], below[:, :, None, column]], axis=2)

    first, last, shard = lax.optimization_barrier((edge(0), edge(29), shard))
    shard = jnp.stack([shard] + [send(shard, around_by_core(2, -by)) for by in (1, 2, 3)])
    left = send(last, column_step(1))
    right = send(first, column_step(-1))
    tall = jnp.concatenate([above[:, :, None], cells, below[:, :, None]], axis=2)
    tall = jnp.concatenate([tall, right[:, :, :, None], left[:, :, :, None]], axis=3)
    own = lax.dynamic_slice_in_dim(tall, 3 * xhi, 5, 1).reshape(3200, 128)
    other = lax.dynamic_slice_in_dim(tall, 3 * (1 - xhi), 5, 1).reshape(3200, 128)
    taps = depth_kernel.reshape(3, 9, 2, 4, 128)
    taps = jnp.where(xhi == 1, taps[::-1], taps)
    other, shard = lax.optimization_barrier((jnp.concatenate([other, taps.reshape(216, 128).astype(BF16)]), shard))
    across = send(other, ACROSS)
    weights = [shard] + [send(shard, around_by_core(1, -by)) for by in (1, 2, 3)]
    across, weights[1] = lax.optimization_barrier((across, weights[1]))
    there = [send(own, CORES), send(across[:3200], CORES)]
    taps = jnp.concatenate([taps, across[3200:].astype(F32).reshape(3, 9, 2, 4, 128)[::-1]], axis=3)
    scale = jnp.array([1.0, 0.5], F32)[None, :, None, None]
    taps = jnp.stack([sum(row[i] * taps[i] for i in range(3) if row[i]) * scale for row in TAPS])

    packed = pack_cells(position, [own, there[0], across, there[1]])
    kept, sent = run_block(position, packed, weights, taps)
    return finish(kept, send(sent, CORES))[:, :, None]


def solution(mesh):
    return jax.shard_map(
        on_device,
        mesh=mesh,
        in_specs=(
            P(None, None, "tile", None, None, "ch"),
            P("tile", None, "ch"),
            P(None, None, None, None, "ch"),
            P("ch", "tile"),
        ),
        out_specs=P(None, "ch", "tile", None, None, None),
        check_vma=False,
    )
```

time: 628 us -> 116 us (0.18)
  waiting for transfers between devices: 283 us -> 20.1 us
  other arithmetic: 124 us -> 4.51 us
  blocking collectives: 100 us -> 0 us
  local copies, waits for them, and re-layouts: 75.6 us -> 13.8 us
  Pallas kernels: 0 us -> 42 us
  starting transfers between devices: 12.4 us -> 35 us
  matrix products: 19.3 us -> 0 us
  between operations: 13.2 us -> 0.24 us
    all_gather x2 -> x0, waiting for transfers between devices: 194 us -> none  [the longest x1 133 us: expand_block(): lax.all_gather(expand_weight, 'tile', axis=0, tiled=True)]
    all_gather x1 -> x0, blocking collectives: 100 us -> none  [on_device(): lax.all_gather(project_weight, 'tile', axis=1, tiled=True)]
    add x1 -> x0, other arithmetic: 91.4 us -> none  [depthwise(): accumulated = accumulated + window.astype(jnp.float32) * kernel[i, j, l]]
    unnamed x12 -> x14, local copies, waits for them, and re-layouts: 67 us -> 3.33 us
    unnamed x4 -> x0, waiting for transfers between devices: 61 us -> none
    pallas_call x0 -> x3, Pallas kernels: none -> 42 us  [the longest x1 39.8 us: run_block(): pl.pallas_call(block_kernel, out_shape=[jax.ShapeDtypeStruct((2, 2, 8, 32...]
    ppermute x4 -> x17, starting transfers between devices: 8.12 us -> 35 us  [send(): return lax.ppermute(value, BOTH, pairs)]
    concatenate x2 -> x3, other arithmetic: 26.5 us -> 2.31 us  [the longest x1 1.26 us: on_device(): jnp.concatenate([tall, right[:, :, :, None], left[:, :, :, None]], axis=3)]
  transfers between devices with their start and end apart: 8 -> 17, of which waited for: 6 -> 5; matrix products, arithmetic and copies ran while one was open for 0% -> 10% of each run, Pallas kernels for 0% -> 1%
where the time goes in v2:
time: 116 us
  Pallas kernels  42 us (36%)
  starting transfers between devices  35 us (30%)
  waiting for transfers between devices  20.1 us (17%)
  local copies, waits for them, and re-layouts  13.8 us (12%)
  other arithmetic  4.51 us (4%)
    pallas_call x1, Pallas kernels, run_block(): pl.pallas_call(block_kernel, out_shape=[jax.ShapeDtypeStruct((2, 2, 8, 32...  39.8 us
    ppermute x17, starting transfers between devices, send(): return lax.ppermute(value, BOTH, pairs)  35 us
    ppermute x17, waiting for transfers between devices, send(): return lax.ppermute(value, BOTH, pairs)  20.1 us
    unnamed x14, local copies, waits for them, and re-layouts  3.33 us
  transfers between devices with their start and end apart: 17, of which 5 were waited for; matrix products, arithmetic and copies ran while one was open for 10% of the time, Pallas kernels for 1%

profile of v2, /device:TPU:1, one launch (start us, length us, event | category | flops | bytes accessed | tf_op | source)
XLA Modules:
  0.0 115.7 jit_solution(7908545552513585721)
XLA Ops:
  0.0 0.9 copy_multiply_fusion
  0.9 0.7 fusion.2
  1.6 2.1 %collective-permute-start.2 = (bf16[3,16,512]{2,1,0:T(8,128)(2,1)S(1)}, bf16[3,16,512]{2,1,0:T(8,128)(2,1)S(1)}, u32[]{:S(2)}, u32[]{:S(2)}) collective-permute-start(bf16[3,16,512]{2,1,0:T(8,128)(2,1)S(1)} %get-tuple-element.41), channel_id=1, source_target_pairs={{0,4},{1,5},{2,6},{3,7},{4,0},{5,1},{6,2},{7,3},{8,12},{9,13},{10,... | collective-permute-start | bytes 147464 | tf_op jit(solution)/shard_map/ppermute | solution.py:69
  3.7 2.5 %collective-permute-start.3 = (bf16[3,16,512]{2,1,0:T(8,128)(2,1)S(1)}, bf16[3,16,512]{2,1,0:T(8,128)(2,1)S(1)}, u32[]{:S(2)}, u32[]{:S(2)}) collective-permute-start(bf16[3,16,512]{2,1,0:T(8,128)(2,1)S(1)} %get-tuple-element.41), channel_id=1, source_target_pairs={{0,64},{1,65},{2,66},{3,67},{4,68},{5,69},{6,70},{7,71},{8,72},{9,... | collective-permute-start | bytes 147464 | tf_op jit(solution)/shard_map/ppermute | solution.py:69
  6.2 0.0 collective-permute-start.4
  6.2 1.9 %fusion.6 = (bf16[2,8,1,30,128]{4,2,3,1,0:T(2,128)(2,1)S(1)}, bf16[2,8,1,30,128]{4,2,3,1,0:T(2,128)(2,1)S(1)}) fusion(bf16[2,8,8,30,128]{4,2,3,1,0:T(8,128)(2,1)} %bitcast.51), kind=kLoop, calls=%fused_computation.32 | loop fusion | bytes 491520 | tf_op jit(solution)/shard_map/slice | solution.py:296
  8.2 2.1 %collective-permute-start = (bf16[2,8,30,128]{3,2,1,0:T(8,128)(2,1)S(1)}, bf16[2,8,30,128]{3,2,1,0:T(8,128)(2,1)S(1)}, u32[]{:S(2)}, u32[]{:S(2)}) collective-permute-start(bf16[2,8,30,128]{3,2,1,0:T(8,128)(2,1)S(1)} %bitcast.65), channel_id=1, source_target_pairs={{0,4},{1,5},{2,6},{3,7},{4,8},{5,9},{6,10},{7,11},{8,12},{9,13},{1... | collective-permute-start | bytes 368648 | tf_op jit(solution)/shard_map/ppermute | solution.py:69
  10.3 1.3 %collective-permute-start.1 = (bf16[2,8,30,128]{3,2,1,0:T(8,128)(2,1)S(1)}, bf16[2,8,30,128]{3,2,1,0:T(8,128)(2,1)S(1)}, u32[]{:S(2)}, u32[]{:S(2)}) collective-permute-start(bf16[2,8,30,128]{3,2,1,0:T(8,128)(2,1)S(1)} %bitcast.66), channel_id=1, source_target_pairs={{4,0},{5,1},{6,2},{7,3},{8,4},{9,5},{10,6},{11,7},{12,8},{13,9},{1... | collective-permute-start | bytes 368648 | tf_op jit(solution)/shard_map/ppermute | solution.py:69
  11.6 0.8 slice_bitcast_fusion
  12.4 0.1 reshape.24
  12.5 0.0 collective-permute-done.2
  12.5 0.0 collective-permute-done.3
  12.5 0.0 collective-permute-done.4
  12.5 0.0 collective-permute-done
  12.6 5.8 %collective-permute-done.1 = bf16[2,8,30,128]{3,2,1,0:T(8,128)(2,1)S(1)} collective-permute-done((bf16[2,8,30,128]{3,2,1,0:T(8,128)(2,1)S(1)}, bf16[2,8,30,128]{3,2,1,0:T(8,128)(2,1)S(1)}, u32[]{:S(2)}, u32[]{:S(2)}) %collective-permute-start.1) | collective-permute-done | bytes 122912 | tf_op jit(solution)/shard_map/ppermute | solution.py:69
  18.4 0.1 pad_maximum_fusion.5
  18.5 1.3 %collective-permute-start.5 = (bf16[2,8,10,128]{3,2,1,0:T(8,128)(2,1)S(1)}, bf16[2,8,10,128]{3,2,1,0:T(8,128)(2,1)S(1)}, u32[]{:S(2)}, u32[]{:S(2)}) collective-permute-start(bf16[2,8,10,128]{3,2,1,0:T(8,128)(2,1)S(1)} %get-tuple-element.14), channel_id=1, source_target_pairs={{1,0},{2,1},{3,2},{5,4},{6,5},{7,6},{9,8},{10,9},{11,10},{13,12},{... | collective-permute-start | bytes 122888 | tf_op jit(solution)/shard_map/ppermute | solution.py:69
  19.8 4.2 %collective-permute-start.6 = (bf16[2,8,10,128]{3,2,1,0:T(8,128)(2,1)S(1)}, bf16[2,8,10,128]{3,2,1,0:T(8,128)(2,1)S(1)}, u32[]{:S(2)}, u32[]{:S(2)}) collective-permute-start(bf16[2,8,10,128]{3,2,1,0:T(8,128)(2,1)S(1)} %get-tuple-element.15), channel_id=1, source_target_pairs={{0,1},{1,2},{2,3},{4,5},{5,6},{6,7},{8,9},{9,10},{10,11},{12,13},{... | collective-permute-start | bytes 122888 | tf_op jit(solution)/shard_map/ppermute | solution.py:69
  24.0 0.9 collective-permute-start.8
  24.9 2.5 %collective-permute-start.9 = (bf16[2,2,3,16,512]{4,3,2,1,0:T(8,128)(2,1)S(1)}, bf16[2,2,3,16,512]{4,3,2,1,0:T(8,128)(2,1)S(1)}, u32[]{:S(2)}, u32[]{:S(2)}) collective-permute-start(bf16[2,2,3,16,512]{4,3,2,1,0:T(8,128)(2,1)S(1)} %bitcast.55), channel_id=1, source_target_pairs={{0,2},{1,3},{2,0},{3,1},{4,6},{5,7},{6,4},{7,5},{8,10},{9,11},{10,... | collective-permute-start | bytes 589832 | tf_op jit(solution)/shard_map/ppermute | solution.py:69
  27.4 0.5 collective-permute-start.10
  27.9 0.2 copy.8
  28.1 0.2 copy.9
  28.3 0.0 collective-permute-done.5
  28.3 0.0 collective-permute-done.6
  28.3 1.3 %pad_maximum_fusion = bf16[2,8,10,32,128]{4,2,3,1,0:T(8,128)(2,1)S(1)} fusion(bf16[2,8,10,1,128]{4,2,3,1,0:T(8,128)(2,1)S(1)} %bitcast.68, bf16[2,8,10,1,128]{4,2,3,1,0:T(8,128)(2,1)S(1)} %bitcast.67, bf16[2,8,1,30,128]{4,2,3,1,0:T(2,128)(2,1)S(1)} %copy.9, bf16[2,8,8,30,128]{4,2,3,1,0:T(8,128)(2,1)S(1)} %bitcast.53, bf16[2,8,1,30,128]{4,2,3,1,0:T(2,128)(2,1)S(1)} %copy.8), kind=kLoop, calls=%fused_computation | loop fusion | flops 6553600 | bytes 2621440 | tf_op jit(solution)/shard_map/concatenate | solution.py:307
  29.6 1.5 %constant_dynamic-slice_fusion = (bf16[2,5,10,32,128]{4,2,3,1,0:T(8,128)(2,1)S(1)}, bf16[2,5,10,32,128]{4,2,3,1,0:T(8,128)(2,1)}) fusion(bf16[2,8,10,32,128]{4,2,3,1,0:T(8,128)(2,1)S(1)} %pad_maximum_fusion, s32[]{:T(128)S(6)} %select_n.46, s32[]{:T(128)S(6)} %select_n.45), kind=kLoop, calls=%fused_computation.28 | loop fusion | bytes 3276808 | tf_op jit(solution)/shard_map/dynamic_slice | solution.py:309
  31.1 0.2 copy.14
  31.3 1.0 pad_maximum_fusion.1
  32.3 0.0 collective-permute-done.8
  32.3 0.0 collective-permute-done.9
  32.3 1.1 collective-permute-done.10
  33.4 0.1 pad_maximum_fusion.2.p0
  33.5 0.0 copy-start.5
  33.5 3.2 %collective-permute-start.11 = (bf16[3416,128]{1,0:T(8,128)(2,1)}, bf16[3416,128]{1,0:T(8,128)(2,1)S(1)}, u32[]{:S(2)}, u32[]{:S(2)}) collective-permute-start(bf16[3416,128]{1,0:T(8,128)(2,1)} %pad_maximum_fusion.1), channel_id=1, source_target_pairs={{0,64},{1,65},{2,66},{3,67},{4,68},{5,69},{6,70},{7,71},{8,72},{9,... | collective-permute-start | bytes 2623496 | tf_op jit(solution)/shard_map/ppermute | solution.py:69
  36.7 1.6 %collective-permute-start.12 = (bf16[4,2,2,3,16,512]{5,4,3,2,1,0:T(8,128)(2,1)S(1)}, bf16[4,2,2,3,16,512]{5,4,3,2,1,0:T(8,128)(2,1)}, u32[]{:S(2)}, u32[]{:S(2)}) collective-permute-start(bf16[4,2,2,3,16,512]{5,4,3,2,1,0:T(8,128)(2,1)S(1)} %pad_maximum_fusion.2.p0), channel_id=1, source_target_pairs={{0,24},{1,25},{2,26},{3,27},{4,28},{5,29},{6,30},{7,31},{8,0},{9,1... | collective-permute-start | bytes 2359304 | tf_op jit(solution)/shard_map/ppermute | solution.py:69
  38.3 0.1 stack.68.pos_ref
  38.4 1.5 %copy.13 = bf16[2,5,10,32,128]{4,3,2,1,0:T(8,128)(2,1)S(1)} copy(bf16[2,5,10,32,128]{4,2,3,1,0:T(8,128)(2,1)} %get-tuple-element.31) | data formatting | bytes 1638400 | tf_op jit(solution)/shard_map/dynamic_slice | solution.py:308
  39.9 5.0 %collective-permute-start.7 = (bf16[3200,128]{1,0:T(8,128)(2,1)S(1)}, bf16[3200,128]{1,0:T(8,128)(2,1)S(1)}, u32[]{:S(2)}, u32[]{:S(2)}) collective-permute-start(bf16[3200,128]{1,0:T(8,128)(2,1)S(1)} %bitcast.48), channel_id=1, source_target_pairs={{0,32},{1,33},{2,34},{3,35},{4,36},{5,37},{6,38},{7,39},{8,40},{9,... | collective-permute-start | bytes 2457608 | tf_op jit(solution)/shard_map/ppermute | solution.py:69
  44.9 1.8 %collective-permute-start.14 = (bf16[4,2,2,3,16,512]{5,4,3,2,1,0:T(8,128)(2,1)S(1)}, bf16[4,2,2,3,16,512]{5,4,3,2,1,0:T(8,128)(2,1)}, u32[]{:S(2)}, u32[]{:S(2)}) collective-permute-start(bf16[4,2,2,3,16,512]{5,4,3,2,1,0:T(8,128)(2,1)S(1)} %pad_maximum_fusion.2.p0), channel_id=1, source_target_pairs={{0,16},{1,17},{2,18},{3,19},{4,20},{5,21},{6,22},{7,23},{8,24},{9,... | collective-permute-start | bytes 2359304 | tf_op jit(solution)/shard_map/ppermute | solution.py:69
  46.7 0.0 collective-permute-start.15
  46.7 9.0 %collective-permute-done.12.p1 = bf16[4,2,2,3,16,512]{5,4,3,2,1,0:T(8,128)(2,1)} collective-permute-done((bf16[4,2,2,3,16,512]{5,4,3,2,1,0:T(8,128)(2,1)S(1)}, bf16[4,2,2,3,16,512]{5,4,3,2,1,0:T(8,128)(2,1)}, u32[]{:S(2)}, u32[]{:S(2)}) %collective-permute-start.12) | collective-permute-done | bytes 786464 | tf_op jit(solution)/shard_map/ppermute | solution.py:69
  55.7 0.6 slice.67
  56.3 0.9 slice.66
  57.2 0.8 rev.7
  58.1 5.8 %collective-permute-start.13 = (bf16[3200,128]{1,0:T(8,128)(2,1)}, bf16[3200,128]{1,0:T(8,128)(2,1)S(1)}, u32[]{:S(2)}, u32[]{:S(2)}) collective-permute-start(bf16[3200,128]{1,0:T(8,128)(2,1)} %slice.66), channel_id=1, source_target_pairs={{0,32},{1,33},{2,34},{3,35},{4,36},{5,37},{6,38},{7,39},{8,40},{9,... | collective-permute-start | bytes 2457608 | tf_op jit(solution)/shard_map/ppermute | solution.py:69
  63.8 0.1 multiply_dynamic-update-slice_fusion.5
  63.9 0.1 multiply_dynamic-update-slice_fusion.4
  64.0 0.1 multiply_dynamic-update-slice_fusion.3
  64.1 0.1 multiply_dynamic-update-slice_fusion.2
  64.1 0.1 multiply_dynamic-update-slice_fusion.1
  64.2 0.1 multiply_dynamic-update-slice_fusion.k_ref
  64.3 0.0 collective-permute-done.7.c1
  64.3 1.7 %collective-permute-done.13.c3 = bf16[3200,128]{1,0:T(8,128)(2,1)S(1)} collective-permute-done((bf16[3200,128]{1,0:T(8,128)(2,1)}, bf16[3200,128]{1,0:T(8,128)(2,1)S(1)}, u32[]{:S(2)}, u32[]{:S(2)}) %collective-permute-start.13) | collective-permute-done | bytes 819232 | tf_op jit(solution)/shard_map/ppermute | solution.py:69
  66.0 1.3 %pack_cells.1.x_ref = bf16[4,2,1600,128]{3,2,1,0:T(8,128)(2,1)S(1)} custom-call(s32[5]{0:T(128)S(1)} %stack.68.pos_ref, bf16[3200,128]{1,0:T(8,128)(2,1)S(1)} %bitcast.49, bf16[3200,128]{1,0:T(8,128)(2,1)S(1)} %collective-permute-done.7.c1, bf16[3416,128]{1,0:T(8,128)(2,1)S(1)} %collective-permute-done.11.c2, bf16[3200,128]{1,0:T(8,128)(2,1)S(1)} %collective-permute-done.13.c3), custom_call_target="tpu_custom_call" | custom-call | tf_op jit(solution)/shard_map/pack_cells/pallas_call | solution.py:123
  67.3 1.7 %copy-done = bf16[4,2,1600,128]{3,2,1,0:T(8,128)(2,1)} copy-done((bf16[4,2,1600,128]{3,2,1,0:T(8,128)(2,1)}, bf16[4,2,1600,128]{3,2,1,0:T(8,128)(2,1)S(1)}, u32[]{:S(2)}) %copy-start) | copy-done | bytes 3276824
  69.0 0.0 collective-permute-done.14.p2
  69.0 0.0 collective-permute-done.15.p3
  69.0 39.8 %gated_block.1 = (f32[2,2,8,32,512]{4,3,2,1,0:T(8,128)}, bf16[2,2,8,32,512]{4,3,2,1,0:T(8,128)(2,1)}) custom-call(s32[5]{0:T(128)S(1)} %stack.68.pos_ref, bf16[4,2,1600,128]{3,2,1,0:T(8,128)(2,1)} %copy-done, bf16[4,2,2,3,16,512]{5,4,3,2,1,0:T(8,128)(2,1)S(1)} %pad_maximum_fusion.2.p0, bf16[4,2,2,3,16,512]{5,4,3,2,1,0:T(8,128)(2,1)} %collective-permute-done.12.p1, ...), custom_call_target="tpu_custom_call" | custom-call | tf_op jit(solution)/shard_map/gated_block/pallas_call | solution.py:241
  108.8 0.4 collective-permute-start.16
  109.1 2.5 %collective-permute-done.16.received = bf16[2,2,8,32,512]{4,3,2,1,0:T(8,128)(2,1)S(1)} collective-permute-done((bf16[2,2,8,32,512]{4,3,2,1,0:T(8,128)(2,1)}, bf16[2,2,8,32,512]{4,3,2,1,0:T(8,128)(2,1)S(1)}, u32[]{:S(2)}, u32[]{:S(2)}) %collective-permute-start.16) | collective-permute-done | bytes 1048608 | tf_op jit(solution)/shard_map/ppermute | solution.py:69
  111.6 1.6 %copy-done.1 = f32[2,2,8,32,512]{4,3,2,1,0:T(8,128)S(1)} copy-done((f32[2,2,8,32,512]{4,3,2,1,0:T(8,128)S(1)}, f32[2,2,8,32,512]{4,3,2,1,0:T(8,128)}, u32[]{:S(2)}) %copy-start.1) | copy-done | bytes 2097176
  113.2 1.0 finish.1
  114.2 1.5 %copy.15 = bf16[2,2,1,8,30,512]{5,3,4,2,1,0:T(8,128)(2,1)} copy(bf16[2,2,1,8,30,512]{5,4,3,1,0,2:T(8,128)(2,1)S(1)} %bitcast.47) | data formatting | bytes 1966080 | tf_op jit(solution)/shard_map/broadcast_in_dim | solution.py:323
  (17 shorter events, 0.2 us)
Async XLA Ops:
  0.0 28.3 %copy-start.2 = (bf16[2,8,1,8,30,128]{5,3,4,2,1,0:T(8,128)(2,1)S(1)}, bf16[2,8,1,8,30,128]{5,3,4,2,1,0:T(8,128)(2,1)}, u32[]{:S(2)}) copy-start(bf16[2,8,1,8,30,128]{5,3,4,2,1,0:T(8,128)(2,1)} %param.5) | copy-start | bytes 2949124
  0.0 12.3 %copy-start.3 = (f32[3,3,3,2,512]{4,3,2,1,0:T(2,128)S(1)}, f32[3,3,3,2,512]{4,3,2,1,0:T(2,128)}, u32[]{:S(2)}) copy-start(f32[3,3,3,2,512]{4,3,2,1,0:T(2,128)} %param.7) | copy-start | bytes 331780
  1.6 10.9 %collective-permute-start.2 = (bf16[3,16,512]{2,1,0:T(8,128)(2,1)S(1)}, bf16[3,16,512]{2,1,0:T(8,128)(2,1)S(1)}, u32[]{:S(2)}, u32[]{:S(2)}) collective-permute-start(bf16[3,16,512]{2,1,0:T(8,128)(2,1)S(1)} %get-tuple-element.41), channel_id=1, source_target_pairs={{0,4},{1,5},{2,6},{3,7},{4,0},{5,1},{6,2},{7,3},{8,12},{9,13},{10,... | collective-permute-start | bytes 147464 | tf_op jit(solution)/shard_map/ppermute | solution.py:69
  3.7 8.8 %collective-permute-start.3 = (bf16[3,16,512]{2,1,0:T(8,128)(2,1)S(1)}, bf16[3,16,512]{2,1,0:T(8,128)(2,1)S(1)}, u32[]{:S(2)}, u32[]{:S(2)}) collective-permute-start(bf16[3,16,512]{2,1,0:T(8,128)(2,1)S(1)} %get-tuple-element.41), channel_id=1, source_target_pairs={{0,64},{1,65},{2,66},{3,67},{4,68},{5,69},{6,70},{7,71},{8,72},{9,... | collective-permute-start | bytes 147464 | tf_op jit(solution)/shard_map/ppermute | solution.py:69
  6.2 6.3 %collective-permute-start.4 = (bf16[3,16,512]{2,1,0:T(8,128)(2,1)S(1)}, bf16[3,16,512]{2,1,0:T(8,128)(2,1)S(1)}, u32[]{:S(2)}, u32[]{:S(2)}) collective-permute-start(bf16[3,16,512]{2,1,0:T(8,128)(2,1)S(1)} %get-tuple-element.41), channel_id=1, source_target_pairs={{0,68},{1,69},{2,70},{3,71},{4,64},{5,65},{6,66},{7,67},{8,76},{9,... | collective-permute-start | bytes 147464 | tf_op jit(solution)/shard_map/ppermute | solution.py:69
  8.2 4.4 %collective-permute-start = (bf16[2,8,30,128]{3,2,1,0:T(8,128)(2,1)S(1)}, bf16[2,8,30,128]{3,2,1,0:T(8,128)(2,1)S(1)}, u32[]{:S(2)}, u32[]{:S(2)}) collective-permute-start(bf16[2,8,30,128]{3,2,1,0:T(8,128)(2,1)S(1)} %bitcast.65), channel_id=1, source_target_pairs={{0,4},{1,5},{2,6},{3,7},{4,8},{5,9},{6,10},{7,11},{8,12},{9,13},{1... | collective-permute-start | bytes 368648 | tf_op jit(solution)/shard_map/ppermute | solution.py:69
  10.3 8.1 %collective-permute-start.1 = (bf16[2,8,30,128]{3,2,1,0:T(8,128)(2,1)S(1)}, bf16[2,8,30,128]{3,2,1,0:T(8,128)(2,1)S(1)}, u32[]{:S(2)}, u32[]{:S(2)}) collective-permute-start(bf16[2,8,30,128]{3,2,1,0:T(8,128)(2,1)S(1)} %bitcast.66), channel_id=1, source_target_pairs={{4,0},{5,1},{6,2},{7,3},{8,4},{9,5},{10,6},{11,7},{12,8},{13,9},{1... | collective-permute-start | bytes 368648 | tf_op jit(solution)/shard_map/ppermute | solution.py:69
  18.5 9.8 %collective-permute-start.5 = (bf16[2,8,10,128]{3,2,1,0:T(8,128)(2,1)S(1)}, bf16[2,8,10,128]{3,2,1,0:T(8,128)(2,1)S(1)}, u32[]{:S(2)}, u32[]{:S(2)}) collective-permute-start(bf16[2,8,10,128]{3,2,1,0:T(8,128)(2,1)S(1)} %get-tuple-element.14), channel_id=1, source_target_pairs={{1,0},{2,1},{3,2},{5,4},{6,5},{7,6},{9,8},{10,9},{11,10},{13,12},{... | collective-permute-start | bytes 122888 | tf_op jit(solution)/shard_map/ppermute | solution.py:69
  19.8 8.5 %collective-permute-start.6 = (bf16[2,8,10,128]{3,2,1,0:T(8,128)(2,1)S(1)}, bf16[2,8,10,128]{3,2,1,0:T(8,128)(2,1)S(1)}, u32[]{:S(2)}, u32[]{:S(2)}) collective-permute-start(bf16[2,8,10,128]{3,2,1,0:T(8,128)(2,1)S(1)} %get-tuple-element.15), channel_id=1, source_target_pairs={{0,1},{1,2},{2,3},{4,5},{5,6},{6,7},{8,9},{9,10},{10,11},{12,13},{... | collective-permute-start | bytes 122888 | tf_op jit(solution)/shard_map/ppermute | solution.py:69
  24.0 8.3 %collective-permute-start.8 = (bf16[2,2,3,16,512]{4,3,2,1,0:T(8,128)(2,1)S(1)}, bf16[2,2,3,16,512]{4,3,2,1,0:T(8,128)(2,1)S(1)}, u32[]{:S(2)}, u32[]{:S(2)}) collective-permute-start(bf16[2,2,3,16,512]{4,3,2,1,0:T(8,128)(2,1)S(1)} %bitcast.54), channel_id=1, source_target_pairs={{0,3},{1,0},{2,1},{3,2},{4,7},{5,4},{6,5},{7,6},{8,11},{9,8},{10,9... | collective-permute-start | bytes 589832 | tf_op jit(solution)/shard_map/ppermute | solution.py:69
  24.9 7.4 %collective-permute-start.9 = (bf16[2,2,3,16,512]{4,3,2,1,0:T(8,128)(2,1)S(1)}, bf16[2,2,3,16,512]{4,3,2,1,0:T(8,128)(2,1)S(1)}, u32[]{:S(2)}, u32[]{:S(2)}) collective-permute-start(bf16[2,2,3,16,512]{4,3,2,1,0:T(8,128)(2,1)S(1)} %bitcast.55), channel_id=1, source_target_pairs={{0,2},{1,3},{2,0},{3,1},{4,6},{5,7},{6,4},{7,5},{8,10},{9,11},{10,... | collective-permute-start | bytes 589832 | tf_op jit(solution)/shard_map/ppermute | solution.py:69
  27.4 6.0 %collective-permute-start.10 = (bf16[2,2,3,16,512]{4,3,2,1,0:T(8,128)(2,1)S(1)}, bf16[2,2,3,16,512]{4,3,2,1,0:T(8,128)(2,1)S(1)}, u32[]{:S(2)}, u32[]{:S(2)}) collective-permute-start(bf16[2,2,3,16,512]{4,3,2,1,0:T(8,128)(2,1)S(1)} %bitcast.56), channel_id=1, source_target_pairs={{0,1},{1,2},{2,3},{3,0},{4,5},{5,6},{6,7},{7,4},{8,9},{9,10},{10,1... | collective-permute-start | bytes 589832 | tf_op jit(solution)/shard_map/ppermute | solution.py:69
  33.5 30.3 %copy-start.5 = (f32[2]{0:T(128)S(1)}, f32[2]{0:T(128)}, u32[]{:S(2)}) copy-start(f32[2]{0:T(128)} %constant.89) | copy-start | bytes 28
  33.5 22.2 %collective-permute-start.11 = (bf16[3416,128]{1,0:T(8,128)(2,1)}, bf16[3416,128]{1,0:T(8,128)(2,1)S(1)}, u32[]{:S(2)}, u32[]{:S(2)}) collective-permute-start(bf16[3416,128]{1,0:T(8,128)(2,1)} %pad_maximum_fusion.1), channel_id=1, source_target_pairs={{0,64},{1,65},{2,66},{3,67},{4,68},{5,69},{6,70},{7,71},{8,72},{9,... | collective-permute-start | bytes 2623496 | tf_op jit(solution)/shard_map/ppermute | solution.py:69
  36.7 19.0 %collective-permute-start.12 = (bf16[4,2,2,3,16,512]{5,4,3,2,1,0:T(8,128)(2,1)S(1)}, bf16[4,2,2,3,16,512]{5,4,3,2,1,0:T(8,128)(2,1)}, u32[]{:S(2)}, u32[]{:S(2)}) collective-permute-start(bf16[4,2,2,3,16,512]{5,4,3,2,1,0:T(8,128)(2,1)S(1)} %pad_maximum_fusion.2.p0), channel_id=1, source_target_pairs={{0,24},{1,25},{2,26},{3,27},{4,28},{5,29},{6,30},{7,31},{8,0},{9,1... | collective-permute-start | bytes 2359304 | tf_op jit(solution)/shard_map/ppermute | solution.py:69
  38.4 25.5 %copy-start.4 = (f32[2]{0:T(128)S(1)}, f32[2]{0:T(128)}, u32[]{:S(2)}) copy-start(f32[2]{0:T(128)} %constant.85.clone) | copy-start | bytes 28
  39.9 24.3 %collective-permute-start.7 = (bf16[3200,128]{1,0:T(8,128)(2,1)S(1)}, bf16[3200,128]{1,0:T(8,128)(2,1)S(1)}, u32[]{:S(2)}, u32[]{:S(2)}) collective-permute-start(bf16[3200,128]{1,0:T(8,128)(2,1)S(1)} %bitcast.48), channel_id=1, source_target_pairs={{0,32},{1,33},{2,34},{3,35},{4,36},{5,37},{6,38},{7,39},{8,40},{9,... | collective-permute-start | bytes 2457608 | tf_op jit(solution)/shard_map/ppermute | solution.py:69
  44.9 24.0 %collective-permute-start.14 = (bf16[4,2,2,3,16,512]{5,4,3,2,1,0:T(8,128)(2,1)S(1)}, bf16[4,2,2,3,16,512]{5,4,3,2,1,0:T(8,128)(2,1)}, u32[]{:S(2)}, u32[]{:S(2)}) collective-permute-start(bf16[4,2,2,3,16,512]{5,4,3,2,1,0:T(8,128)(2,1)S(1)} %pad_maximum_fusion.2.p0), channel_id=1, source_target_pairs={{0,16},{1,17},{2,18},{3,19},{4,20},{5,21},{6,22},{7,23},{8,24},{9,... | collective-permute-start | bytes 2359304 | tf_op jit(solution)/shard_map/ppermute | solution.py:69
  46.7 22.3 %collective-permute-start.15 = (bf16[4,2,2,3,16,512]{5,4,3,2,1,0:T(8,128)(2,1)S(1)}, bf16[4,2,2,3,16,512]{5,4,3,2,1,0:T(8,128)(2,1)}, u32[]{:S(2)}, u32[]{:S(2)}) collective-permute-start(bf16[4,2,2,3,16,512]{5,4,3,2,1,0:T(8,128)(2,1)S(1)} %pad_maximum_fusion.2.p0), channel_id=1, source_target_pairs={{0,8},{1,9},{2,10},{3,11},{4,12},{5,13},{6,14},{7,15},{8,16},{9,17... | collective-permute-start | bytes 2359304 | tf_op jit(solution)/shard_map/ppermute | solution.py:69
  58.1 7.9 %collective-permute-start.13 = (bf16[3200,128]{1,0:T(8,128)(2,1)}, bf16[3200,128]{1,0:T(8,128)(2,1)S(1)}, u32[]{:S(2)}, u32[]{:S(2)}) collective-permute-start(bf16[3200,128]{1,0:T(8,128)(2,1)} %slice.66), channel_id=1, source_target_pairs={{0,32},{1,33},{2,34},{3,35},{4,36},{5,37},{6,38},{7,39},{8,40},{9,... | collective-permute-start | bytes 2457608 | tf_op jit(solution)/shard_map/ppermute | solution.py:69
  67.3 1.7 %copy-start = (bf16[4,2,1600,128]{3,2,1,0:T(8,128)(2,1)}, bf16[4,2,1600,128]{3,2,1,0:T(8,128)(2,1)S(1)}, u32[]{:S(2)}) copy-start(bf16[4,2,1600,128]{3,2,1,0:T(8,128)(2,1)S(1)} %pack_cells.1.x_ref) | copy-start | bytes 9830404
  108.8 2.9 %collective-permute-start.16 = (bf16[2,2,8,32,512]{4,3,2,1,0:T(8,128)(2,1)}, bf16[2,2,8,32,512]{4,3,2,1,0:T(8,128)(2,1)S(1)}, u32[]{:S(2)}, u32[]{:S(2)}) collective-permute-start(bf16[2,2,8,32,512]{4,3,2,1,0:T(8,128)(2,1)} %get-tuple-element.22), channel_id=1, source_target_pairs={{0,32},{1,33},{2,34},{3,35},{4,36},{5,37},{6,38},{7,39},{8,40},{9,... | collective-permute-start | bytes 3145736 | tf_op jit(solution)/shard_map/ppermute | solution.py:69
  111.6 1.6 %copy-start.1 = (f32[2,2,8,32,512]{4,3,2,1,0:T(8,128)S(1)}, f32[2,2,8,32,512]{4,3,2,1,0:T(8,128)}, u32[]{:S(2)}) copy-start(f32[2,2,8,32,512]{4,3,2,1,0:T(8,128)} %get-tuple-element.21.kept) | copy-start | bytes 6291460

commit v3 on v2

v3 whole, which is shorter than its diff:
```python
import functools

import jax
import jax.numpy as jnp
from jax import lax
from jax.experimental import pallas as pl
from jax.experimental.pallas import tpu as pltpu
from jax.sharding import PartitionSpec as P

F32 = jnp.float32
BF16 = jnp.bfloat16
BOTH = ("ch", "tile")


def device_pairs(move):
    pairs = []
    for ch in range(4):
        for tile in range(32):
            x, core = (ch // 2) * 2 + (tile // 4) % 2, ch % 2
            y, z = tile // 8, tile % 4
            to = move(x, y, z, core)
            if to is not None:
                tx, ty, tz, tc = to
                target = ((tx // 2) * 2 + tc) * 32 + (ty * 2 + tx % 2) * 4 + tz
                pairs.append((ch * 32 + tile, target))
    return pairs


def around(axis, by):
    def move(x, y, z, core):
        at = [x, y, z]
        at[axis] = (at[axis] + by) % 4
        return (*at, core)

    return device_pairs(move)


def around_by_core(first, by):
    def move(x, y, z, core):
        at = [x, y, z]
        at[first if core == 0 else 3 - first] = (at[first if core == 0 else 3 - first] + by) % 4
        return (*at, core)

    return device_pairs(move)


def column_step(by):
    def move(x, y, z, core):
        return (x, y, z + by, core) if 0 <= z + by < 4 else None

    return device_pairs(move)


def row_step(by):
    def move(x, y, z, core):
        row = y * 2 + x % 2 + by
        return ((x // 2) * 2 + row % 2, row // 2, z, core) if 0 <= row < 8 else None

    return device_pairs(move)


ACROSS = around(0, 2)
BESIDE = device_pairs(lambda x, y, z, core: (x ^ 1, y, z, core))
DIAGONAL = device_pairs(lambda x, y, z, core: (x ^ 3, y, z, core))
CORES = device_pairs(lambda x, y, z, core: (x, y, z, 1 - core))


def send(value, pairs):
    return lax.ppermute(value, BOTH, pairs)


def forward(frames):
    d1, d2, d3, d4, d5 = frames
    a, b = d4 - 4.0 * d2, d3 - 4.0 * d1
    c, e = d4 - d2, d3 - d1
    e = e + e
    return a - d2, a + b, a - b, c + e, c - e, d5 - d3 - (e + e)


def backward(m):
    p, q, r, s = m[1] + m[2], m[1] - m[2], m[3] + m[4], m[3] - m[4]
    s = s + s
    return m[0] + p + r, q + s, p + 4.0 * r, q + 4.0 * s + m[5]


TAPS = (
    (1 / 4, 0, 0),
    (-1 / 6, -1 / 6, -1 / 6),
    (-1 / 6, 1 / 6, -1 / 6),
    (1 / 24, 1 / 12, 1 / 6),
    (1 / 24, -1 / 12, 1 / 6),
    (0, 0, 1),
)


ROW_TAPS = ((1, 0, 0), (1 / 2, 1 / 2, 1 / 2), (1 / 2, -1 / 2, 1 / 2), (0, 0, 1))


def from_left(x):
    return jnp.concatenate([pltpu.roll(x[24:32], 1, 0), x[0:24]], axis=0)


def from_right(x):
    return jnp.concatenate([x[8:32], pltpu.roll(x[0:8], 7, 0)], axis=0)


def pack_kernel(pos_ref, m0, m1, m2, m3, own_rim, across_rim, core_rim, x_ref, rows):
    xhi, core = pos_ref[0], pos_ref[1]
    ch = xhi * 2 + core

    def one(i, _):
        b, f = i // 5, i % 5
        to = jnp.where(xhi == 1, 4 - f, f)
        for r, main in enumerate((m0, m1, m2, m3)):
            rim = (own_rim, core_rim, across_rim, core_rim)[r]
            at = pl.multiple_of(i * 80 + (800 if r == 3 else 0), 16)
            strips = rim[pl.ds(at, 80), :].astype(F32)
            rows[r, 0:32, :] = strips[0:32]
            rows[r, 288:320, :] = strips[32:64]
            for h in range(8):
                rows[r, (h + 1) * 32:(h + 1) * 32 + 32, :] = main[pl.ds(pl.multiple_of(i * 256 + h * 32, 32), 32), :].astype(F32)
            rows[r, pl.ds(62, 8, stride=32), :] = strips[64:72]
            rows[r, pl.ds(63, 8, stride=32), :] = strips[72:80]
            for h in range(10):
                tile = jnp.concatenate([rows[r, pl.ds(h * 32 + q, 8, stride=4), :] for q in range(4)], axis=0)
                x_ref[ch ^ r, b, pl.ds(pl.multiple_of((h * 5 + to) * 32, 32), 32), :] = tile.astype(BF16)
        return 0

    lax.fori_loop(0, 10, one, 0)


def pack_cells(position, pieces):
    vmem = pl.BlockSpec(memory_space=pltpu.VMEM)
    return pl.pallas_call(
        pack_kernel,
        out_shape=jax.ShapeDtypeStruct((4, 2, 1600, 128), BF16),
        in_specs=[pl.BlockSpec(memory_space=pltpu.SMEM)] + [vmem] * 7,
        out_specs=vmem,
        scratch_shapes=[pltpu.VMEM((4, 320, 128), F32)],
        compiler_params=pltpu.CompilerParams(vmem_limit_bytes=32 * 2**20),
        name="pack_cells",
    )(position, *pieces)


def block_kernel(pos_ref, x_ref, p0, p1, p2, p3, k_ref, kept_ref, sent_ref, w_scr, wp_scr, t0, t1, hidden, acc, rows):
    xhi, core, y, z, xlo = (pos_ref[i] for i in range(5))
    for r, piece in enumerate((p0, p1, p2, p3)):
        for o in range(4):
            py = jnp.where(core == 0, y + r, y + o) % 4
            pz = jnp.where(core == 0, z + o, z + r) % 4
            for p in range(2):
                row = pl.ds(pl.multiple_of(((py * 2 + (xlo ^ p)) * 4 + pz) * 16, 16), 16)
                for half in range(2):
                    for g in range(2):
                        w_scr[g, half, row, :] = piece[o, half, p, g]
                    wp_scr[row, half * 512:(half + 1) * 512] = piece[o, half, p, 2]

    def weights(g, c):
        return w_scr[g, c // 2, :, pl.ds(pl.multiple_of((c % 2) * 256, 256), 256)]

    def expand(s, row, g, t):
        b, c = s // 4, s % 4
        at = pl.ds(pl.multiple_of(row * 160, 32), 160)
        cells = jnp.concatenate([x_ref[m, b, at, :] for m in range(4)], axis=1)
        half = jnp.dot(cells, weights(g, c), preferred_element_type=F32)
        half = half * jnp.tanh(half) + half
        for q in range(2):
            frames = [half[f * 32:(f + 1) * 32, q * 128:(q + 1) * 128] for f in range(5)]
            for m, v in enumerate(forward(frames)):
                t[g * 2 + q, m, row] = v

    def filtered(t, group, g, tap, h):
        terms = [[], []]
        for m in range(6):
            d = [t[group, m, h + i] for i in range(4)]
            d = [d[0] - d[2], d[1] + d[2], d[2] - d[1], d[1] - d[3]]
            p = []
            for i in range(4):
                x = [d[i] * k_ref[m, i * 3 + l, g, pl.ds(tap, 1), :] for l in range(3)]
                p.append(x[1] + from_left(x[0]) + from_right(x[2]))
            terms[0].append(p[0] + p[1] + p[2])
            terms[1].append(p[1] - p[2] - p[3])
        return [backward(m) for m in terms]

    def gate_rows(t, c, h):
        for q in range(2):
            value = filtered(t, q, 0, c * 2 + q, h)
            gate = filtered(t, 2 + q, 1, c * 2 + q, h)
            for r in range(2):
                both = [(v * (u * jnp.tanh(u) + u)).astype(BF16) for v, u in zip(value[r], gate[r])]
                at = pl.ds(pl.multiple_of((h + r) * 128, 128), 128)
                hidden[c, at, q * 128:(q + 1) * 128] = jnp.concatenate(both, axis=0)

    def project(b):
        def part(i, _):
            at = pl.ds(pl.multiple_of(i * 512, 512), 512)
            units = jnp.concatenate([hidden[c, at, :] for c in range(4)], axis=1)
            new = lax.dot_general(units, wp_scr[...], (((1,), (1,)), ((), ())), preferred_element_type=F32)
            acc[b, at, :] = new
            return 0

        lax.fori_loop(0, 2, part, 0)

    def first(row, _):
        for g in range(2):
            expand(0, row, g, t0)
        return 0

    lax.fori_loop(0, 10, first, 0)

    def step(s, now, later):
        def half(it, _):
            for r in range(2):
                gate_rows(now, s % 4, it * 4 + 2 * r)
                if later is not None:
                    for u in range(5):
                        expand(s + 1, it * 5 + u, r, later)
            return 0

        lax.fori_loop(0, 2, half, 0)

    def pair(i, _):
        step(2 * i, t0, t1)
        step(2 * i + 1, t1, t0)

        @pl.when(i == 1)
        def _():
            project(0)

        return 0

    lax.fori_loop(0, 3, pair, 0)
    step(6, t0, t1)
    step(7, t1, None)
    project(1)

    def move(i, _):
        b, f, h = i // 16, i // 8 % 2, i % 8
        for slot in range(2):
            true = (core ^ slot) * 2 + f
            frame = jnp.where(xhi == 1, 3 - true, true)
            at = pl.ds(pl.multiple_of((h * 4 + frame) * 32, 32), 32)
            total = acc[b, at, :]
            if slot == 0:
                cells_at = pl.ds(pl.multiple_of(((h + 1) * 5 + frame) * 32, 32), 32)
                cells = jnp.concatenate([x_ref[m, b, cells_at, :] for m in range(4)], axis=1)
                total = total + cells.astype(F32)
            for v in range(4):
                for q in range(4):
                    rows[slot * 4 + v, pl.ds(q, 8, stride=4), :] = total[q * 8:(q + 1) * 8, v * 128:(v + 1) * 128]
            total = jnp.concatenate([rows[slot * 4 + v] for v in range(4)], axis=1)
            if slot == 0:
                kept_ref[b, f, h] = total
            else:
                sent_ref[b, f, h] = total.astype(BF16)
        return 0

    lax.fori_loop(0, 32, move, 0)


def run_block(position, cells, weights, taps):
    vmem = pl.BlockSpec(memory_space=pltpu.VMEM)
    return pl.pallas_call(
        block_kernel,
        out_shape=[jax.ShapeDtypeStruct((2, 2, 8, 32, 512), t) for t in (F32, BF16)],
        in_specs=[pl.BlockSpec(memory_space=pltpu.SMEM)] + [vmem] * 6,
        out_specs=[vmem] * 2,
        scratch_shapes=[
            pltpu.VMEM((2, 2, 512, 512), BF16),
            pltpu.VMEM((512, 1024), BF16),
            pltpu.VMEM((4, 6, 10, 32, 128), F32),
            pltpu.VMEM((4, 6, 10, 32, 128), F32),
            pltpu.VMEM((4, 1024, 256), BF16),
            pltpu.VMEM((2, 1024, 512), F32),
            pltpu.VMEM((8, 32, 128), F32),
        ],
        compiler_params=pltpu.CompilerParams(vmem_limit_bytes=52 * 2**20),
        name="gated_block",
    )(position, cells, *weights, taps)


def on_device(latent, expand_weight, depth_kernel, project_weight):
    ch, tile = lax.axis_index("ch"), lax.axis_index("tile")
    xhi, core = ch // 2, ch % 2
    y, xlo, z = tile // 8, (tile // 4) % 2, tile % 4
    position = jnp.stack([xhi, core, y, z, xlo]).astype(jnp.int32)
    cells = latent[:, :, 0]

    half = expand_weight * jnp.asarray(0.5, BF16)
    shard = jnp.stack([half[:, 0], half[:, 1], project_weight.T])
    shard = jnp.stack([shard, send(shard, BESIDE), send(shard, ACROSS), send(shard, DIAGONAL)])
    shard = shard.reshape(2, 2, 3, 16, 512)
    above = send(cells[:, :, 7], row_step(1))
    below = send(cells[:, :, 0], row_step(-1))

    shard, cells = lax.optimization_barrier((shard, cells))
    near = [shard] + [send(shard, around_by_core(2, -by)) for by in (1, 2, 3)]
    wide = jnp.pad(cells, ((0, 0),) * 3 + ((0, 2), (0, 0)))
    own = lax.dynamic_slice_in_dim(wide, 3 * xhi, 5, 1).reshape(2560, 128)
    across = send(lax.dynamic_slice_in_dim(wide, 3 * (1 - xhi), 5, 1).reshape(2560, 128), ACROSS)
    own_there = send(own, CORES)

    def edge(column):
        return jnp.concatenate([above[:, :, None, column], cells[:, :, :, column], below[:, :, None, column]], axis=2)

    shard, first, last = lax.optimization_barrier((jnp.stack(near), edge(0), edge(29)))
    weights = [shard] + [send(shard, around_by_core(1, -by)) for by in (1, 2, 3)]
    left = send(last, column_step(1))
    right = send(first, column_step(-1))

    def rim(start):
        a, b, l, r = (lax.dynamic_slice_in_dim(v, start, 5, 1) for v in (above, below, left, right))
        return jnp.concatenate(
            [a, r[:, :, :1], l[:, :, :1], b, r[:, :, 9:], l[:, :, 9:], r[:, :, 1:9], l[:, :, 1:9]],
            axis=2).reshape(800, 128)

    taps = depth_kernel.reshape(3, 9, 2, 4, 128)
    taps = jnp.where(xhi == 1, taps[::-1], taps)
    own_rim = rim(3 * xhi)
    across_rim = send(jnp.concatenate([rim(3 * (1 - xhi)), taps.reshape(216, 128).astype(BF16)]), ACROSS)
    across, across_rim, weights[1] = lax.optimization_barrier((across, across_rim, weights[1]))
    core_rim = send(jnp.concatenate([own_rim, across_rim[:800]]), CORES)
    pieces = [own, own_there, across, send(across, CORES), own_rim, across_rim, core_rim]
    taps = jnp.concatenate([taps, across_rim[800:].astype(F32).reshape(3, 9, 2, 4, 128)[::-1]], axis=3)
    by_frame = [sum(row[i] * taps[i] for i in range(3) if row[i]) for row in TAPS]
    by_frame = jnp.stack(by_frame).reshape(6, 3, 3, 2, 8, 128)
    by_row = [sum(row[j] * by_frame[:, j] for j in range(3) if row[j]) for row in ROW_TAPS]
    taps = jnp.stack(by_row, axis=1).reshape(6, 12, 2, 8, 128)
    taps = taps * jnp.array([1.0, 0.5], F32)[None, None, :, None, None]

    packed = pack_cells(position, pieces)
    kept, sent = run_block(position, packed, weights, taps)
    total = kept + send(sent, CORES).astype(F32)
    return total[:, :, None, :, :30].astype(BF16)


def solution(mesh):
    return jax.shard_map(
        on_device,
        mesh=mesh,
        in_specs=(
            P(None, None, "tile", None, None, "ch"),
            P("tile", None, "ch"),
            P(None, None, None, None, "ch"),
            P("ch", "tile"),
        ),
        out_specs=P(None, "ch", "tile", None, None, None),
        check_vma=False,
    )
```

time: 116 us -> 108 us (0.931)
  waiting for transfers between devices: 20.1 us -> 12.6 us
  Pallas kernels: 42 us -> 38.5 us
  starting transfers between devices: 35 us -> 36.3 us
    ppermute x17 -> x19, waiting for transfers between devices: 20.1 us -> 12.6 us  [send(): return lax.ppermute(value, BOTH, pairs)]
    concatenate x0 -> x2, local copies, waits for them, and re-layouts: none -> 3.18 us  [rim(): jnp.concatenate([a, r[:, :, :1], l[:, :, :1], b, r[:, :, 9:], l[:, :, 9:]...]
    pallas_call x1, Pallas kernels: 39.8 us -> 36.8 us  [run_block(): pl.pallas_call(block_kernel, out_shape=[jax.ShapeDtypeStruct((2, 2, 8, 32...]
    dynamic_slice x3 -> x5, local copies, waits for them, and re-layouts: 3.3 us -> 1.22 us  [the longest x2 1.05 us: on_device(): lax.dynamic_slice_in_dim(wide, 3 * (1 - xhi), 5, 1).reshape(2560, 128)]
    convert_element_type x0 -> x1, other arithmetic: none -> 1.95 us  [on_device(): return total[:, :, None, :, :30].astype(BF16)]
    broadcast_in_dim x3 -> x0, local copies, waits for them, and re-layouts: 1.87 us -> none  [the longest x1 1.49 us: on_device(): return finish(kept, send(sent, CORES))[:, :, None]]
    unnamed x14 -> x15, local copies, waits for them, and re-layouts: 3.33 us -> 1.76 us
    slice x3 -> x7, local copies, waits for them, and re-layouts: 3.48 us -> 5.04 us  [the longest x1 1.91 us: on_device(): below = send(cells[:, :, 0], row_step(-1))]
  transfers between devices with their start and end apart: 17 -> 19, of which waited for: 5 -> 8; matrix products, arithmetic and copies ran while one was open for 10% -> 12% of each run, Pallas kernels for 1% -> 2%
where the time goes in v3:
time: 108 us
  Pallas kernels  38.5 us (36%)
  starting transfers between devices  36.3 us (34%)
  local copies, waits for them, and re-layouts  14.4 us (13%)
  waiting for transfers between devices  12.6 us (12%)
  other arithmetic  5.63 us (5%)
    pallas_call x1, Pallas kernels, run_block(): pl.pallas_call(block_kernel, out_shape=[jax.ShapeDtypeStruct((2, 2, 8, 32...  36.8 us
    ppermute x19, starting transfers between devices, send(): return lax.ppermute(value, BOTH, pairs)  36.3 us
    ppermute x19, waiting for transfers between devices, send(): return lax.ppermute(value, BOTH, pairs)  12.6 us
    concatenate x2, local copies, waits for them, and re-layouts, rim(): jnp.concatenate([a, r[:, :, :1], l[:, :, :1], b, r[:, :, 9:], l[:, :, 9:]...  3.18 us
  transfers between devices with their start and end apart: 19, of which 8 were waited for; matrix products, arithmetic and copies ran while one was open for 12% of the time, Pallas kernels for 2%

profile of v3, /device:TPU:1, one launch (start us, length us, event | category | flops | bytes accessed | tf_op | source)
XLA Modules:
  0.0 107.8 jit_solution(12688532764264568945)
XLA Ops:
  0.0 0.9 copy_multiply_fusion
  0.9 0.7 fusion.4
  1.6 2.1 %collective-permute-start = (bf16[3,16,512]{2,1,0:T(8,128)(2,1)S(1)}, bf16[3,16,512]{2,1,0:T(8,128)(2,1)S(1)}, u32[]{:S(2)}, u32[]{:S(2)}) collective-permute-start(bf16[3,16,512]{2,1,0:T(8,128)(2,1)S(1)} %get-tuple-element.64), channel_id=1, source_target_pairs={{0,4},{1,5},{2,6},{3,7},{4,0},{5,1},{6,2},{7,3},{8,12},{9,13},{10,... | collective-permute-start | bytes 147464 | tf_op jit(solution)/shard_map/ppermute | solution.py:69
  3.7 2.5 %collective-permute-start.1 = (bf16[3,16,512]{2,1,0:T(8,128)(2,1)S(1)}, bf16[3,16,512]{2,1,0:T(8,128)(2,1)S(1)}, u32[]{:S(2)}, u32[]{:S(2)}) collective-permute-start(bf16[3,16,512]{2,1,0:T(8,128)(2,1)S(1)} %get-tuple-element.64), channel_id=1, source_target_pairs={{0,64},{1,65},{2,66},{3,67},{4,68},{5,69},{6,70},{7,71},{8,72},{9,... | collective-permute-start | bytes 147464 | tf_op jit(solution)/shard_map/ppermute | solution.py:69
  6.2 0.0 collective-permute-start.2
  6.2 1.9 %fusion.8 = (bf16[2,8,1,30,128]{4,2,3,1,0:T(2,128)(2,1)S(1)}, bf16[2,8,1,30,128]{4,2,3,1,0:T(2,128)(2,1)S(1)}) fusion(bf16[2,8,8,30,128]{4,2,3,1,0:T(8,128)(2,1)} %bitcast.53), kind=kLoop, calls=%fused_computation.60 | loop fusion | bytes 491520 | tf_op jit(solution)/shard_map/slice | solution.py:294
  8.2 2.1 %collective-permute-start.5 = (bf16[2,8,30,128]{3,2,1,0:T(8,128)(2,1)S(1)}, bf16[2,8,30,128]{3,2,1,0:T(8,128)(2,1)S(1)}, u32[]{:S(2)}, u32[]{:S(2)}) collective-permute-start(bf16[2,8,30,128]{3,2,1,0:T(8,128)(2,1)S(1)} %bitcast.75), channel_id=1, source_target_pairs={{0,4},{1,5},{2,6},{3,7},{4,8},{5,9},{6,10},{7,11},{8,12},{9,13},{1... | collective-permute-start | bytes 368648 | tf_op jit(solution)/shard_map/ppermute | solution.py:69
  10.3 1.3 %collective-permute-start.9 = (bf16[2,8,30,128]{3,2,1,0:T(8,128)(2,1)S(1)}, bf16[2,8,30,128]{3,2,1,0:T(8,128)(2,1)S(1)}, u32[]{:S(2)}, u32[]{:S(2)}) collective-permute-start(bf16[2,8,30,128]{3,2,1,0:T(8,128)(2,1)S(1)} %bitcast.74), channel_id=1, source_target_pairs={{4,0},{5,1},{6,2},{7,3},{8,4},{9,5},{10,6},{11,7},{12,8},{13,9},{1... | collective-permute-start | bytes 368648 | tf_op jit(solution)/shard_map/ppermute | solution.py:69
  11.6 0.1 reshape.42
  11.8 0.0 collective-permute-done
  11.8 0.0 collective-permute-done.1
  11.8 0.0 collective-permute-done.2
  11.8 5.8 %collective-permute-start.6 = (bf16[2,2,3,16,512]{4,3,2,1,0:T(8,128)(2,1)S(1)}, bf16[2,2,3,16,512]{4,3,2,1,0:T(8,128)(2,1)S(1)}, u32[]{:S(2)}, u32[]{:S(2)}) collective-permute-start(bf16[2,2,3,16,512]{4,3,2,1,0:T(8,128)(2,1)S(1)} %bitcast.59), channel_id=1, source_target_pairs={{0,3},{1,0},{2,1},{3,2},{4,7},{5,4},{6,5},{7,6},{8,11},{9,8},{10,9... | collective-permute-start | bytes 589832 | tf_op jit(solution)/shard_map/ppermute | solution.py:69
  17.6 0.3 collective-permute-start.7
  18.0 0.7 collective-permute-start.8
  18.7 0.1 pad_dynamic-slice_fusion
  18.8 1.0 copy.8
  19.7 0.0 collective-permute-done.5
  19.7 1.5 %collective-permute-start.4 = (bf16[2560,128]{1,0:T(8,128)(2,1)}, bf16[2560,128]{1,0:T(8,128)(2,1)S(1)}, u32[]{:S(2)}, u32[]{:S(2)}) collective-permute-start(bf16[2560,128]{1,0:T(8,128)(2,1)} %bitcast.16), channel_id=1, source_target_pairs={{0,64},{1,65},{2,66},{3,67},{4,68},{5,69},{6,70},{7,71},{8,72},{9,... | collective-permute-start | bytes 1966088 | tf_op jit(solution)/shard_map/ppermute | solution.py:69
  21.3 0.0 collective-permute-done.9
  21.3 0.1 pad_maximum_fusion.6
  21.4 0.9 collective-permute-done.6
  22.3 1.6 %collective-permute-done.7 = bf16[2,2,3,16,512]{4,3,2,1,0:T(8,128)(2,1)S(1)} collective-permute-done((bf16[2,2,3,16,512]{4,3,2,1,0:T(8,128)(2,1)S(1)}, bf16[2,2,3,16,512]{4,3,2,1,0:T(8,128)(2,1)S(1)}, u32[]{:S(2)}, u32[]{:S(2)}) %collective-permute-start.7) | collective-permute-done | bytes 196640 | tf_op jit(solution)/shard_map/ppermute | solution.py:69
  24.0 2.1 %collective-permute-done.8 = bf16[2,2,3,16,512]{4,3,2,1,0:T(8,128)(2,1)S(1)} collective-permute-done((bf16[2,2,3,16,512]{4,3,2,1,0:T(8,128)(2,1)S(1)}, bf16[2,2,3,16,512]{4,3,2,1,0:T(8,128)(2,1)S(1)}, u32[]{:S(2)}, u32[]{:S(2)}) %collective-permute-start.8) | collective-permute-done | bytes 196640 | tf_op jit(solution)/shard_map/ppermute | solution.py:69
  26.0 0.1 pad_maximum_fusion.p0
  26.1 3.5 %collective-permute-start.11 = (bf16[2,8,10,128]{3,2,1,0:T(8,128)(2,1)S(1)}, bf16[2,8,10,128]{3,2,1,0:T(8,128)(2,1)S(1)}, u32[]{:S(2)}, u32[]{:S(2)}) collective-permute-start(bf16[2,8,10,128]{3,2,1,0:T(8,128)(2,1)S(1)} %get-tuple-element.18), channel_id=1, source_target_pairs={{0,1},{1,2},{2,3},{4,5},{5,6},{6,7},{8,9},{9,10},{10,11},{12,13},{... | collective-permute-start | bytes 122888 | tf_op jit(solution)/shard_map/ppermute | solution.py:69
  29.7 1.3 %collective-permute-start.10 = (bf16[2,8,10,128]{3,2,1,0:T(8,128)(2,1)S(1)}, bf16[2,8,10,128]{3,2,1,0:T(8,128)(2,1)S(1)}, u32[]{:S(2)}, u32[]{:S(2)}) collective-permute-start(bf16[2,8,10,128]{3,2,1,0:T(8,128)(2,1)S(1)} %get-tuple-element.17), channel_id=1, source_target_pairs={{1,0},{2,1},{3,2},{5,4},{6,5},{7,6},{9,8},{10,9},{11,10},{13,12},{... | collective-permute-start | bytes 122888 | tf_op jit(solution)/shard_map/ppermute | solution.py:69
  31.0 4.3 %collective-permute-start.13 = (bf16[4,2,2,3,16,512]{5,4,3,2,1,0:T(8,128)(2,1)S(1)}, bf16[4,2,2,3,16,512]{5,4,3,2,1,0:T(8,128)(2,1)}, u32[]{:S(2)}, u32[]{:S(2)}) collective-permute-start(bf16[4,2,2,3,16,512]{5,4,3,2,1,0:T(8,128)(2,1)S(1)} %pad_maximum_fusion.p0), channel_id=1, source_target_pairs={{0,24},{1,25},{2,26},{3,27},{4,28},{5,29},{6,30},{7,31},{8,0},{9,1... | collective-permute-start | bytes 2359304 | tf_op jit(solution)/shard_map/ppermute | solution.py:69
  35.3 0.0 collective-permute-done.11
  35.3 0.6 constant_dynamic-slice_fusion.4
  35.9 0.0 collective-permute-done.10
  35.9 0.6 constant_dynamic-slice_fusion.2
  36.5 0.6 constant_dynamic-slice_fusion.9
  37.2 0.6 constant_dynamic-slice_fusion.10
  37.8 0.2 concatenate.24
  38.0 0.7 pad_maximum_fusion.3
  38.7 1.4 %collective-permute-start.12 = (bf16[1016,128]{1,0:T(8,128)(2,1)}, bf16[1016,128]{1,0:T(8,128)(2,1)S(1)}, u32[]{:S(2)}, u32[]{:S(2)}) collective-permute-start(bf16[1016,128]{1,0:T(8,128)(2,1)} %pad_maximum_fusion.3), channel_id=1, source_target_pairs={{0,64},{1,65},{2,66},{3,67},{4,68},{5,69},{6,70},{7,71},{8,72},{9,... | collective-permute-start | bytes 780296 | tf_op jit(solution)/shard_map/ppermute | solution.py:69
  40.1 0.1 stack.84.pos_ref
  40.2 0.1 copy.7
  40.3 1.7 %collective-permute-start.3 = (bf16[2560,128]{1,0:T(8,128)(2,1)S(1)}, bf16[2560,128]{1,0:T(8,128)(2,1)S(1)}, u32[]{:S(2)}, u32[]{:S(2)}) collective-permute-start(bf16[2560,128]{1,0:T(8,128)(2,1)S(1)} %bitcast.49), channel_id=1, source_target_pairs={{0,32},{1,33},{2,34},{3,35},{4,36},{5,37},{6,38},{7,39},{8,40},{9,... | collective-permute-start | bytes 1966088 | tf_op jit(solution)/shard_map/ppermute | solution.py:69
  42.0 2.6 %collective-permute-start.16 = (bf16[4,2,2,3,16,512]{5,4,3,2,1,0:T(8,128)(2,1)S(1)}, bf16[4,2,2,3,16,512]{5,4,3,2,1,0:T(8,128)(2,1)}, u32[]{:S(2)}, u32[]{:S(2)}) collective-permute-start(bf16[4,2,2,3,16,512]{5,4,3,2,1,0:T(8,128)(2,1)S(1)} %pad_maximum_fusion.p0), channel_id=1, source_target_pairs={{0,16},{1,17},{2,18},{3,19},{4,20},{5,21},{6,22},{7,23},{8,24},{9,... | collective-permute-start | bytes 2359304 | tf_op jit(solution)/shard_map/ppermute | solution.py:69
  44.6 3.0 %concatenate.26 = bf16[2,5,80,128]{3,2,1,0:T(8,128)(2,1)S(1)} concatenate(bf16[2,5,30,128]{3,2,1,0:T(8,128)(2,1)S(1)} %get-tuple-element.44, bf16[2,5,1,128]{3,2,1,0:T(2,128)(2,1)} %get-tuple-element.60, bf16[2,5,1,128]{3,2,1,0:T(2,128)(2,1)} %get-tuple-element.56, bf16[2,5,30,128]{3,2,1,0:T(8,128)(2,1)S(1)} %get-tuple-element.42, bf16[2,5,1,128]{3,2,1,0:T(2,128)(2,1)} %get-tuple-element.59, ...), dimensions={2} | concatenate | bytes 409600 | tf_op jit(solution)/shard_map/concatenate | solution.py:313
  47.6 0.2 collective-permute-done.12.across_rim
  47.8 1.0 collective-permute-start.17
  48.8 0.0 collective-permute-done.4.m2
  48.8 0.0 collective-permute-done.13.p1
  48.8 0.6 slice.133
  49.5 1.5 %rev.7 = f32[3,9,2,4,128]{4,3,2,1,0:T(4,128)} reverse(bf16[3,9,2,4,128]{4,3,2,1,0:T(4,128)(2,1)} %bitcast.69), dimensions={0} | reverse | bytes 165888 | tf_op jit(solution)/shard_map/rev | solution.py:324
  50.9 0.9 add_add_fusion.2
  51.9 0.0 copy-start.3
  51.9 2.0 %collective-permute-start.15 = (bf16[1600,128]{1,0:T(8,128)(2,1)S(1)}, bf16[1600,128]{1,0:T(8,128)(2,1)S(1)}, u32[]{:S(2)}, u32[]{:S(2)}) collective-permute-start(bf16[1600,128]{1,0:T(8,128)(2,1)S(1)} %pad_maximum_fusion.2), channel_id=1, source_target_pairs={{0,32},{1,33},{2,34},{3,35},{4,36},{5,37},{6,38},{7,39},{8,40},{9,... | collective-permute-start | bytes 1228808 | tf_op jit(solution)/shard_map/ppermute | solution.py:69
  53.9 0.3 collective-permute-start.14
  54.4 0.1 broadcast_multiply_fusion.k_ref
  54.5 0.0 collective-permute-done.3.m1
  54.5 0.8 collective-permute-done.15.core_rim
  55.3 0.9 collective-permute-done.14.m3
  56.2 1.7 %pack_cells.1.x_ref = bf16[4,2,1600,128]{3,2,1,0:T(8,128)(2,1)S(1)} custom-call(s32[5]{0:T(128)S(1)} %stack.84.pos_ref, bf16[2560,128]{1,0:T(8,128)(2,1)S(1)} %bitcast.50, bf16[2560,128]{1,0:T(8,128)(2,1)S(1)} %collective-permute-done.3.m1, bf16[2560,128]{1,0:T(8,128)(2,1)S(1)} %collective-permute-done.4.m2, ...), custom_call_target="tpu_custom_call" | custom-call | tf_op jit(solution)/shard_map/pack_cells/pallas_call | solution.py:134
  57.9 1.7 %copy-done = bf16[4,2,1600,128]{3,2,1,0:T(8,128)(2,1)} copy-done((bf16[4,2,1600,128]{3,2,1,0:T(8,128)(2,1)}, bf16[4,2,1600,128]{3,2,1,0:T(8,128)(2,1)S(1)}, u32[]{:S(2)}) %copy-start) | copy-done | bytes 3276824
  59.6 3.6 %collective-permute-done.17.p3 = bf16[4,2,2,3,16,512]{5,4,3,2,1,0:T(8,128)(2,1)} collective-permute-done((bf16[4,2,2,3,16,512]{5,4,3,2,1,0:T(8,128)(2,1)S(1)}, bf16[4,2,2,3,16,512]{5,4,3,2,1,0:T(8,128)(2,1)}, u32[]{:S(2)}, u32[]{:S(2)}) %collective-permute-start.17) | collective-permute-done | bytes 786464 | tf_op jit(solution)/shard_map/ppermute | solution.py:69
  63.2 36.8 %gated_block.1 = (f32[2,2,8,32,512]{4,3,2,1,0:T(8,128)}, bf16[2,2,8,32,512]{4,3,2,1,0:T(8,128)(2,1)}) custom-call(s32[5]{0:T(128)S(1)} %stack.84.pos_ref, bf16[4,2,1600,128]{3,2,1,0:T(8,128)(2,1)} %copy-done, bf16[4,2,2,3,16,512]{5,4,3,2,1,0:T(8,128)(2,1)S(1)} %pad_maximum_fusion.p0, bf16[4,2,2,3,16,512]{5,4,3,2,1,0:T(8,128)(2,1)} %collective-permute-done.13.p1, ...), custom_call_target="tpu_custom_call" | custom-call | tf_op jit(solution)/shard_map/gated_block/pallas_call | solution.py:263
  100.0 1.8 %collective-permute-start.18 = (bf16[2,2,8,32,512]{4,3,2,1,0:T(8,128)(2,1)}, bf16[2,2,8,32,512]{4,3,2,1,0:T(8,128)(2,1)S(1)}, u32[]{:S(2)}, u32[]{:S(2)}) collective-permute-start(bf16[2,2,8,32,512]{4,3,2,1,0:T(8,128)(2,1)} %get-tuple-element.24), channel_id=1, source_target_pairs={{0,32},{1,33},{2,34},{3,35},{4,36},{5,37},{6,38},{7,39},{8,40},{9,... | collective-permute-start | bytes 3145736 | tf_op jit(solution)/shard_map/ppermute | solution.py:69
  101.8 2.5 %collective-permute-done.18 = bf16[2,2,8,32,512]{4,3,2,1,0:T(8,128)(2,1)S(1)} collective-permute-done((bf16[2,2,8,32,512]{4,3,2,1,0:T(8,128)(2,1)}, bf16[2,2,8,32,512]{4,3,2,1,0:T(8,128)(2,1)S(1)}, u32[]{:S(2)}, u32[]{:S(2)}) %collective-permute-start.18) | collective-permute-done | bytes 1048608 | tf_op jit(solution)/shard_map/ppermute | solution.py:69
  104.3 2.0 %fusion.1 = bf16[2,2,1,8,30,512]{5,4,3,1,0,2:T(8,128)(2,1)S(1)} fusion(f32[2,2,8,32,512]{4,3,2,1,0:T(8,128)} %get-tuple-element.23, bf16[2,2,8,32,512]{4,3,2,1,0:T(8,128)(2,1)S(1)} %collective-permute-done.18), kind=kLoop, calls=%fused_computation.2 | loop fusion | flops 1474560 | bytes 3932160 | tf_op jit(solution)/shard_map/convert_element_type | solution.py:334
  106.3 1.5 %copy.12 = bf16[2,2,1,8,30,512]{5,3,4,2,1,0:T(8,128)(2,1)} copy(bf16[2,2,1,8,30,512]{5,4,3,1,0,2:T(8,128)(2,1)S(1)} %fusion.1) | data formatting | bytes 1966080 | tf_op jit(solution)/shard_map/convert_element_type | solution.py:334
  (29 shorter events, 0.4 us)
Async XLA Ops:
  0.0 18.7 %copy-start.1 = (bf16[2,8,1,8,30,128]{5,3,4,2,1,0:T(8,128)(2,1)S(1)}, bf16[2,8,1,8,30,128]{5,3,4,2,1,0:T(8,128)(2,1)}, u32[]{:S(2)}) copy-start(bf16[2,8,1,8,30,128]{5,3,4,2,1,0:T(8,128)(2,1)} %param.5) | copy-start | bytes 2949124
  0.0 11.6 %copy-start.2 = (f32[3,3,3,2,512]{4,3,2,1,0:T(2,128)S(1)}, f32[3,3,3,2,512]{4,3,2,1,0:T(2,128)}, u32[]{:S(2)}) copy-start(f32[3,3,3,2,512]{4,3,2,1,0:T(2,128)} %param.7) | copy-start | bytes 331780
  1.6 10.2 %collective-permute-start = (bf16[3,16,512]{2,1,0:T(8,128)(2,1)S(1)}, bf16[3,16,512]{2,1,0:T(8,128)(2,1)S(1)}, u32[]{:S(2)}, u32[]{:S(2)}) collective-permute-start(bf16[3,16,512]{2,1,0:T(8,128)(2,1)S(1)} %get-tuple-element.64), channel_id=1, source_target_pairs={{0,4},{1,5},{2,6},{3,7},{4,0},{5,1},{6,2},{7,3},{8,12},{9,13},{10,... | collective-permute-start | bytes 147464 | tf_op jit(solution)/shard_map/ppermute | solution.py:69
  3.7 8.1 %collective-permute-start.1 = (bf16[3,16,512]{2,1,0:T(8,128)(2,1)S(1)}, bf16[3,16,512]{2,1,0:T(8,128)(2,1)S(1)}, u32[]{:S(2)}, u32[]{:S(2)}) collective-permute-start(bf16[3,16,512]{2,1,0:T(8,128)(2,1)S(1)} %get-tuple-element.64), channel_id=1, source_target_pairs={{0,64},{1,65},{2,66},{3,67},{4,68},{5,69},{6,70},{7,71},{8,72},{9,... | collective-permute-start | bytes 147464 | tf_op jit(solution)/shard_map/ppermute | solution.py:69
  6.2 5.6 %collective-permute-start.2 = (bf16[3,16,512]{2,1,0:T(8,128)(2,1)S(1)}, bf16[3,16,512]{2,1,0:T(8,128)(2,1)S(1)}, u32[]{:S(2)}, u32[]{:S(2)}) collective-permute-start(bf16[3,16,512]{2,1,0:T(8,128)(2,1)S(1)} %get-tuple-element.64), channel_id=1, source_target_pairs={{0,68},{1,69},{2,70},{3,71},{4,64},{5,65},{6,66},{7,67},{8,76},{9,... | collective-permute-start | bytes 147464 | tf_op jit(solution)/shard_map/ppermute | solution.py:69
  8.2 11.6 %collective-permute-start.5 = (bf16[2,8,30,128]{3,2,1,0:T(8,128)(2,1)S(1)}, bf16[2,8,30,128]{3,2,1,0:T(8,128)(2,1)S(1)}, u32[]{:S(2)}, u32[]{:S(2)}) collective-permute-start(bf16[2,8,30,128]{3,2,1,0:T(8,128)(2,1)S(1)} %bitcast.75), channel_id=1, source_target_pairs={{0,4},{1,5},{2,6},{3,7},{4,8},{5,9},{6,10},{7,11},{8,12},{9,13},{1... | collective-permute-start | bytes 368648 | tf_op jit(solution)/shard_map/ppermute | solution.py:69
  10.3 11.0 %collective-permute-start.9 = (bf16[2,8,30,128]{3,2,1,0:T(8,128)(2,1)S(1)}, bf16[2,8,30,128]{3,2,1,0:T(8,128)(2,1)S(1)}, u32[]{:S(2)}, u32[]{:S(2)}) collective-permute-start(bf16[2,8,30,128]{3,2,1,0:T(8,128)(2,1)S(1)} %bitcast.74), channel_id=1, source_target_pairs={{4,0},{5,1},{6,2},{7,3},{8,4},{9,5},{10,6},{11,7},{12,8},{13,9},{1... | collective-permute-start | bytes 368648 | tf_op jit(solution)/shard_map/ppermute | solution.py:69
  11.8 10.5 %collective-permute-start.6 = (bf16[2,2,3,16,512]{4,3,2,1,0:T(8,128)(2,1)S(1)}, bf16[2,2,3,16,512]{4,3,2,1,0:T(8,128)(2,1)S(1)}, u32[]{:S(2)}, u32[]{:S(2)}) collective-permute-start(bf16[2,2,3,16,512]{4,3,2,1,0:T(8,128)(2,1)S(1)} %bitcast.59), channel_id=1, source_target_pairs={{0,3},{1,0},{2,1},{3,2},{4,7},{5,4},{6,5},{7,6},{8,11},{9,8},{10,9... | collective-permute-start | bytes 589832 | tf_op jit(solution)/shard_map/ppermute | solution.py:69
  17.6 6.4 %collective-permute-start.7 = (bf16[2,2,3,16,512]{4,3,2,1,0:T(8,128)(2,1)S(1)}, bf16[2,2,3,16,512]{4,3,2,1,0:T(8,128)(2,1)S(1)}, u32[]{:S(2)}, u32[]{:S(2)}) collective-permute-start(bf16[2,2,3,16,512]{4,3,2,1,0:T(8,128)(2,1)S(1)} %bitcast.60), channel_id=1, source_target_pairs={{0,2},{1,3},{2,0},{3,1},{4,6},{5,7},{6,4},{7,5},{8,10},{9,11},{10,... | collective-permute-start | bytes 589832 | tf_op jit(solution)/shard_map/ppermute | solution.py:69
  18.0 8.1 %collective-permute-start.8 = (bf16[2,2,3,16,512]{4,3,2,1,0:T(8,128)(2,1)S(1)}, bf16[2,2,3,16,512]{4,3,2,1,0:T(8,128)(2,1)S(1)}, u32[]{:S(2)}, u32[]{:S(2)}) collective-permute-start(bf16[2,2,3,16,512]{4,3,2,1,0:T(8,128)(2,1)S(1)} %bitcast.61), channel_id=1, source_target_pairs={{0,1},{1,2},{2,3},{3,0},{4,5},{5,6},{6,7},{7,4},{8,9},{9,10},{10,1... | collective-permute-start | bytes 589832 | tf_op jit(solution)/shard_map/ppermute | solution.py:69
  19.7 29.1 %collective-permute-start.4 = (bf16[2560,128]{1,0:T(8,128)(2,1)}, bf16[2560,128]{1,0:T(8,128)(2,1)S(1)}, u32[]{:S(2)}, u32[]{:S(2)}) collective-permute-start(bf16[2560,128]{1,0:T(8,128)(2,1)} %bitcast.16), channel_id=1, source_target_pairs={{0,64},{1,65},{2,66},{3,67},{4,68},{5,69},{6,70},{7,71},{8,72},{9,... | collective-permute-start | bytes 1966088 | tf_op jit(solution)/shard_map/ppermute | solution.py:69
  26.1 9.2 %collective-permute-start.11 = (bf16[2,8,10,128]{3,2,1,0:T(8,128)(2,1)S(1)}, bf16[2,8,10,128]{3,2,1,0:T(8,128)(2,1)S(1)}, u32[]{:S(2)}, u32[]{:S(2)}) collective-permute-start(bf16[2,8,10,128]{3,2,1,0:T(8,128)(2,1)S(1)} %get-tuple-element.18), channel_id=1, source_target_pairs={{0,1},{1,2},{2,3},{4,5},{5,6},{6,7},{8,9},{9,10},{10,11},{12,13},{... | collective-permute-start | bytes 122888 | tf_op jit(solution)/shard_map/ppermute | solution.py:69
  29.7 6.2 %collective-permute-start.10 = (bf16[2,8,10,128]{3,2,1,0:T(8,128)(2,1)S(1)}, bf16[2,8,10,128]{3,2,1,0:T(8,128)(2,1)S(1)}, u32[]{:S(2)}, u32[]{:S(2)}) collective-permute-start(bf16[2,8,10,128]{3,2,1,0:T(8,128)(2,1)S(1)} %get-tuple-element.17), channel_id=1, source_target_pairs={{1,0},{2,1},{3,2},{5,4},{6,5},{7,6},{9,8},{10,9},{11,10},{13,12},{... | collective-permute-start | bytes 122888 | tf_op jit(solution)/shard_map/ppermute | solution.py:69
  31.0 17.8 %collective-permute-start.13 = (bf16[4,2,2,3,16,512]{5,4,3,2,1,0:T(8,128)(2,1)S(1)}, bf16[4,2,2,3,16,512]{5,4,3,2,1,0:T(8,128)(2,1)}, u32[]{:S(2)}, u32[]{:S(2)}) collective-permute-start(bf16[4,2,2,3,16,512]{5,4,3,2,1,0:T(8,128)(2,1)S(1)} %pad_maximum_fusion.p0), channel_id=1, source_target_pairs={{0,24},{1,25},{2,26},{3,27},{4,28},{5,29},{6,30},{7,31},{8,0},{9,1... | collective-permute-start | bytes 2359304 | tf_op jit(solution)/shard_map/ppermute | solution.py:69
  38.7 9.1 %collective-permute-start.12 = (bf16[1016,128]{1,0:T(8,128)(2,1)}, bf16[1016,128]{1,0:T(8,128)(2,1)S(1)}, u32[]{:S(2)}, u32[]{:S(2)}) collective-permute-start(bf16[1016,128]{1,0:T(8,128)(2,1)} %pad_maximum_fusion.3), channel_id=1, source_target_pairs={{0,64},{1,65},{2,66},{3,67},{4,68},{5,69},{6,70},{7,71},{8,72},{9,... | collective-permute-start | bytes 780296 | tf_op jit(solution)/shard_map/ppermute | solution.py:69
  40.3 14.2 %collective-permute-start.3 = (bf16[2560,128]{1,0:T(8,128)(2,1)S(1)}, bf16[2560,128]{1,0:T(8,128)(2,1)S(1)}, u32[]{:S(2)}, u32[]{:S(2)}) collective-permute-start(bf16[2560,128]{1,0:T(8,128)(2,1)S(1)} %bitcast.49), channel_id=1, source_target_pairs={{0,32},{1,33},{2,34},{3,35},{4,36},{5,37},{6,38},{7,39},{8,40},{9,... | collective-permute-start | bytes 1966088 | tf_op jit(solution)/shard_map/ppermute | solution.py:69
  42.0 17.6 %collective-permute-start.16 = (bf16[4,2,2,3,16,512]{5,4,3,2,1,0:T(8,128)(2,1)S(1)}, bf16[4,2,2,3,16,512]{5,4,3,2,1,0:T(8,128)(2,1)}, u32[]{:S(2)}, u32[]{:S(2)}) collective-permute-start(bf16[4,2,2,3,16,512]{5,4,3,2,1,0:T(8,128)(2,1)S(1)} %pad_maximum_fusion.p0), channel_id=1, source_target_pairs={{0,16},{1,17},{2,18},{3,19},{4,20},{5,21},{6,22},{7,23},{8,24},{9,... | collective-permute-start | bytes 2359304 | tf_op jit(solution)/shard_map/ppermute | solution.py:69
  47.8 15.4 %collective-permute-start.17 = (bf16[4,2,2,3,16,512]{5,4,3,2,1,0:T(8,128)(2,1)S(1)}, bf16[4,2,2,3,16,512]{5,4,3,2,1,0:T(8,128)(2,1)}, u32[]{:S(2)}, u32[]{:S(2)}) collective-permute-start(bf16[4,2,2,3,16,512]{5,4,3,2,1,0:T(8,128)(2,1)S(1)} %pad_maximum_fusion.p0), channel_id=1, source_target_pairs={{0,8},{1,9},{2,10},{3,11},{4,12},{5,13},{6,14},{7,15},{8,16},{9,17... | collective-permute-start | bytes 2359304 | tf_op jit(solution)/shard_map/ppermute | solution.py:69
  51.9 2.5 %copy-start.3 = (f32[2]{0:T(128)S(1)}, f32[2]{0:T(128)}, u32[]{:S(2)}) copy-start(f32[2]{0:T(128)} %constant.91.clone) | copy-start | bytes 28
  51.9 3.4 %collective-permute-start.15 = (bf16[1600,128]{1,0:T(8,128)(2,1)S(1)}, bf16[1600,128]{1,0:T(8,128)(2,1)S(1)}, u32[]{:S(2)}, u32[]{:S(2)}) collective-permute-start(bf16[1600,128]{1,0:T(8,128)(2,1)S(1)} %pad_maximum_fusion.2), channel_id=1, source_target_pairs={{0,32},{1,33},{2,34},{3,35},{4,36},{5,37},{6,38},{7,39},{8,40},{9,... | collective-permute-start | bytes 1228808 | tf_op jit(solution)/shard_map/ppermute | solution.py:69
  53.9 2.3 %collective-permute-start.14 = (bf16[2560,128]{1,0:T(8,128)(2,1)S(1)}, bf16[2560,128]{1,0:T(8,128)(2,1)S(1)}, u32[]{:S(2)}, u32[]{:S(2)}) collective-permute-start(bf16[2560,128]{1,0:T(8,128)(2,1)S(1)} %collective-permute-done.4.m2), channel_id=1, source_target_pairs={{0,32},{1,33},{2,34},{3,35},{4,36},{5,37},{6,38},{7,39},{8,40},{9,... | collective-permute-start | bytes 1966088 | tf_op jit(solution)/shard_map/ppermute | solution.py:69
  57.9 1.7 %copy-start = (bf16[4,2,1600,128]{3,2,1,0:T(8,128)(2,1)}, bf16[4,2,1600,128]{3,2,1,0:T(8,128)(2,1)S(1)}, u32[]{:S(2)}) copy-start(bf16[4,2,1600,128]{3,2,1,0:T(8,128)(2,1)S(1)} %pack_cells.1.x_ref) | copy-start | bytes 9830404
  100.0 4.3 %collective-permute-start.18 = (bf16[2,2,8,32,512]{4,3,2,1,0:T(8,128)(2,1)}, bf16[2,2,8,32,512]{4,3,2,1,0:T(8,128)(2,1)S(1)}, u32[]{:S(2)}, u32[]{:S(2)}) collective-permute-start(bf16[2,2,8,32,512]{4,3,2,1,0:T(8,128)(2,1)} %get-tuple-element.24), channel_id=1, source_target_pairs={{0,32},{1,33},{2,34},{3,35},{4,36},{5,37},{6,38},{7,39},{8,40},{9,... | collective-permute-start | bytes 3145736 | tf_op jit(solution)/shard_map/ppermute | solution.py:69

commit v4 on v3

--- a/solution.py
+++ b/solution.py
@@ -104,21 +104,53 @@
     return jnp.concatenate([x[8:32], pltpu.roll(x[0:8], 7, 0)], axis=0)
 
 
-def pack_kernel(pos_ref, m0, m1, m2, m3, own_rim, across_rim, core_rim, x_ref, rows):
-    xhi, core = pos_ref[0], pos_ref[1]
-    ch = xhi * 2 + core
+def rim_kernel(pos_ref, above, below, left, right, own_ref, other_ref, tile, edge):
+    xhi = pos_ref[0]
+
+    def one(i, _):
+        for out, start in ((own_ref, 3 * xhi), (other_ref, 3 * (1 - xhi))):
+            b, f = i // 5, start + i % 5
+            tile[0:30, :] = above[b, f].astype(F32)
+            tile[32:62, :] = below[b, f].astype(F32)
+            for k, side in enumerate((right, left)):
+                edge[k, 0:10, :] = side[b, f].astype(F32)
+                tile[30 + k:31 + k, :] = edge[k, 0:1, :]
+                tile[62 + k:63 + k, :] = edge[k, 9:10, :]
+                tile[64 + 8 * k:72 + 8 * k, :] = edge[k, 1:9, :]
+            out[pl.ds(pl.multiple_of(i * 80, 16), 80), :] = tile[...].astype(BF16)
+        return 0
+
+    lax.fori_loop(0, 10, one, 0)
+
+
+def pack_rims(position, above, below, left, right):
+    vmem = pl.BlockSpec(memory_space=pltpu.VMEM)
+    return pl.pallas_call(
+        rim_kernel,
+        out_shape=[jax.ShapeDtypeStruct((800, 128), BF16)] * 2,
+        in_specs=[pl.BlockSpec(memory_space=pltpu.SMEM)] + [vmem] * 4,
+        out_specs=[vmem] * 2,
+        scratch_shapes=[pltpu.VMEM((80, 128), F32), pltpu.VMEM((2, 16, 128), F32)],
+        compiler_params=pltpu.CompilerParams(vmem_limit_bytes=16 * 2**20),
+        name="pack_rims",
+    )(position, above, below, left, right)
+
+
+def pack_kernel(pos_ref, m0, m1, m2, m3, r0, r1, r2, r3, x_ref, rows):
+    xhi = pos_ref[0]
+    ch = xhi * 2 + pos_ref[1]
+    mains, rims = (m0, m1, m2, m3), (r0, r1, r2, r3)
 
     def one(i, _):
         b, f = i // 5, i % 5
         to = jnp.where(xhi == 1, 4 - f, f)
-        for r, main in enumerate((m0, m1, m2, m3)):
-            rim = (own_rim, core_rim, across_rim, core_rim)[r]
-            at = pl.multiple_of(i * 80 + (800 if r == 3 else 0), 16)
-            strips = rim[pl.ds(at, 80), :].astype(F32)
+        for r, (main, rim) in enumerate(zip(mains, rims)):
+            strips = rim[pl.ds(pl.multiple_of(i * 80, 16), 80), :].astype(F32)
             rows[r, 0:32, :] = strips[0:32]
             rows[r, 288:320, :] = strips[32:64]
             for h in range(8):
-                rows[r, (h + 1) * 32:(h + 1) * 32 + 32, :] = main[pl.ds(pl.multiple_of(i * 256 + h * 32, 32), 32), :].astype(F32)
+                at = pl.ds(pl.multiple_of(i * 256 + h * 32, 32), 32)
+                rows[r, (h + 1) * 32:(h + 2) * 32, :] = main[at, :].astype(F32)
             rows[r, pl.ds(62, 8, stride=32), :] = strips[64:72]
             rows[r, pl.ds(63, 8, stride=32), :] = strips[72:80]
             for h in range(10):
@@ -129,20 +161,21 @@
     lax.fori_loop(0, 10, one, 0)
 
 
-def pack_cells(position, pieces):
+def pack_cells(position, mains, rims):
     vmem = pl.BlockSpec(memory_space=pltpu.VMEM)
     return pl.pallas_call(
         pack_kernel,
         out_shape=jax.ShapeDtypeStruct((4, 2, 1600, 128), BF16),
-        in_specs=[pl.BlockSpec(memory_space=pltpu.SMEM)] + [vmem] * 7,
+        in_specs=[pl.BlockSpec(memory_space=pltpu.SMEM)] + [vmem] * 8,
         out_specs=vmem,
         scratch_shapes=[pltpu.VMEM((4, 320, 128), F32)],
-        compiler_params=pltpu.CompilerParams(vmem_limit_bytes=32 * 2**20),
+        compiler_params=pltpu.CompilerParams(vmem_limit_bytes=16 * 2**20),
         name="pack_cells",
-    )(position, *pieces)
-
-
-def block_kernel(pos_ref, x_ref, p0, p1, p2, p3, k_ref, kept_ref, sent_ref, w_scr, wp_scr, t0, t1, hidden, acc, rows):
+    )(position, *mains, *rims)
+
+
+def block_kernel(pos_ref, x_ref, p0, p1, p2, p3, k_ref, kept_ref, sent_ref,
+                 w_scr, wp_scr, t0, t1, hidden, acc, rows):
     xhi, core, y, z, xlo = (pos_ref[i] for i in range(5))
     for r, piece in enumerate((p0, p1, p2, p3)):
         for o in range(4):
@@ -288,8 +321,15 @@
 
     half = expand_weight * jnp.asarray(0.5, BF16)
     shard = jnp.stack([half[:, 0], half[:, 1], project_weight.T])
-    shard = jnp.stack([shard, send(shard, BESIDE), send(shard, ACROSS), send(shard, DIAGONAL)])
+    taps = depth_kernel.reshape(3, 9, 2, 512)
+    back = taps[::-1]
+    there = jnp.where(xhi == 1, taps, back).astype(BF16).reshape(54, 512)
+    taps = jnp.where(xhi == 1, back, taps)
+    far = send(jnp.concatenate([shard.reshape(48, 512), there]), ACROSS)
+    shard = jnp.stack([shard, send(shard, BESIDE), far[:48].reshape(3, 16, 512), send(shard, DIAGONAL)])
     shard = shard.reshape(2, 2, 3, 16, 512)
+    taps = jnp.concatenate(
+        [taps.reshape(3, 9, 2, 4, 128), far[48:].astype(F32).reshape(3, 9, 2, 4, 128)], axis=3)
     above = send(cells[:, :, 7], row_step(1))
     below = send(cells[:, :, 0], row_step(-1))
 
@@ -303,33 +343,21 @@
     def edge(column):
         return jnp.concatenate([above[:, :, None, column], cells[:, :, :, column], below[:, :, None, column]], axis=2)
 
-    shard, first, last = lax.optimization_barrier((jnp.stack(near), edge(0), edge(29)))
+    left, right = send(edge(29), column_step(1)), send(edge(0), column_step(-1))
+    shard, left, right = lax.optimization_barrier((jnp.stack(near), left, right))
     weights = [shard] + [send(shard, around_by_core(1, -by)) for by in (1, 2, 3)]
-    left = send(last, column_step(1))
-    right = send(first, column_step(-1))
-
-    def rim(start):
-        a, b, l, r = (lax.dynamic_slice_in_dim(v, start, 5, 1) for v in (above, below, left, right))
-        return jnp.concatenate(
-            [a, r[:, :, :1], l[:, :, :1], b, r[:, :, 9:], l[:, :, 9:], r[:, :, 1:9], l[:, :, 1:9]],
-            axis=2).reshape(800, 128)
-
-    taps = depth_kernel.reshape(3, 9, 2, 4, 128)
-    taps = jnp.where(xhi == 1, taps[::-1], taps)
-    own_rim = rim(3 * xhi)
-    across_rim = send(jnp.concatenate([rim(3 * (1 - xhi)), taps.reshape(216, 128).astype(BF16)]), ACROSS)
-    across, across_rim, weights[1] = lax.optimization_barrier((across, across_rim, weights[1]))
-    core_rim = send(jnp.concatenate([own_rim, across_rim[:800]]), CORES)
-    pieces = [own, own_there, across, send(across, CORES), own_rim, across_rim, core_rim]
-    taps = jnp.concatenate([taps, across_rim[800:].astype(F32).reshape(3, 9, 2, 4, 128)[::-1]], axis=3)
+    own_rim, other_rim = pack_rims(position, above, below, left, right)
+    across_rim = send(other_rim, ACROSS)
+    across, across_rim, weights[2] = lax.optimization_barrier((across, across_rim, weights[2]))
+    rims = [own_rim, send(own_rim, CORES), across_rim, send(across_rim, CORES)]
+    mains = [own, own_there, across, send(across, CORES)]
     by_frame = [sum(row[i] * taps[i] for i in range(3) if row[i]) for row in TAPS]
     by_frame = jnp.stack(by_frame).reshape(6, 3, 3, 2, 8, 128)
     by_row = [sum(row[j] * by_frame[:, j] for j in range(3) if row[j]) for row in ROW_TAPS]
     taps = jnp.stack(by_row, axis=1).reshape(6, 12, 2, 8, 128)
     taps = taps * jnp.array([1.0, 0.5], F32)[None, None, :, None, None]
 
-    packed = pack_cells(position, pieces)
-    kept, sent = run_block(position, packed, weights, taps)
+    kept, sent = run_block(position, pack_cells(position, mains, rims), weights, taps)
     total = kept + send(sent, CORES).astype(F32)
     return total[:, :, None, :, :30].astype(BF16)
 

time: 108 us -> 105 us (0.972)
  local copies, waits for them, and re-layouts: 14.4 us -> 8.05 us
  starting transfers between devices: 36.3 us -> 38 us
    slice x7 -> x4, local copies, waits for them, and re-layouts: 5.04 us -> 0.16 us  [the longest x3 0.16 us: edge(): cells[:, :, :, column]]
    unnamed x15 -> x18, local copies, waits for them, and re-layouts: 1.76 us -> 4.95 us
    concatenate x2 -> x0, local copies, waits for them, and re-layouts: 3.18 us -> none  [rim(): jnp.concatenate([a, r[:, :, :1], l[:, :, :1], b, r[:, :, 9:], l[:, :, 9:]...]
    ppermute x19 -> x20, starting transfers between devices: 36.3 us -> 38 us  [send(): return lax.ppermute(value, BOTH, pairs)]
    rev x1 -> x0, local copies, waits for them, and re-layouts: 1.47 us -> none  [on_device(): across_rim[800:].astype(F32).reshape(3, 9, 2, 4, 128)[::-1]]
    ppermute x19 -> x20, waiting for transfers between devices: 12.6 us -> 13 us  [send(): return lax.ppermute(value, BOTH, pairs)]
  transfers between devices with their start and end apart: 19 -> 20, of which waited for: 8 -> 5; matrix products, arithmetic and copies ran while one was open for 12% -> 5% of each run, Pallas kernels for 2% -> 2%
where the time goes in v4:
time: 105 us
  Pallas kernels  39.4 us (38%)
  starting transfers between devices  38 us (36%)
  waiting for transfers between devices  13 us (12%)
  local copies, waits for them, and re-layouts  8.05 us (8%)
  other arithmetic  6.13 us (6%)
    ppermute x20, starting transfers between devices, send(): return lax.ppermute(value, BOTH, pairs)  38 us
    pallas_call x1, Pallas kernels, run_block(): pl.pallas_call(block_kernel, out_shape=[jax.ShapeDtypeStruct((2, 2, 8, 32...  36.9 us
    ppermute x20, waiting for transfers between devices, send(): return lax.ppermute(value, BOTH, pairs)  13 us
    unnamed x18, local copies, waits for them, and re-layouts  4.95 us
  transfers between devices with their start and end apart: 20, of which 5 were waited for; matrix products, arithmetic and copies ran while one was open for 5% of the time, Pallas kernels for 2%

profile of v4, /device:TPU:1, one launch (start us, length us, event | category | flops | bytes accessed | tf_op | source)
XLA Modules:
  0.0 105.1 jit_solution(4074894606765353951)
XLA Ops:
  0.0 0.8 copy_multiply_fusion
  0.8 0.7 fusion.5
  1.5 2.1 %collective-permute-start = (bf16[3,16,512]{2,1,0:T(8,128)(2,1)S(1)}, bf16[3,16,512]{2,1,0:T(8,128)(2,1)S(1)}, u32[]{:S(2)}, u32[]{:S(2)}) collective-permute-start(bf16[3,16,512]{2,1,0:T(8,128)(2,1)S(1)} %get-tuple-element.52), channel_id=1, source_target_pairs={{0,4},{1,5},{2,6},{3,7},{4,0},{5,1},{6,2},{7,3},{8,12},{9,13},{10,... | collective-permute-start | bytes 147464 | tf_op jit(solution)/shard_map/ppermute | solution.py:69
  3.7 1.8 %collective-permute-start.2 = (bf16[3,16,512]{2,1,0:T(8,128)(2,1)S(1)}, bf16[3,16,512]{2,1,0:T(8,128)(2,1)S(1)}, u32[]{:S(2)}, u32[]{:S(2)}) collective-permute-start(bf16[3,16,512]{2,1,0:T(8,128)(2,1)S(1)} %get-tuple-element.52), channel_id=1, source_target_pairs={{0,68},{1,69},{2,70},{3,71},{4,64},{5,65},{6,66},{7,67},{8,76},{9,... | collective-permute-start | bytes 147464 | tf_op jit(solution)/shard_map/ppermute | solution.py:69
  5.5 1.0 fusion.2
  6.6 0.7 collective-permute-start.1
  7.3 1.4 %copy.28 = bf16[2,8,1,8,30,128]{5,4,1,0,3,2:T(8,128)(2,1)S(1)} copy(bf16[2,8,1,8,30,128]{5,3,4,2,1,0:T(8,128)(2,1)} %param.5) | data formatting | bytes 1966080 | tf_op args[0]
  8.7 0.7 slice_bitcast_fusion
  9.4 2.7 %collective-permute-start.5 = (bf16[2,8,30,128]{3,2,1,0:T(8,128)(2,1)}, bf16[2,8,30,128]{3,2,1,0:T(8,128)(2,1)S(1)}, u32[]{:S(2)}, u32[]{:S(2)}) collective-permute-start(bf16[2,8,30,128]{3,2,1,0:T(8,128)(2,1)} %get-tuple-element.36), channel_id=1, source_target_pairs={{0,4},{1,5},{2,6},{3,7},{4,8},{5,9},{6,10},{7,11},{8,12},{9,13},{1... | collective-permute-start | bytes 368648 | tf_op jit(solution)/shard_map/ppermute | solution.py:69
  12.1 1.3 %collective-permute-start.6 = (bf16[2,8,30,128]{3,2,1,0:T(8,128)(2,1)S(1)}, bf16[2,8,30,128]{3,2,1,0:T(8,128)(2,1)S(1)}, u32[]{:S(2)}, u32[]{:S(2)}) collective-permute-start(bf16[2,8,30,128]{3,2,1,0:T(8,128)(2,1)S(1)} %get-tuple-element.35), channel_id=1, source_target_pairs={{4,0},{5,1},{6,2},{7,3},{8,4},{9,5},{10,6},{11,7},{12,8},{13,9},{1... | collective-permute-start | bytes 368648 | tf_op jit(solution)/shard_map/ppermute | solution.py:69
  13.4 0.0 copy-done.4
  13.5 0.1 reshape.45
  13.7 0.1 stack.81.pos_ref
  13.8 0.0 collective-permute-done.1
  13.8 0.0 collective-permute-done
  13.8 0.0 collective-permute-done.2
  13.8 5.0 %collective-permute-start.7 = (bf16[2,2,3,16,512]{4,3,2,1,0:T(8,128)(2,1)S(1)}, bf16[2,2,3,16,512]{4,3,2,1,0:T(8,128)(2,1)S(1)}, u32[]{:S(2)}, u32[]{:S(2)}) collective-permute-start(bf16[2,2,3,16,512]{4,3,2,1,0:T(8,128)(2,1)S(1)} %bitcast.54), channel_id=1, source_target_pairs={{0,3},{1,0},{2,1},{3,2},{4,7},{5,4},{6,5},{7,6},{8,11},{9,8},{10,9... | collective-permute-start | bytes 589832 | tf_op jit(solution)/shard_map/ppermute | solution.py:69
  18.8 0.3 collective-permute-start.8
  19.1 0.7 collective-permute-start.9
  19.8 0.1 fusion.8
  20.0 0.4 pad_dynamic-slice_fusion
  20.4 0.1 copy.20
  20.5 0.1 add_add_fusion.2
  20.6 0.0 collective-permute-done.5.above
  20.6 2.4 %collective-permute-start.4 = (bf16[2560,128]{1,0:T(8,128)(2,1)S(1)}, bf16[2560,128]{1,0:T(8,128)(2,1)S(1)}, u32[]{:S(2)}, u32[]{:S(2)}) collective-permute-start(bf16[2560,128]{1,0:T(8,128)(2,1)S(1)} %bitcast.59), channel_id=1, source_target_pairs={{0,64},{1,65},{2,66},{3,67},{4,68},{5,69},{6,70},{7,71},{8,72},{9,... | collective-permute-start | bytes 1966088 | tf_op jit(solution)/shard_map/ppermute | solution.py:69
  23.0 0.0 collective-permute-done.6.below
  23.1 3.5 %collective-permute-start.10 = (bf16[2,8,10,128]{3,2,1,0:T(8,128)(2,1)S(1)}, bf16[2,8,10,128]{3,2,1,0:T(8,128)(2,1)S(1)}, u32[]{:S(2)}, u32[]{:S(2)}) collective-permute-start(bf16[2,8,10,128]{3,2,1,0:T(8,128)(2,1)S(1)} %pad_maximum_fusion.5), channel_id=1, source_target_pairs={{0,1},{1,2},{2,3},{4,5},{5,6},{6,7},{8,9},{9,10},{10,11},{12,13},{... | collective-permute-start | bytes 122888 | tf_op jit(solution)/shard_map/ppermute | solution.py:69
  26.7 0.0 collective-permute-done.7
  26.7 1.3 %collective-permute-start.11 = (bf16[2,8,10,128]{3,2,1,0:T(8,128)(2,1)S(1)}, bf16[2,8,10,128]{3,2,1,0:T(8,128)(2,1)S(1)}, u32[]{:S(2)}, u32[]{:S(2)}) collective-permute-start(bf16[2,8,10,128]{3,2,1,0:T(8,128)(2,1)S(1)} %pad_maximum_fusion.6), channel_id=1, source_target_pairs={{1,0},{2,1},{3,2},{5,4},{6,5},{7,6},{9,8},{10,9},{11,10},{13,12},{... | collective-permute-start | bytes 122888 | tf_op jit(solution)/shard_map/ppermute | solution.py:69
  28.0 0.0 collective-permute-done.8
  28.0 0.0 collective-permute-done.9
  28.0 1.1 %pad_maximum_fusion.p0 = bf16[4,2,2,3,16,512]{5,4,3,2,1,0:T(8,128)(2,1)S(1)} fusion(bf16[1,2,2,3,16,512]{5,4,3,2,1,0:T(8,128)(2,1)} %bitcast.24, bf16[1,2,2,3,16,512]{5,4,3,2,1,0:T(8,128)(2,1)} %bitcast.23, bf16[1,2,2,3,16,512]{5,4,3,2,1,0:T(8,128)(2,1)S(1)} %bitcast.67, bf16[1,2,2,3,16,512]{5,4,3,2,1,0:T(8,128)(2,1)S(1)} %bitcast.57), kind=kLoop, calls=%fused_computation.6 | loop fusion | flops 1179648 | bytes 1572864 | tf_op jit(solution)/shard_map/stack | solution.py:347
  29.2 0.0 collective-permute-done.10.left
  29.2 3.0 %collective-permute-done.11.right = bf16[2,8,10,128]{3,2,1,0:T(8,128)(2,1)S(1)} collective-permute-done((bf16[2,8,10,128]{3,2,1,0:T(8,128)(2,1)S(1)}, bf16[2,8,10,128]{3,2,1,0:T(8,128)(2,1)S(1)}, u32[]{:S(2)}, u32[]{:S(2)}) %collective-permute-start.11) | collective-permute-done | bytes 40992 | tf_op jit(solution)/shard_map/ppermute | solution.py:69
  32.2 3.6 %collective-permute-start.13 = (bf16[4,2,2,3,16,512]{5,4,3,2,1,0:T(8,128)(2,1)S(1)}, bf16[4,2,2,3,16,512]{5,4,3,2,1,0:T(8,128)(2,1)S(1)}, u32[]{:S(2)}, u32[]{:S(2)}) collective-permute-start(bf16[4,2,2,3,16,512]{5,4,3,2,1,0:T(8,128)(2,1)S(1)} %pad_maximum_fusion.p0), channel_id=1, source_target_pairs={{0,16},{1,17},{2,18},{3,19},{4,20},{5,21},{6,22},{7,23},{8,24},{9,... | collective-permute-start | bytes 2359304 | tf_op jit(solution)/shard_map/ppermute | solution.py:69
  35.9 0.0 copy-start.5
  35.9 0.8 pack_rims.1
  36.7 0.2 collective-permute-start.12
  37.0 0.7 collective-permute-start.17
  37.7 0.7 collective-permute-start.18
  38.5 0.1 copy.19
  38.5 4.7 %collective-permute-done.12.r2 = bf16[800,128]{1,0:T(8,128)(2,1)S(1)} collective-permute-done((bf16[800,128]{1,0:T(8,128)(2,1)S(1)}, bf16[800,128]{1,0:T(8,128)(2,1)S(1)}, u32[]{:S(2)}, u32[]{:S(2)}) %collective-permute-start.12) | collective-permute-done | bytes 204832 | tf_op jit(solution)/shard_map/ppermute | solution.py:69
  43.2 6.4 %collective-permute-start.3 = (bf16[2560,128]{1,0:T(8,128)(2,1)S(1)}, bf16[2560,128]{1,0:T(8,128)(2,1)S(1)}, u32[]{:S(2)}, u32[]{:S(2)}) collective-permute-start(bf16[2560,128]{1,0:T(8,128)(2,1)S(1)} %bitcast.48), channel_id=1, source_target_pairs={{0,32},{1,33},{2,34},{3,35},{4,36},{5,37},{6,38},{7,39},{8,40},{9,... | collective-permute-start | bytes 1966088 | tf_op jit(solution)/shard_map/ppermute | solution.py:69
  49.6 0.0 collective-permute-done.4.m2
  49.6 0.0 collective-permute-done.13.p2
  49.6 1.8 %collective-permute-start.14 = (bf16[2560,128]{1,0:T(8,128)(2,1)S(1)}, bf16[2560,128]{1,0:T(8,128)(2,1)S(1)}, u32[]{:S(2)}, u32[]{:S(2)}) collective-permute-start(bf16[2560,128]{1,0:T(8,128)(2,1)S(1)} %collective-permute-done.4.m2), channel_id=1, source_target_pairs={{0,32},{1,33},{2,34},{3,35},{4,36},{5,37},{6,38},{7,39},{8,40},{9,... | collective-permute-start | bytes 1966088 | tf_op jit(solution)/shard_map/ppermute | solution.py:69
  51.4 0.1 collective-permute-start.15
  51.6 1.8 %collective-permute-done.15.r1 = bf16[800,128]{1,0:T(8,128)(2,1)S(1)} collective-permute-done((bf16[800,128]{1,0:T(8,128)(2,1)S(1)}, bf16[800,128]{1,0:T(8,128)(2,1)S(1)}, u32[]{:S(2)}, u32[]{:S(2)}) %collective-permute-start.15) | collective-permute-done | bytes 204832 | tf_op jit(solution)/shard_map/ppermute | solution.py:69
  53.4 0.4 collective-permute-start.16
  53.8 0.1 broadcast_multiply_fusion.k_ref
  53.9 0.0 collective-permute-done.3.m1
  53.9 0.9 collective-permute-done.16.r3
  54.9 0.0 collective-permute-done.14.m3
  54.9 1.7 %pack_cells.1.x_ref = bf16[4,2,1600,128]{3,2,1,0:T(8,128)(2,1)S(1)} custom-call(s32[5]{0:T(128)S(1)} %stack.81.pos_ref, bf16[2560,128]{1,0:T(8,128)(2,1)S(1)} %bitcast.49, bf16[2560,128]{1,0:T(8,128)(2,1)S(1)} %collective-permute-done.3.m1, bf16[2560,128]{1,0:T(8,128)(2,1)S(1)} %collective-permute-done.4.m2, ...), custom_call_target="tpu_custom_call" | custom-call | tf_op jit(solution)/shard_map/pack_cells/pallas_call | solution.py:166
  56.6 1.7 %copy-done = bf16[4,2,1600,128]{3,2,1,0:T(8,128)(2,1)} copy-done((bf16[4,2,1600,128]{3,2,1,0:T(8,128)(2,1)}, bf16[4,2,1600,128]{3,2,1,0:T(8,128)(2,1)S(1)}, u32[]{:S(2)}) %copy-start) | copy-done | bytes 3276824
  58.3 0.0 collective-permute-done.17.p1
  58.3 0.0 collective-permute-done.18.p3
  58.3 0.9 copy-done.2
  59.1 0.9 copy-done.3
  60.1 36.9 %gated_block.1 = (f32[2,2,8,32,512]{4,3,2,1,0:T(8,128)}, bf16[2,2,8,32,512]{4,3,2,1,0:T(8,128)(2,1)}) custom-call(s32[5]{0:T(128)S(1)} %stack.81.pos_ref, bf16[4,2,1600,128]{3,2,1,0:T(8,128)(2,1)} %copy-done, bf16[4,2,2,3,16,512]{5,4,3,2,1,0:T(8,128)(2,1)S(1)} %pad_maximum_fusion.p0, bf16[4,2,2,3,16,512]{5,4,3,2,1,0:T(8,128)(2,1)} %copy-done.2, ...), custom_call_target="tpu_custom_call" | custom-call | tf_op jit(solution)/shard_map/gated_block/pallas_call | solution.py:296
  97.0 2.1 %collective-permute-start.19 = (bf16[2,2,8,32,512]{4,3,2,1,0:T(8,128)(2,1)}, bf16[2,2,8,32,512]{4,3,2,1,0:T(8,128)(2,1)S(1)}, u32[]{:S(2)}, u32[]{:S(2)}) collective-permute-start(bf16[2,2,8,32,512]{4,3,2,1,0:T(8,128)(2,1)} %get-tuple-element.28), channel_id=1, source_target_pairs={{0,32},{1,33},{2,34},{3,35},{4,36},{5,37},{6,38},{7,39},{8,40},{9,... | collective-permute-start | bytes 3145736 | tf_op jit(solution)/shard_map/ppermute | solution.py:69
  99.1 2.5 %collective-permute-done.19 = bf16[2,2,8,32,512]{4,3,2,1,0:T(8,128)(2,1)S(1)} collective-permute-done((bf16[2,2,8,32,512]{4,3,2,1,0:T(8,128)(2,1)}, bf16[2,2,8,32,512]{4,3,2,1,0:T(8,128)(2,1)S(1)}, u32[]{:S(2)}, u32[]{:S(2)}) %collective-permute-start.19) | collective-permute-done | bytes 1048608 | tf_op jit(solution)/shard_map/ppermute | solution.py:69
  101.6 2.0 %fusion.1 = bf16[2,2,1,8,30,512]{5,4,3,1,0,2:T(8,128)(2,1)S(1)} fusion(f32[2,2,8,32,512]{4,3,2,1,0:T(8,128)} %get-tuple-element.27, bf16[2,2,8,32,512]{4,3,2,1,0:T(8,128)(2,1)S(1)} %collective-permute-done.19), kind=kLoop, calls=%fused_computation.2 | loop fusion | flops 1474560 | bytes 3932160 | tf_op jit(solution)/shard_map/convert_element_type | solution.py:362
  103.6 1.5 %copy.23 = bf16[2,2,1,8,30,512]{5,3,4,2,1,0:T(8,128)(2,1)} copy(bf16[2,2,1,8,30,512]{5,4,3,1,0,2:T(8,128)(2,1)S(1)} %fusion.1) | data formatting | bytes 1966080 | tf_op jit(solution)/shard_map/convert_element_type | solution.py:362
  (30 shorter events, 0.5 us)
Async XLA Ops:
  0.0 13.4 %copy-start.4 = (f32[3,3,3,2,512]{4,3,2,1,0:T(2,128)S(1)}, f32[3,3,3,2,512]{4,3,2,1,0:T(2,128)}, u32[]{:S(2)}) copy-start(f32[3,3,3,2,512]{4,3,2,1,0:T(2,128)} %param.7) | copy-start | bytes 331780
  1.5 12.2 %collective-permute-start = (bf16[3,16,512]{2,1,0:T(8,128)(2,1)S(1)}, bf16[3,16,512]{2,1,0:T(8,128)(2,1)S(1)}, u32[]{:S(2)}, u32[]{:S(2)}) collective-permute-start(bf16[3,16,512]{2,1,0:T(8,128)(2,1)S(1)} %get-tuple-element.52), channel_id=1, source_target_pairs={{0,4},{1,5},{2,6},{3,7},{4,0},{5,1},{6,2},{7,3},{8,12},{9,13},{10,... | collective-permute-start | bytes 147464 | tf_op jit(solution)/shard_map/ppermute | solution.py:69
  3.7 10.1 %collective-permute-start.2 = (bf16[3,16,512]{2,1,0:T(8,128)(2,1)S(1)}, bf16[3,16,512]{2,1,0:T(8,128)(2,1)S(1)}, u32[]{:S(2)}, u32[]{:S(2)}) collective-permute-start(bf16[3,16,512]{2,1,0:T(8,128)(2,1)S(1)} %get-tuple-element.52), channel_id=1, source_target_pairs={{0,68},{1,69},{2,70},{3,71},{4,64},{5,65},{6,66},{7,67},{8,76},{9,... | collective-permute-start | bytes 147464 | tf_op jit(solution)/shard_map/ppermute | solution.py:69
  6.6 7.2 %collective-permute-start.1 = (bf16[102,512]{1,0:T(8,128)(2,1)S(1)}, bf16[102,512]{1,0:T(8,128)(2,1)S(1)}, u32[]{:S(2)}, u32[]{:S(2)}) collective-permute-start(bf16[102,512]{1,0:T(8,128)(2,1)S(1)} %pad_maximum_fusion.3), channel_id=1, source_target_pairs={{0,64},{1,65},{2,66},{3,67},{4,68},{5,69},{6,70},{7,71},{8,72},{9,... | collective-permute-start | bytes 313352 | tf_op jit(solution)/shard_map/ppermute | solution.py:69
  9.4 11.2 %collective-permute-start.5 = (bf16[2,8,30,128]{3,2,1,0:T(8,128)(2,1)}, bf16[2,8,30,128]{3,2,1,0:T(8,128)(2,1)S(1)}, u32[]{:S(2)}, u32[]{:S(2)}) collective-permute-start(bf16[2,8,30,128]{3,2,1,0:T(8,128)(2,1)} %get-tuple-element.36), channel_id=1, source_target_pairs={{0,4},{1,5},{2,6},{3,7},{4,8},{5,9},{6,10},{7,11},{8,12},{9,13},{1... | collective-permute-start | bytes 368648 | tf_op jit(solution)/shard_map/ppermute | solution.py:69
  12.1 10.9 %collective-permute-start.6 = (bf16[2,8,30,128]{3,2,1,0:T(8,128)(2,1)S(1)}, bf16[2,8,30,128]{3,2,1,0:T(8,128)(2,1)S(1)}, u32[]{:S(2)}, u32[]{:S(2)}) collective-permute-start(bf16[2,8,30,128]{3,2,1,0:T(8,128)(2,1)S(1)} %get-tuple-element.35), channel_id=1, source_target_pairs={{4,0},{5,1},{6,2},{7,3},{8,4},{9,5},{10,6},{11,7},{12,8},{13,9},{1... | collective-permute-start | bytes 368648 | tf_op jit(solution)/shard_map/ppermute | solution.py:69
  13.8 12.9 %collective-permute-start.7 = (bf16[2,2,3,16,512]{4,3,2,1,0:T(8,128)(2,1)S(1)}, bf16[2,2,3,16,512]{4,3,2,1,0:T(8,128)(2,1)S(1)}, u32[]{:S(2)}, u32[]{:S(2)}) collective-permute-start(bf16[2,2,3,16,512]{4,3,2,1,0:T(8,128)(2,1)S(1)} %bitcast.54), channel_id=1, source_target_pairs={{0,3},{1,0},{2,1},{3,2},{4,7},{5,4},{6,5},{7,6},{8,11},{9,8},{10,9... | collective-permute-start | bytes 589832 | tf_op jit(solution)/shard_map/ppermute | solution.py:69
  18.8 9.2 %collective-permute-start.8 = (bf16[2,2,3,16,512]{4,3,2,1,0:T(8,128)(2,1)S(1)}, bf16[2,2,3,16,512]{4,3,2,1,0:T(8,128)(2,1)}, u32[]{:S(2)}, u32[]{:S(2)}) collective-permute-start(bf16[2,2,3,16,512]{4,3,2,1,0:T(8,128)(2,1)S(1)} %bitcast.55), channel_id=1, source_target_pairs={{0,2},{1,3},{2,0},{3,1},{4,6},{5,7},{6,4},{7,5},{8,10},{9,11},{10,... | collective-permute-start | bytes 589832 | tf_op jit(solution)/shard_map/ppermute | solution.py:69
  19.1 8.9 %collective-permute-start.9 = (bf16[2,2,3,16,512]{4,3,2,1,0:T(8,128)(2,1)S(1)}, bf16[2,2,3,16,512]{4,3,2,1,0:T(8,128)(2,1)}, u32[]{:S(2)}, u32[]{:S(2)}) collective-permute-start(bf16[2,2,3,16,512]{4,3,2,1,0:T(8,128)(2,1)S(1)} %bitcast.56), channel_id=1, source_target_pairs={{0,1},{1,2},{2,3},{3,0},{4,5},{5,6},{6,7},{7,4},{8,9},{9,10},{10,1... | collective-permute-start | bytes 589832 | tf_op jit(solution)/shard_map/ppermute | solution.py:69
  20.6 29.0 %collective-permute-start.4 = (bf16[2560,128]{1,0:T(8,128)(2,1)S(1)}, bf16[2560,128]{1,0:T(8,128)(2,1)S(1)}, u32[]{:S(2)}, u32[]{:S(2)}) collective-permute-start(bf16[2560,128]{1,0:T(8,128)(2,1)S(1)} %bitcast.59), channel_id=1, source_target_pairs={{0,64},{1,65},{2,66},{3,67},{4,68},{5,69},{6,70},{7,71},{8,72},{9,... | collective-permute-start | bytes 1966088 | tf_op jit(solution)/shard_map/ppermute | solution.py:69
  23.1 6.1 %collective-permute-start.10 = (bf16[2,8,10,128]{3,2,1,0:T(8,128)(2,1)S(1)}, bf16[2,8,10,128]{3,2,1,0:T(8,128)(2,1)S(1)}, u32[]{:S(2)}, u32[]{:S(2)}) collective-permute-start(bf16[2,8,10,128]{3,2,1,0:T(8,128)(2,1)S(1)} %pad_maximum_fusion.5), channel_id=1, source_target_pairs={{0,1},{1,2},{2,3},{4,5},{5,6},{6,7},{8,9},{9,10},{10,11},{12,13},{... | collective-permute-start | bytes 122888 | tf_op jit(solution)/shard_map/ppermute | solution.py:69
  26.7 5.5 %collective-permute-start.11 = (bf16[2,8,10,128]{3,2,1,0:T(8,128)(2,1)S(1)}, bf16[2,8,10,128]{3,2,1,0:T(8,128)(2,1)S(1)}, u32[]{:S(2)}, u32[]{:S(2)}) collective-permute-start(bf16[2,8,10,128]{3,2,1,0:T(8,128)(2,1)S(1)} %pad_maximum_fusion.6), channel_id=1, source_target_pairs={{1,0},{2,1},{3,2},{5,4},{6,5},{7,6},{9,8},{10,9},{11,10},{13,12},{... | collective-permute-start | bytes 122888 | tf_op jit(solution)/shard_map/ppermute | solution.py:69
  32.2 17.4 %collective-permute-start.13 = (bf16[4,2,2,3,16,512]{5,4,3,2,1,0:T(8,128)(2,1)S(1)}, bf16[4,2,2,3,16,512]{5,4,3,2,1,0:T(8,128)(2,1)S(1)}, u32[]{:S(2)}, u32[]{:S(2)}) collective-permute-start(bf16[4,2,2,3,16,512]{5,4,3,2,1,0:T(8,128)(2,1)S(1)} %pad_maximum_fusion.p0), channel_id=1, source_target_pairs={{0,16},{1,17},{2,18},{3,19},{4,20},{5,21},{6,22},{7,23},{8,24},{9,... | collective-permute-start | bytes 2359304 | tf_op jit(solution)/shard_map/ppermute | solution.py:69
  35.9 17.9 %copy-start.5 = (f32[2]{0:T(128)S(1)}, f32[2]{0:T(128)}, u32[]{:S(2)}) copy-start(f32[2]{0:T(128)} %constant.91.clone) | copy-start | bytes 28
  36.7 6.5 %collective-permute-start.12 = (bf16[800,128]{1,0:T(8,128)(2,1)S(1)}, bf16[800,128]{1,0:T(8,128)(2,1)S(1)}, u32[]{:S(2)}, u32[]{:S(2)}) collective-permute-start(bf16[800,128]{1,0:T(8,128)(2,1)S(1)} %get-tuple-element.21), channel_id=1, source_target_pairs={{0,64},{1,65},{2,66},{3,67},{4,68},{5,69},{6,70},{7,71},{8,72},{9,... | collective-permute-start | bytes 614408 | tf_op jit(solution)/shard_map/ppermute | solution.py:69
  37.0 21.3 %collective-permute-start.17 = (bf16[4,2,2,3,16,512]{5,4,3,2,1,0:T(8,128)(2,1)S(1)}, bf16[4,2,2,3,16,512]{5,4,3,2,1,0:T(8,128)(2,1)S(1)}, u32[]{:S(2)}, u32[]{:S(2)}) collective-permute-start(bf16[4,2,2,3,16,512]{5,4,3,2,1,0:T(8,128)(2,1)S(1)} %pad_maximum_fusion.p0), channel_id=1, source_target_pairs={{0,24},{1,25},{2,26},{3,27},{4,28},{5,29},{6,30},{7,31},{8,0},{9,1... | collective-permute-start | bytes 2359304 | tf_op jit(solution)/shard_map/ppermute | solution.py:69
  37.7 20.6 %collective-permute-start.18 = (bf16[4,2,2,3,16,512]{5,4,3,2,1,0:T(8,128)(2,1)S(1)}, bf16[4,2,2,3,16,512]{5,4,3,2,1,0:T(8,128)(2,1)S(1)}, u32[]{:S(2)}, u32[]{:S(2)}) collective-permute-start(bf16[4,2,2,3,16,512]{5,4,3,2,1,0:T(8,128)(2,1)S(1)} %pad_maximum_fusion.p0), channel_id=1, source_target_pairs={{0,8},{1,9},{2,10},{3,11},{4,12},{5,13},{6,14},{7,15},{8,16},{9,17... | collective-permute-start | bytes 2359304 | tf_op jit(solution)/shard_map/ppermute | solution.py:69
  43.2 10.7 %collective-permute-start.3 = (bf16[2560,128]{1,0:T(8,128)(2,1)S(1)}, bf16[2560,128]{1,0:T(8,128)(2,1)S(1)}, u32[]{:S(2)}, u32[]{:S(2)}) collective-permute-start(bf16[2560,128]{1,0:T(8,128)(2,1)S(1)} %bitcast.48), channel_id=1, source_target_pairs={{0,32},{1,33},{2,34},{3,35},{4,36},{5,37},{6,38},{7,39},{8,40},{9,... | collective-permute-start | bytes 1966088 | tf_op jit(solution)/shard_map/ppermute | solution.py:69
  49.6 7.0 %copy-start.1 = (bf16[4,2,2,3,16,512]{5,4,3,2,1,0:T(8,128)(2,1)}, bf16[4,2,2,3,16,512]{5,4,3,2,1,0:T(8,128)(2,1)S(1)}, u32[]{:S(2)}) copy-start(bf16[4,2,2,3,16,512]{5,4,3,2,1,0:T(8,128)(2,1)S(1)} %collective-permute-done.13.p2) | copy-start | bytes 2359300
  49.6 5.3 %collective-permute-start.14 = (bf16[2560,128]{1,0:T(8,128)(2,1)S(1)}, bf16[2560,128]{1,0:T(8,128)(2,1)S(1)}, u32[]{:S(2)}, u32[]{:S(2)}) collective-permute-start(bf16[2560,128]{1,0:T(8,128)(2,1)S(1)} %collective-permute-done.4.m2), channel_id=1, source_target_pairs={{0,32},{1,33},{2,34},{3,35},{4,36},{5,37},{6,38},{7,39},{8,40},{9,... | collective-permute-start | bytes 1966088 | tf_op jit(solution)/shard_map/ppermute | solution.py:69
  51.4 2.0 %collective-permute-start.15 = (bf16[800,128]{1,0:T(8,128)(2,1)S(1)}, bf16[800,128]{1,0:T(8,128)(2,1)S(1)}, u32[]{:S(2)}, u32[]{:S(2)}) collective-permute-start(bf16[800,128]{1,0:T(8,128)(2,1)S(1)} %get-tuple-element.24.r0), channel_id=1, source_target_pairs={{0,32},{1,33},{2,34},{3,35},{4,36},{5,37},{6,38},{7,39},{8,40},{9,... | collective-permute-start | bytes 614408 | tf_op jit(solution)/shard_map/ppermute | solution.py:69
  53.4 1.5 %collective-permute-start.16 = (bf16[800,128]{1,0:T(8,128)(2,1)S(1)}, bf16[800,128]{1,0:T(8,128)(2,1)S(1)}, u32[]{:S(2)}, u32[]{:S(2)}) collective-permute-start(bf16[800,128]{1,0:T(8,128)(2,1)S(1)} %collective-permute-done.12.r2), channel_id=1, source_target_pairs={{0,32},{1,33},{2,34},{3,35},{4,36},{5,37},{6,38},{7,39},{8,40},{9,... | collective-permute-start | bytes 614408 | tf_op jit(solution)/shard_map/ppermute | solution.py:69
  56.6 1.7 %copy-start = (bf16[4,2,1600,128]{3,2,1,0:T(8,128)(2,1)}, bf16[4,2,1600,128]{3,2,1,0:T(8,128)(2,1)S(1)}, u32[]{:S(2)}) copy-start(bf16[4,2,1600,128]{3,2,1,0:T(8,128)(2,1)S(1)} %pack_cells.1.x_ref) | copy-start | bytes 9830404
  58.3 0.9 copy-start.2
  59.1 0.9 copy-start.3
  97.0 4.6 %collective-permute-start.19 = (bf16[2,2,8,32,512]{4,3,2,1,0:T(8,128)(2,1)}, bf16[2,2,8,32,512]{4,3,2,1,0:T(8,128)(2,1)S(1)}, u32[]{:S(2)}, u32[]{:S(2)}) collective-permute-start(bf16[2,2,8,32,512]{4,3,2,1,0:T(8,128)(2,1)} %get-tuple-element.28), channel_id=1, source_target_pairs={{0,32},{1,33},{2,34},{3,35},{4,36},{5,37},{6,38},{7,39},{8,40},{9,... | collective-permute-start | bytes 3145736 | tf_op jit(solution)/shard_map/ppermute | solution.py:69

commit v5 on v4

--- a/solution.py
+++ b/solution.py
@@ -268,27 +268,29 @@
     project(1)
 
     def move(i, _):
-        b, f, h = i // 16, i // 8 % 2, i % 8
-        for slot in range(2):
-            true = (core ^ slot) * 2 + f
-            frame = jnp.where(xhi == 1, 3 - true, true)
-            at = pl.ds(pl.multiple_of((h * 4 + frame) * 32, 32), 32)
-            total = acc[b, at, :]
-            if slot == 0:
-                cells_at = pl.ds(pl.multiple_of(((h + 1) * 5 + frame) * 32, 32), 32)
-                cells = jnp.concatenate([x_ref[m, b, cells_at, :] for m in range(4)], axis=1)
-                total = total + cells.astype(F32)
-            for v in range(4):
-                for q in range(4):
-                    rows[slot * 4 + v, pl.ds(q, 8, stride=4), :] = total[q * 8:(q + 1) * 8, v * 128:(v + 1) * 128]
-            total = jnp.concatenate([rows[slot * 4 + v] for v in range(4)], axis=1)
-            if slot == 0:
-                kept_ref[b, f, h] = total
-            else:
-                sent_ref[b, f, h] = total.astype(BF16)
-        return 0
-
-    lax.fori_loop(0, 32, move, 0)
+        for u in range(8):
+            b, f, h = i // 2, i % 2, u
+            for slot in range(2):
+                true = (core ^ slot) * 2 + f
+                frame = jnp.where(xhi == 1, 3 - true, true)
+                at = pl.ds(pl.multiple_of((h * 4 + frame) * 32, 32), 32)
+                total = acc[b, at, :]
+                if slot == 0:
+                    cells_at = pl.ds(pl.multiple_of(((h + 1) * 5 + frame) * 32, 32), 32)
+                    cells = jnp.concatenate([x_ref[m, b, cells_at, :] for m in range(4)], axis=1)
+                    total = total + cells.astype(F32)
+                own = u * 8 + slot * 4
+                for v in range(4):
+                    for q in range(4):
+                        rows[own + v, pl.ds(q, 8, stride=4), :] = total[q * 8:(q + 1) * 8, v * 128:(v + 1) * 128]
+        for u in range(8):
+            for slot, out in ((0, kept_ref), (1, sent_ref)):
+                own = u * 8 + slot * 4
+                total = jnp.concatenate([rows[own + v] for v in range(4)], axis=1)
+                out[i // 2, i % 2, u] = total.astype(out.dtype)
+        return 0
+
+    lax.fori_loop(0, 4, move, 0)
 
 
 def run_block(position, cells, weights, taps):
@@ -305,9 +307,9 @@
             pltpu.VMEM((4, 6, 10, 32, 128), F32),
             pltpu.VMEM((4, 1024, 256), BF16),
             pltpu.VMEM((2, 1024, 512), F32),
-            pltpu.VMEM((8, 32, 128), F32),
+            pltpu.VMEM((64, 32, 128), F32),
         ],
-        compiler_params=pltpu.CompilerParams(vmem_limit_bytes=52 * 2**20),
+        compiler_params=pltpu.CompilerParams(vmem_limit_bytes=32 * 2**20),
         name="gated_block",
     )(position, cells, *weights, taps)
 
@@ -344,7 +346,7 @@
         return jnp.concatenate([above[:, :, None, column], cells[:, :, :, column], below[:, :, None, column]], axis=2)
 
     left, right = send(edge(29), column_step(1)), send(edge(0), column_step(-1))
-    shard, left, right = lax.optimization_barrier((jnp.stack(near), left, right))
+    shard, left, right, own_there = lax.optimization_barrier((jnp.stack(near), left, right, own_there))
     weights = [shard] + [send(shard, around_by_core(1, -by)) for by in (1, 2, 3)]
     own_rim, other_rim = pack_rims(position, above, below, left, right)
     across_rim = send(other_rim, ACROSS)

time: 105 us -> 97.2 us (0.926)
  Pallas kernels: 39.4 us -> 35.3 us
  local copies, waits for them, and re-layouts: 8.05 us -> 4.55 us
  other arithmetic: 6.13 us -> 4.6 us
  starting transfers between devices: 38 us -> 39.4 us
    pallas_call x1, Pallas kernels: 36.9 us -> 32.7 us  [run_block(): pl.pallas_call(block_kernel, out_shape=[jax.ShapeDtypeStruct((2, 2, 8, 32...]
    unnamed x18 -> x10, local copies, waits for them, and re-layouts: 4.95 us -> 1.46 us
    convert_element_type x1, other arithmetic: 1.97 us -> 0.43 us  [on_device(): return total[:, :, None, :, :30].astype(BF16)]
    ppermute x20, starting transfers between devices: 38 us -> 39.4 us  [send(): return lax.ppermute(value, BOTH, pairs)]
  transfers between devices with their start and end apart: 20 -> 20, of which waited for: 5 -> 6; matrix products, arithmetic and copies ran while one was open for 5% -> 6% of each run, Pallas kernels for 2% -> 3%
where the time goes in v5:
time: 97.2 us; the launch traced here: 96.9 us
  starting transfers between devices  39.4 us (41%)
  Pallas kernels  35.3 us (36%)
  waiting for transfers between devices  12.6 us (13%)
  other arithmetic  4.6 us (5%)
  local copies, waits for them, and re-layouts  4.55 us (5%)
    ppermute x20, starting transfers between devices, send(): return lax.ppermute(value, BOTH, pairs)  39.4 us
    pallas_call x1, Pallas kernels, run_block(): pl.pallas_call(block_kernel, out_shape=[jax.ShapeDtypeStruct((2, 2, 8, 32...  32.7 us
    ppermute x20, waiting for transfers between devices, send(): return lax.ppermute(value, BOTH, pairs)  12.6 us
  transfers between devices with their start and end apart: 20, of which 6 were waited for; matrix products, arithmetic and copies ran while one was open for 6% of the time, Pallas kernels for 3%

profile of v5, /device:TPU:1, one launch (start us, length us, event | category | flops | bytes accessed | tf_op | source)
XLA Modules:
  0.0 96.9 jit_solution(7270819105917718866)
XLA Ops:
  0.0 0.0 copy-start
  0.0 0.8 copy_multiply_fusion
  0.8 0.7 fusion.5
  1.5 2.1 %collective-permute-start = (bf16[3,16,512]{2,1,0:T(8,128)(2,1)S(1)}, bf16[3,16,512]{2,1,0:T(8,128)(2,1)S(1)}, u32[]{:S(2)}, u32[]{:S(2)}) collective-permute-start(bf16[3,16,512]{2,1,0:T(8,128)(2,1)S(1)} %get-tuple-element.54), channel_id=1, source_target_pairs={{0,4},{1,5},{2,6},{3,7},{4,0},{5,1},{6,2},{7,3},{8,12},{9,13},{10,... | collective-permute-start | bytes 147464 | tf_op jit(solution)/shard_map/ppermute | solution.py:69
  3.7 1.8 %collective-permute-start.2 = (bf16[3,16,512]{2,1,0:T(8,128)(2,1)S(1)}, bf16[3,16,512]{2,1,0:T(8,128)(2,1)S(1)}, u32[]{:S(2)}, u32[]{:S(2)}) collective-permute-start(bf16[3,16,512]{2,1,0:T(8,128)(2,1)S(1)} %get-tuple-element.54), channel_id=1, source_target_pairs={{0,68},{1,69},{2,70},{3,71},{4,64},{5,65},{6,66},{7,67},{8,76},{9,... | collective-permute-start | bytes 147464 | tf_op jit(solution)/shard_map/ppermute | solution.py:69
  5.5 1.0 %fusion.2 = bf16[3,9,2,512]{3,2,1,0:T(2,128)(2,1)S(1)} fusion(f32[3,9,2,512]{3,2,1,0:T(2,128)} %bitcast.60, pred[]{:T(512)S(6)} %eq.8), kind=kLoop, calls=%fused_computation.20 | loop fusion | flops 27648 | bytes 165889 | tf_op jit(solution)/shard_map/convert_element_type | solution.py:328
  6.6 0.7 collective-permute-start.1
  7.3 1.4 %copy.28 = bf16[2,8,1,8,30,128]{5,4,1,0,3,2:T(8,128)(2,1)S(1)} copy(bf16[2,8,1,8,30,128]{5,3,4,2,1,0:T(8,128)(2,1)} %param.5) | data formatting | bytes 1966080 | tf_op args[0]
  8.7 0.7 slice_bitcast_fusion.1
  9.4 2.7 %collective-permute-start.6 = (bf16[2,8,30,128]{3,2,1,0:T(8,128)(2,1)}, bf16[2,8,30,128]{3,2,1,0:T(8,128)(2,1)S(1)}, u32[]{:S(2)}, u32[]{:S(2)}) collective-permute-start(bf16[2,8,30,128]{3,2,1,0:T(8,128)(2,1)} %get-tuple-element.39), channel_id=1, source_target_pairs={{0,4},{1,5},{2,6},{3,7},{4,8},{5,9},{6,10},{7,11},{8,12},{9,13},{1... | collective-permute-start | bytes 368648 | tf_op jit(solution)/shard_map/ppermute | solution.py:69
  12.1 1.3 %collective-permute-start.7 = (bf16[2,8,30,128]{3,2,1,0:T(8,128)(2,1)S(1)}, bf16[2,8,30,128]{3,2,1,0:T(8,128)(2,1)S(1)}, u32[]{:S(2)}, u32[]{:S(2)}) collective-permute-start(bf16[2,8,30,128]{3,2,1,0:T(8,128)(2,1)S(1)} %get-tuple-element.40), channel_id=1, source_target_pairs={{4,0},{5,1},{6,2},{7,3},{8,4},{9,5},{10,6},{11,7},{12,8},{13,9},{1... | collective-permute-start | bytes 368648 | tf_op jit(solution)/shard_map/ppermute | solution.py:69
  13.4 0.0 copy-done
  13.5 0.1 reshape.45
  13.7 0.1 stack.81.pos_ref
  13.8 0.0 collective-permute-done.1
  13.8 0.0 collective-permute-done
  13.8 0.0 collective-permute-done.2
  13.8 5.0 %collective-permute-start.3 = (bf16[2,2,3,16,512]{4,3,2,1,0:T(8,128)(2,1)S(1)}, bf16[2,2,3,16,512]{4,3,2,1,0:T(8,128)(2,1)S(1)}, u32[]{:S(2)}, u32[]{:S(2)}) collective-permute-start(bf16[2,2,3,16,512]{4,3,2,1,0:T(8,128)(2,1)S(1)} %bitcast.54), channel_id=1, source_target_pairs={{0,3},{1,0},{2,1},{3,2},{4,7},{5,4},{6,5},{7,6},{8,11},{9,8},{10,9... | collective-permute-start | bytes 589832 | tf_op jit(solution)/shard_map/ppermute | solution.py:69
  18.8 0.3 collective-permute-start.4
  19.1 0.7 collective-permute-start.5
  19.8 0.1 fusion.8
  20.0 0.4 pad_dynamic-slice_fusion
  20.4 0.1 copy.19
  20.5 0.1 copy.22
  20.6 0.1 add_add_fusion.2
  20.6 0.0 collective-permute-done.6.above
  20.6 1.2 %collective-permute-start.10 = (bf16[2560,128]{1,0:T(8,128)(2,1)S(1)}, bf16[2560,128]{1,0:T(8,128)(2,1)S(1)}, u32[]{:S(2)}, u32[]{:S(2)}) collective-permute-start(bf16[2560,128]{1,0:T(8,128)(2,1)S(1)} %bitcast.48), channel_id=1, source_target_pairs={{0,32},{1,33},{2,34},{3,35},{4,36},{5,37},{6,38},{7,39},{8,40},{9,... | collective-permute-start | bytes 1966088 | tf_op jit(solution)/shard_map/ppermute | solution.py:69
  21.9 0.0 collective-permute-done.7.below
  21.9 2.5 %collective-permute-start.11 = (bf16[2560,128]{1,0:T(8,128)(2,1)S(1)}, bf16[2560,128]{1,0:T(8,128)(2,1)S(1)}, u32[]{:S(2)}, u32[]{:S(2)}) collective-permute-start(bf16[2560,128]{1,0:T(8,128)(2,1)S(1)} %bitcast.59), channel_id=1, source_target_pairs={{0,64},{1,65},{2,66},{3,67},{4,68},{5,69},{6,70},{7,71},{8,72},{9,... | collective-permute-start | bytes 1966088 | tf_op jit(solution)/shard_map/ppermute | solution.py:69
  24.5 0.0 collective-permute-done.3
  24.6 3.9 %collective-permute-start.8 = (bf16[2,8,10,128]{3,2,1,0:T(8,128)(2,1)S(1)}, bf16[2,8,10,128]{3,2,1,0:T(8,128)(2,1)S(1)}, u32[]{:S(2)}, u32[]{:S(2)}) collective-permute-start(bf16[2,8,10,128]{3,2,1,0:T(8,128)(2,1)S(1)} %pad_maximum_fusion.5), channel_id=1, source_target_pairs={{0,1},{1,2},{2,3},{4,5},{5,6},{6,7},{8,9},{9,10},{10,11},{12,13},{... | collective-permute-start | bytes 122888 | tf_op jit(solution)/shard_map/ppermute | solution.py:69
  28.4 0.0 collective-permute-done.4
  28.4 1.3 %collective-permute-start.9 = (bf16[2,8,10,128]{3,2,1,0:T(8,128)(2,1)S(1)}, bf16[2,8,10,128]{3,2,1,0:T(8,128)(2,1)S(1)}, u32[]{:S(2)}, u32[]{:S(2)}) collective-permute-start(bf16[2,8,10,128]{3,2,1,0:T(8,128)(2,1)S(1)} %pad_maximum_fusion.6), channel_id=1, source_target_pairs={{1,0},{2,1},{3,2},{5,4},{6,5},{7,6},{9,8},{10,9},{11,10},{13,12},{... | collective-permute-start | bytes 122888 | tf_op jit(solution)/shard_map/ppermute | solution.py:69
  29.7 0.0 collective-permute-done.5
  29.7 1.1 %pad_maximum_fusion.p0 = bf16[4,2,2,3,16,512]{5,4,3,2,1,0:T(8,128)(2,1)S(1)} fusion(bf16[1,2,2,3,16,512]{5,4,3,2,1,0:T(8,128)(2,1)} %bitcast.21, bf16[1,2,2,3,16,512]{5,4,3,2,1,0:T(8,128)(2,1)} %bitcast.20, bf16[1,2,2,3,16,512]{5,4,3,2,1,0:T(8,128)(2,1)S(1)} %bitcast.67, bf16[1,2,2,3,16,512]{5,4,3,2,1,0:T(8,128)(2,1)S(1)} %bitcast.57), kind=kLoop, calls=%fused_computation.6 | loop fusion | flops 1179648 | bytes 1572864 | tf_op jit(solution)/shard_map/stack | solution.py:349
  30.9 0.0 copy-start.1
  30.9 0.0 collective-permute-done.8.left
  30.9 2.8 %collective-permute-done.9.right = bf16[2,8,10,128]{3,2,1,0:T(8,128)(2,1)S(1)} collective-permute-done((bf16[2,8,10,128]{3,2,1,0:T(8,128)(2,1)S(1)}, bf16[2,8,10,128]{3,2,1,0:T(8,128)(2,1)S(1)}, u32[]{:S(2)}, u32[]{:S(2)}) %collective-permute-start.9) | collective-permute-done | bytes 40992 | tf_op jit(solution)/shard_map/ppermute | solution.py:69
  33.7 0.0 collective-permute-done.10.m1
  33.7 2.0 %collective-permute-start.13 = (bf16[4,2,2,3,16,512]{5,4,3,2,1,0:T(8,128)(2,1)S(1)}, bf16[4,2,2,3,16,512]{5,4,3,2,1,0:T(8,128)(2,1)S(1)}, u32[]{:S(2)}, u32[]{:S(2)}) collective-permute-start(bf16[4,2,2,3,16,512]{5,4,3,2,1,0:T(8,128)(2,1)S(1)} %pad_maximum_fusion.p0), channel_id=1, source_target_pairs={{0,16},{1,17},{2,18},{3,19},{4,20},{5,21},{6,22},{7,23},{8,24},{9,... | collective-permute-start | bytes 2359304 | tf_op jit(solution)/shard_map/ppermute | solution.py:69
  35.8 0.8 pack_rims.1
  36.6 2.4 %collective-permute-start.12 = (bf16[800,128]{1,0:T(8,128)(2,1)S(1)}, bf16[800,128]{1,0:T(8,128)(2,1)S(1)}, u32[]{:S(2)}, u32[]{:S(2)}) collective-permute-start(bf16[800,128]{1,0:T(8,128)(2,1)S(1)} %get-tuple-element.23), channel_id=1, source_target_pairs={{0,64},{1,65},{2,66},{3,67},{4,68},{5,69},{6,70},{7,71},{8,72},{9,... | collective-permute-start | bytes 614408 | tf_op jit(solution)/shard_map/ppermute | solution.py:69
  39.0 0.7 collective-permute-start.17
  39.8 0.7 collective-permute-start.18
  40.5 0.0 collective-permute-done.11.m2
  40.5 2.6 %collective-permute-done.12.r2 = bf16[800,128]{1,0:T(8,128)(2,1)S(1)} collective-permute-done((bf16[800,128]{1,0:T(8,128)(2,1)S(1)}, bf16[800,128]{1,0:T(8,128)(2,1)S(1)}, u32[]{:S(2)}, u32[]{:S(2)}) %collective-permute-start.12) | collective-permute-done | bytes 204832 | tf_op jit(solution)/shard_map/ppermute | solution.py:69
  43.1 3.3 %collective-permute-done.13.p2 = bf16[4,2,2,3,16,512]{5,4,3,2,1,0:T(8,128)(2,1)S(1)} collective-permute-done((bf16[4,2,2,3,16,512]{5,4,3,2,1,0:T(8,128)(2,1)S(1)}, bf16[4,2,2,3,16,512]{5,4,3,2,1,0:T(8,128)(2,1)S(1)}, u32[]{:S(2)}, u32[]{:S(2)}) %collective-permute-start.13) | collective-permute-done | bytes 786464 | tf_op jit(solution)/shard_map/ppermute | solution.py:69
  46.4 4.4 %collective-permute-start.14 = (bf16[2560,128]{1,0:T(8,128)(2,1)S(1)}, bf16[2560,128]{1,0:T(8,128)(2,1)S(1)}, u32[]{:S(2)}, u32[]{:S(2)}) collective-permute-start(bf16[2560,128]{1,0:T(8,128)(2,1)S(1)} %collective-permute-done.11.m2), channel_id=1, source_target_pairs={{0,32},{1,33},{2,34},{3,35},{4,36},{5,37},{6,38},{7,39},{8,40},{9,... | collective-permute-start | bytes 1966088 | tf_op jit(solution)/shard_map/ppermute | solution.py:69
  50.9 0.1 collective-permute-start.15
  51.0 0.5 collective-permute-start.16
  51.5 0.0 copy-done.1
  51.5 0.1 broadcast_multiply_fusion.k_ref
  51.6 1.2 %collective-permute-done.15.r1 = bf16[800,128]{1,0:T(8,128)(2,1)S(1)} collective-permute-done((bf16[800,128]{1,0:T(8,128)(2,1)S(1)}, bf16[800,128]{1,0:T(8,128)(2,1)S(1)}, u32[]{:S(2)}, u32[]{:S(2)}) %collective-permute-start.15) | collective-permute-done | bytes 204832 | tf_op jit(solution)/shard_map/ppermute | solution.py:69
  52.8 0.3 collective-permute-done.16.r3
  53.1 0.0 collective-permute-done.14.m3
  53.1 1.7 %pack_cells.1.x_ref = bf16[4,2,1600,128]{3,2,1,0:T(8,128)(2,1)S(1)} custom-call(s32[5]{0:T(128)S(1)} %stack.81.pos_ref, bf16[2560,128]{1,0:T(8,128)(2,1)S(1)} %bitcast.49, bf16[2560,128]{1,0:T(8,128)(2,1)S(1)} %collective-permute-done.10.m1, bf16[2560,128]{1,0:T(8,128)(2,1)S(1)} %collective-permute-done.11.m2, ...), custom_call_target="tpu_custom_call" | custom-call | tf_op jit(solution)/shard_map/pack_cells/pallas_call | solution.py:166
  54.8 0.0 collective-permute-done.17.p1
  54.8 0.0 collective-permute-done.18.p3
  54.8 32.7 %gated_block.1 = (f32[2,2,8,32,512]{4,3,2,1,0:T(8,128)S(1)}, bf16[2,2,8,32,512]{4,3,2,1,0:T(8,128)(2,1)S(1)}) custom-call(s32[5]{0:T(128)S(1)} %stack.81.pos_ref, bf16[4,2,1600,128]{3,2,1,0:T(8,128)(2,1)S(1)} %pack_cells.1.x_ref, bf16[4,2,2,3,16,512]{5,4,3,2,1,0:T(8,128)(2,1)S(1)} %pad_maximum_fusion.p0, ...), custom_call_target="tpu_custom_call" | custom-call | tf_op jit(solution)/shard_map/gated_block/pallas_call | solution.py:298
  87.6 5.1 %collective-permute-start.19 = (bf16[2,2,8,32,512]{4,3,2,1,0:T(8,128)(2,1)S(1)}, bf16[2,2,8,32,512]{4,3,2,1,0:T(8,128)(2,1)S(1)}, u32[]{:S(2)}, u32[]{:S(2)}) collective-permute-start(bf16[2,2,8,32,512]{4,3,2,1,0:T(8,128)(2,1)S(1)} %get-tuple-element.30), channel_id=1, source_target_pairs={{0,32},{1,33},{2,34},{3,35},{4,36},{5,37},{6,38},{7,39},{8,40},{9,... | collective-permute-start | bytes 3145736 | tf_op jit(solution)/shard_map/ppermute | solution.py:69
  92.6 2.3 %collective-permute-done.19 = bf16[2,2,8,32,512]{4,3,2,1,0:T(8,128)(2,1)S(1)} collective-permute-done((bf16[2,2,8,32,512]{4,3,2,1,0:T(8,128)(2,1)S(1)}, bf16[2,2,8,32,512]{4,3,2,1,0:T(8,128)(2,1)S(1)}, u32[]{:S(2)}, u32[]{:S(2)}) %collective-permute-start.19) | collective-permute-done | bytes 1048608 | tf_op jit(solution)/shard_map/ppermute | solution.py:69
  94.9 0.4 fusion.1
  95.4 1.5 %copy.23 = bf16[2,2,1,8,30,512]{5,3,4,2,1,0:T(8,128)(2,1)} copy(bf16[2,2,1,8,30,512]{5,4,3,1,0,2:T(8,128)(2,1)S(1)} %fusion.1) | data formatting | bytes 1966080 | tf_op jit(solution)/shard_map/convert_element_type | solution.py:364
  (23 shorter events, 0.5 us)
Async XLA Ops:
  0.0 13.4 %copy-start = (f32[3,3,3,2,512]{4,3,2,1,0:T(2,128)S(1)}, f32[3,3,3,2,512]{4,3,2,1,0:T(2,128)}, u32[]{:S(2)}) copy-start(f32[3,3,3,2,512]{4,3,2,1,0:T(2,128)} %param.7) | copy-start | bytes 331780
  1.5 12.2 %collective-permute-start = (bf16[3,16,512]{2,1,0:T(8,128)(2,1)S(1)}, bf16[3,16,512]{2,1,0:T(8,128)(2,1)S(1)}, u32[]{:S(2)}, u32[]{:S(2)}) collective-permute-start(bf16[3,16,512]{2,1,0:T(8,128)(2,1)S(1)} %get-tuple-element.54), channel_id=1, source_target_pairs={{0,4},{1,5},{2,6},{3,7},{4,0},{5,1},{6,2},{7,3},{8,12},{9,13},{10,... | collective-permute-start | bytes 147464 | tf_op jit(solution)/shard_map/ppermute | solution.py:69
  3.7 10.1 %collective-permute-start.2 = (bf16[3,16,512]{2,1,0:T(8,128)(2,1)S(1)}, bf16[3,16,512]{2,1,0:T(8,128)(2,1)S(1)}, u32[]{:S(2)}, u32[]{:S(2)}) collective-permute-start(bf16[3,16,512]{2,1,0:T(8,128)(2,1)S(1)} %get-tuple-element.54), channel_id=1, source_target_pairs={{0,68},{1,69},{2,70},{3,71},{4,64},{5,65},{6,66},{7,67},{8,76},{9,... | collective-permute-start | bytes 147464 | tf_op jit(solution)/shard_map/ppermute | solution.py:69
  6.6 7.2 %collective-permute-start.1 = (bf16[102,512]{1,0:T(8,128)(2,1)S(1)}, bf16[102,512]{1,0:T(8,128)(2,1)S(1)}, u32[]{:S(2)}, u32[]{:S(2)}) collective-permute-start(bf16[102,512]{1,0:T(8,128)(2,1)S(1)} %pad_maximum_fusion.3), channel_id=1, source_target_pairs={{0,64},{1,65},{2,66},{3,67},{4,68},{5,69},{6,70},{7,71},{8,72},{9,... | collective-permute-start | bytes 313352 | tf_op jit(solution)/shard_map/ppermute | solution.py:69
  9.4 11.3 %collective-permute-start.6 = (bf16[2,8,30,128]{3,2,1,0:T(8,128)(2,1)}, bf16[2,8,30,128]{3,2,1,0:T(8,128)(2,1)S(1)}, u32[]{:S(2)}, u32[]{:S(2)}) collective-permute-start(bf16[2,8,30,128]{3,2,1,0:T(8,128)(2,1)} %get-tuple-element.39), channel_id=1, source_target_pairs={{0,4},{1,5},{2,6},{3,7},{4,8},{5,9},{6,10},{7,11},{8,12},{9,13},{1... | collective-permute-start | bytes 368648 | tf_op jit(solution)/shard_map/ppermute | solution.py:69
  12.1 9.8 %collective-permute-start.7 = (bf16[2,8,30,128]{3,2,1,0:T(8,128)(2,1)S(1)}, bf16[2,8,30,128]{3,2,1,0:T(8,128)(2,1)S(1)}, u32[]{:S(2)}, u32[]{:S(2)}) collective-permute-start(bf16[2,8,30,128]{3,2,1,0:T(8,128)(2,1)S(1)} %get-tuple-element.40), channel_id=1, source_target_pairs={{4,0},{5,1},{6,2},{7,3},{8,4},{9,5},{10,6},{11,7},{12,8},{13,9},{1... | collective-permute-start | bytes 368648 | tf_op jit(solution)/shard_map/ppermute | solution.py:69
  13.8 10.7 %collective-permute-start.3 = (bf16[2,2,3,16,512]{4,3,2,1,0:T(8,128)(2,1)S(1)}, bf16[2,2,3,16,512]{4,3,2,1,0:T(8,128)(2,1)S(1)}, u32[]{:S(2)}, u32[]{:S(2)}) collective-permute-start(bf16[2,2,3,16,512]{4,3,2,1,0:T(8,128)(2,1)S(1)} %bitcast.54), channel_id=1, source_target_pairs={{0,3},{1,0},{2,1},{3,2},{4,7},{5,4},{6,5},{7,6},{8,11},{9,8},{10,9... | collective-permute-start | bytes 589832 | tf_op jit(solution)/shard_map/ppermute | solution.py:69
  18.8 9.6 %collective-permute-start.4 = (bf16[2,2,3,16,512]{4,3,2,1,0:T(8,128)(2,1)S(1)}, bf16[2,2,3,16,512]{4,3,2,1,0:T(8,128)(2,1)}, u32[]{:S(2)}, u32[]{:S(2)}) collective-permute-start(bf16[2,2,3,16,512]{4,3,2,1,0:T(8,128)(2,1)S(1)} %bitcast.55), channel_id=1, source_target_pairs={{0,2},{1,3},{2,0},{3,1},{4,6},{5,7},{6,4},{7,5},{8,10},{9,11},{10,... | collective-permute-start | bytes 589832 | tf_op jit(solution)/shard_map/ppermute | solution.py:69
  19.1 10.6 %collective-permute-start.5 = (bf16[2,2,3,16,512]{4,3,2,1,0:T(8,128)(2,1)S(1)}, bf16[2,2,3,16,512]{4,3,2,1,0:T(8,128)(2,1)}, u32[]{:S(2)}, u32[]{:S(2)}) collective-permute-start(bf16[2,2,3,16,512]{4,3,2,1,0:T(8,128)(2,1)S(1)} %bitcast.56), channel_id=1, source_target_pairs={{0,1},{1,2},{2,3},{3,0},{4,5},{5,6},{6,7},{7,4},{8,9},{9,10},{10,1... | collective-permute-start | bytes 589832 | tf_op jit(solution)/shard_map/ppermute | solution.py:69
  20.6 13.1 %collective-permute-start.10 = (bf16[2560,128]{1,0:T(8,128)(2,1)S(1)}, bf16[2560,128]{1,0:T(8,128)(2,1)S(1)}, u32[]{:S(2)}, u32[]{:S(2)}) collective-permute-start(bf16[2560,128]{1,0:T(8,128)(2,1)S(1)} %bitcast.48), channel_id=1, source_target_pairs={{0,32},{1,33},{2,34},{3,35},{4,36},{5,37},{6,38},{7,39},{8,40},{9,... | collective-permute-start | bytes 1966088 | tf_op jit(solution)/shard_map/ppermute | solution.py:69
  21.9 18.6 %collective-permute-start.11 = (bf16[2560,128]{1,0:T(8,128)(2,1)S(1)}, bf16[2560,128]{1,0:T(8,128)(2,1)S(1)}, u32[]{:S(2)}, u32[]{:S(2)}) collective-permute-start(bf16[2560,128]{1,0:T(8,128)(2,1)S(1)} %bitcast.59), channel_id=1, source_target_pairs={{0,64},{1,65},{2,66},{3,67},{4,68},{5,69},{6,70},{7,71},{8,72},{9,... | collective-permute-start | bytes 1966088 | tf_op jit(solution)/shard_map/ppermute | solution.py:69
  24.6 6.3 %collective-permute-start.8 = (bf16[2,8,10,128]{3,2,1,0:T(8,128)(2,1)S(1)}, bf16[2,8,10,128]{3,2,1,0:T(8,128)(2,1)S(1)}, u32[]{:S(2)}, u32[]{:S(2)}) collective-permute-start(bf16[2,8,10,128]{3,2,1,0:T(8,128)(2,1)S(1)} %pad_maximum_fusion.5), channel_id=1, source_target_pairs={{0,1},{1,2},{2,3},{4,5},{5,6},{6,7},{8,9},{9,10},{10,11},{12,13},{... | collective-permute-start | bytes 122888 | tf_op jit(solution)/shard_map/ppermute | solution.py:69
  28.4 5.3 %collective-permute-start.9 = (bf16[2,8,10,128]{3,2,1,0:T(8,128)(2,1)S(1)}, bf16[2,8,10,128]{3,2,1,0:T(8,128)(2,1)S(1)}, u32[]{:S(2)}, u32[]{:S(2)}) collective-permute-start(bf16[2,8,10,128]{3,2,1,0:T(8,128)(2,1)S(1)} %pad_maximum_fusion.6), channel_id=1, source_target_pairs={{1,0},{2,1},{3,2},{5,4},{6,5},{7,6},{9,8},{10,9},{11,10},{13,12},{... | collective-permute-start | bytes 122888 | tf_op jit(solution)/shard_map/ppermute | solution.py:69
  30.9 20.6 %copy-start.1 = (f32[2]{0:T(128)S(1)}, f32[2]{0:T(128)}, u32[]{:S(2)}) copy-start(f32[2]{0:T(128)} %constant.91.clone) | copy-start | bytes 28
  33.7 12.7 %collective-permute-start.13 = (bf16[4,2,2,3,16,512]{5,4,3,2,1,0:T(8,128)(2,1)S(1)}, bf16[4,2,2,3,16,512]{5,4,3,2,1,0:T(8,128)(2,1)S(1)}, u32[]{:S(2)}, u32[]{:S(2)}) collective-permute-start(bf16[4,2,2,3,16,512]{5,4,3,2,1,0:T(8,128)(2,1)S(1)} %pad_maximum_fusion.p0), channel_id=1, source_target_pairs={{0,16},{1,17},{2,18},{3,19},{4,20},{5,21},{6,22},{7,23},{8,24},{9,... | collective-permute-start | bytes 2359304 | tf_op jit(solution)/shard_map/ppermute | solution.py:69
  36.6 6.5 %collective-permute-start.12 = (bf16[800,128]{1,0:T(8,128)(2,1)S(1)}, bf16[800,128]{1,0:T(8,128)(2,1)S(1)}, u32[]{:S(2)}, u32[]{:S(2)}) collective-permute-start(bf16[800,128]{1,0:T(8,128)(2,1)S(1)} %get-tuple-element.23), channel_id=1, source_target_pairs={{0,64},{1,65},{2,66},{3,67},{4,68},{5,69},{6,70},{7,71},{8,72},{9,... | collective-permute-start | bytes 614408 | tf_op jit(solution)/shard_map/ppermute | solution.py:69
  39.0 15.7 %collective-permute-start.17 = (bf16[4,2,2,3,16,512]{5,4,3,2,1,0:T(8,128)(2,1)S(1)}, bf16[4,2,2,3,16,512]{5,4,3,2,1,0:T(8,128)(2,1)S(1)}, u32[]{:S(2)}, u32[]{:S(2)}) collective-permute-start(bf16[4,2,2,3,16,512]{5,4,3,2,1,0:T(8,128)(2,1)S(1)} %pad_maximum_fusion.p0), channel_id=1, source_target_pairs={{0,24},{1,25},{2,26},{3,27},{4,28},{5,29},{6,30},{7,31},{8,0},{9,1... | collective-permute-start | bytes 2359304 | tf_op jit(solution)/shard_map/ppermute | solution.py:69
  39.8 15.0 %collective-permute-start.18 = (bf16[4,2,2,3,16,512]{5,4,3,2,1,0:T(8,128)(2,1)S(1)}, bf16[4,2,2,3,16,512]{5,4,3,2,1,0:T(8,128)(2,1)S(1)}, u32[]{:S(2)}, u32[]{:S(2)}) collective-permute-start(bf16[4,2,2,3,16,512]{5,4,3,2,1,0:T(8,128)(2,1)S(1)} %pad_maximum_fusion.p0), channel_id=1, source_target_pairs={{0,8},{1,9},{2,10},{3,11},{4,12},{5,13},{6,14},{7,15},{8,16},{9,17... | collective-permute-start | bytes 2359304 | tf_op jit(solution)/shard_map/ppermute | solution.py:69
  46.4 6.7 %collective-permute-start.14 = (bf16[2560,128]{1,0:T(8,128)(2,1)S(1)}, bf16[2560,128]{1,0:T(8,128)(2,1)S(1)}, u32[]{:S(2)}, u32[]{:S(2)}) collective-permute-start(bf16[2560,128]{1,0:T(8,128)(2,1)S(1)} %collective-permute-done.11.m2), channel_id=1, source_target_pairs={{0,32},{1,33},{2,34},{3,35},{4,36},{5,37},{6,38},{7,39},{8,40},{9,... | collective-permute-start | bytes 1966088 | tf_op jit(solution)/shard_map/ppermute | solution.py:69
  50.9 1.9 %collective-permute-start.15 = (bf16[800,128]{1,0:T(8,128)(2,1)S(1)}, bf16[800,128]{1,0:T(8,128)(2,1)S(1)}, u32[]{:S(2)}, u32[]{:S(2)}) collective-permute-start(bf16[800,128]{1,0:T(8,128)(2,1)S(1)} %get-tuple-element.26.r0), channel_id=1, source_target_pairs={{0,32},{1,33},{2,34},{3,35},{4,36},{5,37},{6,38},{7,39},{8,40},{9,... | collective-permute-start | bytes 614408 | tf_op jit(solution)/shard_map/ppermute | solution.py:69
  51.0 2.1 %collective-permute-start.16 = (bf16[800,128]{1,0:T(8,128)(2,1)S(1)}, bf16[800,128]{1,0:T(8,128)(2,1)S(1)}, u32[]{:S(2)}, u32[]{:S(2)}) collective-permute-start(bf16[800,128]{1,0:T(8,128)(2,1)S(1)} %collective-permute-done.12.r2), channel_id=1, source_target_pairs={{0,32},{1,33},{2,34},{3,35},{4,36},{5,37},{6,38},{7,39},{8,40},{9,... | collective-permute-start | bytes 614408 | tf_op jit(solution)/shard_map/ppermute | solution.py:69
  87.6 7.4 %collective-permute-start.19 = (bf16[2,2,8,32,512]{4,3,2,1,0:T(8,128)(2,1)S(1)}, bf16[2,2,8,32,512]{4,3,2,1,0:T(8,128)(2,1)S(1)}, u32[]{:S(2)}, u32[]{:S(2)}) collective-permute-start(bf16[2,2,8,32,512]{4,3,2,1,0:T(8,128)(2,1)S(1)} %get-tuple-element.30), channel_id=1, source_target_pairs={{0,32},{1,33},{2,34},{3,35},{4,36},{5,37},{6,38},{7,39},{8,40},{9,... | collective-permute-start | bytes 3145736 | tf_op jit(solution)/shard_map/ppermute | solution.py:69

commit v6 on v5

--- a/solution.py
+++ b/solution.py
@@ -191,16 +191,17 @@
     def weights(g, c):
         return w_scr[g, c // 2, :, pl.ds(pl.multiple_of((c % 2) * 256, 256), 256)]
 
-    def expand(s, row, g, t):
+    def expand(s, row, g, t, count=1):
         b, c = s // 4, s % 4
-        at = pl.ds(pl.multiple_of(row * 160, 32), 160)
+        at = pl.ds(pl.multiple_of(row * 160, 32), count * 160)
         cells = jnp.concatenate([x_ref[m, b, at, :] for m in range(4)], axis=1)
         half = jnp.dot(cells, weights(g, c), preferred_element_type=F32)
         half = half * jnp.tanh(half) + half
-        for q in range(2):
-            frames = [half[f * 32:(f + 1) * 32, q * 128:(q + 1) * 128] for f in range(5)]
-            for m, v in enumerate(forward(frames)):
-                t[g * 2 + q, m, row] = v
+        for k in range(count):
+            for q in range(2):
+                frames = [half[(k * 5 + f) * 32:(k * 5 + f + 1) * 32, q * 128:(q + 1) * 128] for f in range(5)]
+                for m, v in enumerate(forward(frames)):
+                    t[g * 2 + q, m, row + k] = v
 
     def filtered(t, group, g, tap, h):
         terms = [[], []]
@@ -234,20 +235,20 @@
 
         lax.fori_loop(0, 2, part, 0)
 
-    def first(row, _):
+    def first(it, _):
         for g in range(2):
-            expand(0, row, g, t0)
-        return 0
-
-    lax.fori_loop(0, 10, first, 0)
+            expand(0, it * 5, g, t0, 5)
+        return 0
+
+    lax.fori_loop(0, 2, first, 0)
 
     def step(s, now, later):
         def half(it, _):
             for r in range(2):
                 gate_rows(now, s % 4, it * 4 + 2 * r)
                 if later is not None:
-                    for u in range(5):
-                        expand(s + 1, it * 5 + u, r, later)
+                    expand(s + 1, it * 5, r, later, 3)
+                    expand(s + 1, it * 5 + 3, r, later, 2)
             return 0
 
         lax.fori_loop(0, 2, half, 0)

time: 97.2 us -> 95.4 us (0.981)
  Pallas kernels: 35.3 us -> 33.5 us
    pallas_call x1, Pallas kernels: 32.7 us -> 31 us  [run_block(): pl.pallas_call(block_kernel, out_shape=[jax.ShapeDtypeStruct((2, 2, 8, 32...]
where the time goes in v6:
time: 95.4 us; the launch traced here: 95.1 us
  starting transfers between devices  39.4 us (41%)
  Pallas kernels  33.5 us (35%)
  waiting for transfers between devices  12.6 us (13%)
  other arithmetic  4.6 us (5%)
  local copies, waits for them, and re-layouts  4.55 us (5%)
    ppermute x20, starting transfers between devices, send(): return lax.ppermute(value, BOTH, pairs)  39.4 us
    pallas_call x1, Pallas kernels, run_block(): pl.pallas_call(block_kernel, out_shape=[jax.ShapeDtypeStruct((2, 2, 8, 32...  31 us
    ppermute x20, waiting for transfers between devices, send(): return lax.ppermute(value, BOTH, pairs)  12.6 us
  transfers between devices with their start and end apart: 20, of which 6 were waited for; matrix products, arithmetic and copies ran while one was open for 6% of the time, Pallas kernels for 3%

profile of v6, /device:TPU:1, one launch (start us, length us, event | category | flops | bytes accessed | tf_op | source)
XLA Modules:
  0.0 95.1 jit_solution(13268407892978099652)
XLA Ops:
  0.0 0.0 copy-start
  0.0 0.8 copy_multiply_fusion
  0.8 0.7 fusion.5
  1.5 2.1 %collective-permute-start = (bf16[3,16,512]{2,1,0:T(8,128)(2,1)S(1)}, bf16[3,16,512]{2,1,0:T(8,128)(2,1)S(1)}, u32[]{:S(2)}, u32[]{:S(2)}) collective-permute-start(bf16[3,16,512]{2,1,0:T(8,128)(2,1)S(1)} %get-tuple-element.54), channel_id=1, source_target_pairs={{0,4},{1,5},{2,6},{3,7},{4,0},{5,1},{6,2},{7,3},{8,12},{9,13},{10,... | collective-permute-start | bytes 147464 | tf_op jit(solution)/shard_map/ppermute | solution.py:69
  3.7 1.8 %collective-permute-start.2 = (bf16[3,16,512]{2,1,0:T(8,128)(2,1)S(1)}, bf16[3,16,512]{2,1,0:T(8,128)(2,1)S(1)}, u32[]{:S(2)}, u32[]{:S(2)}) collective-permute-start(bf16[3,16,512]{2,1,0:T(8,128)(2,1)S(1)} %get-tuple-element.54), channel_id=1, source_target_pairs={{0,68},{1,69},{2,70},{3,71},{4,64},{5,65},{6,66},{7,67},{8,76},{9,... | collective-permute-start | bytes 147464 | tf_op jit(solution)/shard_map/ppermute | solution.py:69
  5.5 1.0 %fusion.2 = bf16[3,9,2,512]{3,2,1,0:T(2,128)(2,1)S(1)} fusion(f32[3,9,2,512]{3,2,1,0:T(2,128)} %bitcast.60, pred[]{:T(512)S(6)} %eq.8), kind=kLoop, calls=%fused_computation.20 | loop fusion | flops 27648 | bytes 165889 | tf_op jit(solution)/shard_map/convert_element_type | solution.py:329
  6.6 0.7 collective-permute-start.1
  7.3 1.4 %copy.28 = bf16[2,8,1,8,30,128]{5,4,1,0,3,2:T(8,128)(2,1)S(1)} copy(bf16[2,8,1,8,30,128]{5,3,4,2,1,0:T(8,128)(2,1)} %param.5) | data formatting | bytes 1966080 | tf_op args[0]
  8.7 0.7 slice_bitcast_fusion.1
  9.4 2.7 %collective-permute-start.6 = (bf16[2,8,30,128]{3,2,1,0:T(8,128)(2,1)}, bf16[2,8,30,128]{3,2,1,0:T(8,128)(2,1)S(1)}, u32[]{:S(2)}, u32[]{:S(2)}) collective-permute-start(bf16[2,8,30,128]{3,2,1,0:T(8,128)(2,1)} %get-tuple-element.39), channel_id=1, source_target_pairs={{0,4},{1,5},{2,6},{3,7},{4,8},{5,9},{6,10},{7,11},{8,12},{9,13},{1... | collective-permute-start | bytes 368648 | tf_op jit(solution)/shard_map/ppermute | solution.py:69
  12.1 1.3 %collective-permute-start.7 = (bf16[2,8,30,128]{3,2,1,0:T(8,128)(2,1)S(1)}, bf16[2,8,30,128]{3,2,1,0:T(8,128)(2,1)S(1)}, u32[]{:S(2)}, u32[]{:S(2)}) collective-permute-start(bf16[2,8,30,128]{3,2,1,0:T(8,128)(2,1)S(1)} %get-tuple-element.40), channel_id=1, source_target_pairs={{4,0},{5,1},{6,2},{7,3},{8,4},{9,5},{10,6},{11,7},{12,8},{13,9},{1... | collective-permute-start | bytes 368648 | tf_op jit(solution)/shard_map/ppermute | solution.py:69
  13.4 0.0 copy-done
  13.5 0.1 reshape.45
  13.7 0.1 stack.81.pos_ref
  13.8 0.0 collective-permute-done.1
  13.8 0.0 collective-permute-done
  13.8 0.0 collective-permute-done.2
  13.8 5.0 %collective-permute-start.3 = (bf16[2,2,3,16,512]{4,3,2,1,0:T(8,128)(2,1)S(1)}, bf16[2,2,3,16,512]{4,3,2,1,0:T(8,128)(2,1)S(1)}, u32[]{:S(2)}, u32[]{:S(2)}) collective-permute-start(bf16[2,2,3,16,512]{4,3,2,1,0:T(8,128)(2,1)S(1)} %bitcast.54), channel_id=1, source_target_pairs={{0,3},{1,0},{2,1},{3,2},{4,7},{5,4},{6,5},{7,6},{8,11},{9,8},{10,9... | collective-permute-start | bytes 589832 | tf_op jit(solution)/shard_map/ppermute | solution.py:69
  18.8 0.3 collective-permute-start.4
  19.1 0.7 collective-permute-start.5
  19.8 0.1 fusion.8
  20.0 0.4 pad_dynamic-slice_fusion
  20.4 0.1 copy.19
  20.5 0.1 copy.22
  20.6 0.1 add_add_fusion.2
  20.6 0.0 collective-permute-done.6.above
  20.6 1.2 %collective-permute-start.10 = (bf16[2560,128]{1,0:T(8,128)(2,1)S(1)}, bf16[2560,128]{1,0:T(8,128)(2,1)S(1)}, u32[]{:S(2)}, u32[]{:S(2)}) collective-permute-start(bf16[2560,128]{1,0:T(8,128)(2,1)S(1)} %bitcast.48), channel_id=1, source_target_pairs={{0,32},{1,33},{2,34},{3,35},{4,36},{5,37},{6,38},{7,39},{8,40},{9,... | collective-permute-start | bytes 1966088 | tf_op jit(solution)/shard_map/ppermute | solution.py:69
  21.9 0.0 collective-permute-done.7.below
  21.9 2.5 %collective-permute-start.11 = (bf16[2560,128]{1,0:T(8,128)(2,1)S(1)}, bf16[2560,128]{1,0:T(8,128)(2,1)S(1)}, u32[]{:S(2)}, u32[]{:S(2)}) collective-permute-start(bf16[2560,128]{1,0:T(8,128)(2,1)S(1)} %bitcast.59), channel_id=1, source_target_pairs={{0,64},{1,65},{2,66},{3,67},{4,68},{5,69},{6,70},{7,71},{8,72},{9,... | collective-permute-start | bytes 1966088 | tf_op jit(solution)/shard_map/ppermute | solution.py:69
  24.5 0.0 collective-permute-done.3
  24.6 3.9 %collective-permute-start.8 = (bf16[2,8,10,128]{3,2,1,0:T(8,128)(2,1)S(1)}, bf16[2,8,10,128]{3,2,1,0:T(8,128)(2,1)S(1)}, u32[]{:S(2)}, u32[]{:S(2)}) collective-permute-start(bf16[2,8,10,128]{3,2,1,0:T(8,128)(2,1)S(1)} %pad_maximum_fusion.5), channel_id=1, source_target_pairs={{0,1},{1,2},{2,3},{4,5},{5,6},{6,7},{8,9},{9,10},{10,11},{12,13},{... | collective-permute-start | bytes 122888 | tf_op jit(solution)/shard_map/ppermute | solution.py:69
  28.4 0.0 collective-permute-done.4
  28.4 1.3 %collective-permute-start.9 = (bf16[2,8,10,128]{3,2,1,0:T(8,128)(2,1)S(1)}, bf16[2,8,10,128]{3,2,1,0:T(8,128)(2,1)S(1)}, u32[]{:S(2)}, u32[]{:S(2)}) collective-permute-start(bf16[2,8,10,128]{3,2,1,0:T(8,128)(2,1)S(1)} %pad_maximum_fusion.6), channel_id=1, source_target_pairs={{1,0},{2,1},{3,2},{5,4},{6,5},{7,6},{9,8},{10,9},{11,10},{13,12},{... | collective-permute-start | bytes 122888 | tf_op jit(solution)/shard_map/ppermute | solution.py:69
  29.7 0.0 collective-permute-done.5
  29.7 1.1 %pad_maximum_fusion.p0 = bf16[4,2,2,3,16,512]{5,4,3,2,1,0:T(8,128)(2,1)S(1)} fusion(bf16[1,2,2,3,16,512]{5,4,3,2,1,0:T(8,128)(2,1)} %bitcast.21, bf16[1,2,2,3,16,512]{5,4,3,2,1,0:T(8,128)(2,1)} %bitcast.20, bf16[1,2,2,3,16,512]{5,4,3,2,1,0:T(8,128)(2,1)S(1)} %bitcast.67, bf16[1,2,2,3,16,512]{5,4,3,2,1,0:T(8,128)(2,1)S(1)} %bitcast.57), kind=kLoop, calls=%fused_computation.6 | loop fusion | flops 1179648 | bytes 1572864 | tf_op jit(solution)/shard_map/stack | solution.py:350
  30.9 0.0 copy-start.1
  30.9 0.0 collective-permute-done.8.left
  30.9 2.8 %collective-permute-done.9.right = bf16[2,8,10,128]{3,2,1,0:T(8,128)(2,1)S(1)} collective-permute-done((bf16[2,8,10,128]{3,2,1,0:T(8,128)(2,1)S(1)}, bf16[2,8,10,128]{3,2,1,0:T(8,128)(2,1)S(1)}, u32[]{:S(2)}, u32[]{:S(2)}) %collective-permute-start.9) | collective-permute-done | bytes 40992 | tf_op jit(solution)/shard_map/ppermute | solution.py:69
  33.7 0.0 collective-permute-done.10.m1
  33.7 2.0 %collective-permute-start.13 = (bf16[4,2,2,3,16,512]{5,4,3,2,1,0:T(8,128)(2,1)S(1)}, bf16[4,2,2,3,16,512]{5,4,3,2,1,0:T(8,128)(2,1)S(1)}, u32[]{:S(2)}, u32[]{:S(2)}) collective-permute-start(bf16[4,2,2,3,16,512]{5,4,3,2,1,0:T(8,128)(2,1)S(1)} %pad_maximum_fusion.p0), channel_id=1, source_target_pairs={{0,16},{1,17},{2,18},{3,19},{4,20},{5,21},{6,22},{7,23},{8,24},{9,... | collective-permute-start | bytes 2359304 | tf_op jit(solution)/shard_map/ppermute | solution.py:69
  35.8 0.8 pack_rims.1
  36.6 2.4 %collective-permute-start.12 = (bf16[800,128]{1,0:T(8,128)(2,1)S(1)}, bf16[800,128]{1,0:T(8,128)(2,1)S(1)}, u32[]{:S(2)}, u32[]{:S(2)}) collective-permute-start(bf16[800,128]{1,0:T(8,128)(2,1)S(1)} %get-tuple-element.23), channel_id=1, source_target_pairs={{0,64},{1,65},{2,66},{3,67},{4,68},{5,69},{6,70},{7,71},{8,72},{9,... | collective-permute-start | bytes 614408 | tf_op jit(solution)/shard_map/ppermute | solution.py:69
  39.0 0.7 collective-permute-start.17
  39.8 0.7 collective-permute-start.18
  40.5 0.0 collective-permute-done.11.m2
  40.5 2.6 %collective-permute-done.12.r2 = bf16[800,128]{1,0:T(8,128)(2,1)S(1)} collective-permute-done((bf16[800,128]{1,0:T(8,128)(2,1)S(1)}, bf16[800,128]{1,0:T(8,128)(2,1)S(1)}, u32[]{:S(2)}, u32[]{:S(2)}) %collective-permute-start.12) | collective-permute-done | bytes 204832 | tf_op jit(solution)/shard_map/ppermute | solution.py:69
  43.1 3.3 %collective-permute-done.13.p2 = bf16[4,2,2,3,16,512]{5,4,3,2,1,0:T(8,128)(2,1)S(1)} collective-permute-done((bf16[4,2,2,3,16,512]{5,4,3,2,1,0:T(8,128)(2,1)S(1)}, bf16[4,2,2,3,16,512]{5,4,3,2,1,0:T(8,128)(2,1)S(1)}, u32[]{:S(2)}, u32[]{:S(2)}) %collective-permute-start.13) | collective-permute-done | bytes 786464 | tf_op jit(solution)/shard_map/ppermute | solution.py:69
  46.4 4.4 %collective-permute-start.14 = (bf16[2560,128]{1,0:T(8,128)(2,1)S(1)}, bf16[2560,128]{1,0:T(8,128)(2,1)S(1)}, u32[]{:S(2)}, u32[]{:S(2)}) collective-permute-start(bf16[2560,128]{1,0:T(8,128)(2,1)S(1)} %collective-permute-done.11.m2), channel_id=1, source_target_pairs={{0,32},{1,33},{2,34},{3,35},{4,36},{5,37},{6,38},{7,39},{8,40},{9,... | collective-permute-start | bytes 1966088 | tf_op jit(solution)/shard_map/ppermute | solution.py:69
  50.9 0.1 collective-permute-start.15
  51.0 0.5 collective-permute-start.16
  51.5 0.0 copy-done.1
  51.5 0.1 broadcast_multiply_fusion.k_ref
  51.6 1.2 %collective-permute-done.15.r1 = bf16[800,128]{1,0:T(8,128)(2,1)S(1)} collective-permute-done((bf16[800,128]{1,0:T(8,128)(2,1)S(1)}, bf16[800,128]{1,0:T(8,128)(2,1)S(1)}, u32[]{:S(2)}, u32[]{:S(2)}) %collective-permute-start.15) | collective-permute-done | bytes 204832 | tf_op jit(solution)/shard_map/ppermute | solution.py:69
  52.8 0.3 collective-permute-done.16.r3
  53.1 0.0 collective-permute-done.14.m3
  53.1 1.7 %pack_cells.1.x_ref = bf16[4,2,1600,128]{3,2,1,0:T(8,128)(2,1)S(1)} custom-call(s32[5]{0:T(128)S(1)} %stack.81.pos_ref, bf16[2560,128]{1,0:T(8,128)(2,1)S(1)} %bitcast.49, bf16[2560,128]{1,0:T(8,128)(2,1)S(1)} %collective-permute-done.10.m1, bf16[2560,128]{1,0:T(8,128)(2,1)S(1)} %collective-permute-done.11.m2, ...), custom_call_target="tpu_custom_call" | custom-call | tf_op jit(solution)/shard_map/pack_cells/pallas_call | solution.py:166
  54.8 0.0 collective-permute-done.17.p1
  54.8 0.0 collective-permute-done.18.p3
  54.8 31.0 %gated_block.1 = (f32[2,2,8,32,512]{4,3,2,1,0:T(8,128)S(1)}, bf16[2,2,8,32,512]{4,3,2,1,0:T(8,128)(2,1)S(1)}) custom-call(s32[5]{0:T(128)S(1)} %stack.81.pos_ref, bf16[4,2,1600,128]{3,2,1,0:T(8,128)(2,1)S(1)} %pack_cells.1.x_ref, bf16[4,2,2,3,16,512]{5,4,3,2,1,0:T(8,128)(2,1)S(1)} %pad_maximum_fusion.p0, ...), custom_call_target="tpu_custom_call" | custom-call | tf_op jit(solution)/shard_map/gated_block/pallas_call | solution.py:299
  85.8 5.1 %collective-permute-start.19 = (bf16[2,2,8,32,512]{4,3,2,1,0:T(8,128)(2,1)S(1)}, bf16[2,2,8,32,512]{4,3,2,1,0:T(8,128)(2,1)S(1)}, u32[]{:S(2)}, u32[]{:S(2)}) collective-permute-start(bf16[2,2,8,32,512]{4,3,2,1,0:T(8,128)(2,1)S(1)} %get-tuple-element.30), channel_id=1, source_target_pairs={{0,32},{1,33},{2,34},{3,35},{4,36},{5,37},{6,38},{7,39},{8,40},{9,... | collective-permute-start | bytes 3145736 | tf_op jit(solution)/shard_map/ppermute | solution.py:69
  90.9 2.3 %collective-permute-done.19 = bf16[2,2,8,32,512]{4,3,2,1,0:T(8,128)(2,1)S(1)} collective-permute-done((bf16[2,2,8,32,512]{4,3,2,1,0:T(8,128)(2,1)S(1)}, bf16[2,2,8,32,512]{4,3,2,1,0:T(8,128)(2,1)S(1)}, u32[]{:S(2)}, u32[]{:S(2)}) %collective-permute-start.19) | collective-permute-done | bytes 1048608 | tf_op jit(solution)/shard_map/ppermute | solution.py:69
  93.2 0.4 fusion.1
  93.6 1.5 %copy.23 = bf16[2,2,1,8,30,512]{5,3,4,2,1,0:T(8,128)(2,1)} copy(bf16[2,2,1,8,30,512]{5,4,3,1,0,2:T(8,128)(2,1)S(1)} %fusion.1) | data formatting | bytes 1966080 | tf_op jit(solution)/shard_map/convert_element_type | solution.py:365
  (23 shorter events, 0.5 us)
Async XLA Ops:
  0.0 13.4 %copy-start = (f32[3,3,3,2,512]{4,3,2,1,0:T(2,128)S(1)}, f32[3,3,3,2,512]{4,3,2,1,0:T(2,128)}, u32[]{:S(2)}) copy-start(f32[3,3,3,2,512]{4,3,2,1,0:T(2,128)} %param.7) | copy-start | bytes 331780
  1.5 12.2 %collective-permute-start = (bf16[3,16,512]{2,1,0:T(8,128)(2,1)S(1)}, bf16[3,16,512]{2,1,0:T(8,128)(2,1)S(1)}, u32[]{:S(2)}, u32[]{:S(2)}) collective-permute-start(bf16[3,16,512]{2,1,0:T(8,128)(2,1)S(1)} %get-tuple-element.54), channel_id=1, source_target_pairs={{0,4},{1,5},{2,6},{3,7},{4,0},{5,1},{6,2},{7,3},{8,12},{9,13},{10,... | collective-permute-start | bytes 147464 | tf_op jit(solution)/shard_map/ppermute | solution.py:69
  3.7 10.1 %collective-permute-start.2 = (bf16[3,16,512]{2,1,0:T(8,128)(2,1)S(1)}, bf16[3,16,512]{2,1,0:T(8,128)(2,1)S(1)}, u32[]{:S(2)}, u32[]{:S(2)}) collective-permute-start(bf16[3,16,512]{2,1,0:T(8,128)(2,1)S(1)} %get-tuple-element.54), channel_id=1, source_target_pairs={{0,68},{1,69},{2,70},{3,71},{4,64},{5,65},{6,66},{7,67},{8,76},{9,... | collective-permute-start | bytes 147464 | tf_op jit(solution)/shard_map/ppermute | solution.py:69
  6.6 7.2 %collective-permute-start.1 = (bf16[102,512]{1,0:T(8,128)(2,1)S(1)}, bf16[102,512]{1,0:T(8,128)(2,1)S(1)}, u32[]{:S(2)}, u32[]{:S(2)}) collective-permute-start(bf16[102,512]{1,0:T(8,128)(2,1)S(1)} %pad_maximum_fusion.3), channel_id=1, source_target_pairs={{0,64},{1,65},{2,66},{3,67},{4,68},{5,69},{6,70},{7,71},{8,72},{9,... | collective-permute-start | bytes 313352 | tf_op jit(solution)/shard_map/ppermute | solution.py:69
  9.4 11.3 %collective-permute-start.6 = (bf16[2,8,30,128]{3,2,1,0:T(8,128)(2,1)}, bf16[2,8,30,128]{3,2,1,0:T(8,128)(2,1)S(1)}, u32[]{:S(2)}, u32[]{:S(2)}) collective-permute-start(bf16[2,8,30,128]{3,2,1,0:T(8,128)(2,1)} %get-tuple-element.39), channel_id=1, source_target_pairs={{0,4},{1,5},{2,6},{3,7},{4,8},{5,9},{6,10},{7,11},{8,12},{9,13},{1... | collective-permute-start | bytes 368648 | tf_op jit(solution)/shard_map/ppermute | solution.py:69
  12.1 9.8 %collective-permute-start.7 = (bf16[2,8,30,128]{3,2,1,0:T(8,128)(2,1)S(1)}, bf16[2,8,30,128]{3,2,1,0:T(8,128)(2,1)S(1)}, u32[]{:S(2)}, u32[]{:S(2)}) collective-permute-start(bf16[2,8,30,128]{3,2,1,0:T(8,128)(2,1)S(1)} %get-tuple-element.40), channel_id=1, source_target_pairs={{4,0},{5,1},{6,2},{7,3},{8,4},{9,5},{10,6},{11,7},{12,8},{13,9},{1... | collective-permute-start | bytes 368648 | tf_op jit(solution)/shard_map/ppermute | solution.py:69
  13.8 10.7 %collective-permute-start.3 = (bf16[2,2,3,16,512]{4,3,2,1,0:T(8,128)(2,1)S(1)}, bf16[2,2,3,16,512]{4,3,2,1,0:T(8,128)(2,1)S(1)}, u32[]{:S(2)}, u32[]{:S(2)}) collective-permute-start(bf16[2,2,3,16,512]{4,3,2,1,0:T(8,128)(2,1)S(1)} %bitcast.54), channel_id=1, source_target_pairs={{0,3},{1,0},{2,1},{3,2},{4,7},{5,4},{6,5},{7,6},{8,11},{9,8},{10,9... | collective-permute-start | bytes 589832 | tf_op jit(solution)/shard_map/ppermute | solution.py:69
  18.8 9.6 %collective-permute-start.4 = (bf16[2,2,3,16,512]{4,3,2,1,0:T(8,128)(2,1)S(1)}, bf16[2,2,3,16,512]{4,3,2,1,0:T(8,128)(2,1)}, u32[]{:S(2)}, u32[]{:S(2)}) collective-permute-start(bf16[2,2,3,16,512]{4,3,2,1,0:T(8,128)(2,1)S(1)} %bitcast.55), channel_id=1, source_target_pairs={{0,2},{1,3},{2,0},{3,1},{4,6},{5,7},{6,4},{7,5},{8,10},{9,11},{10,... | collective-permute-start | bytes 589832 | tf_op jit(solution)/shard_map/ppermute | solution.py:69
  19.1 10.6 %collective-permute-start.5 = (bf16[2,2,3,16,512]{4,3,2,1,0:T(8,128)(2,1)S(1)}, bf16[2,2,3,16,512]{4,3,2,1,0:T(8,128)(2,1)}, u32[]{:S(2)}, u32[]{:S(2)}) collective-permute-start(bf16[2,2,3,16,512]{4,3,2,1,0:T(8,128)(2,1)S(1)} %bitcast.56), channel_id=1, source_target_pairs={{0,1},{1,2},{2,3},{3,0},{4,5},{5,6},{6,7},{7,4},{8,9},{9,10},{10,1... | collective-permute-start | bytes 589832 | tf_op jit(solution)/shard_map/ppermute | solution.py:69
  20.6 13.1 %collective-permute-start.10 = (bf16[2560,128]{1,0:T(8,128)(2,1)S(1)}, bf16[2560,128]{1,0:T(8,128)(2,1)S(1)}, u32[]{:S(2)}, u32[]{:S(2)}) collective-permute-start(bf16[2560,128]{1,0:T(8,128)(2,1)S(1)} %bitcast.48), channel_id=1, source_target_pairs={{0,32},{1,33},{2,34},{3,35},{4,36},{5,37},{6,38},{7,39},{8,40},{9,... | collective-permute-start | bytes 1966088 | tf_op jit(solution)/shard_map/ppermute | solution.py:69
  21.9 18.6 %collective-permute-start.11 = (bf16[2560,128]{1,0:T(8,128)(2,1)S(1)}, bf16[2560,128]{1,0:T(8,128)(2,1)S(1)}, u32[]{:S(2)}, u32[]{:S(2)}) collective-permute-start(bf16[2560,128]{1,0:T(8,128)(2,1)S(1)} %bitcast.59), channel_id=1, source_target_pairs={{0,64},{1,65},{2,66},{3,67},{4,68},{5,69},{6,70},{7,71},{8,72},{9,... | collective-permute-start | bytes 1966088 | tf_op jit(solution)/shard_map/ppermute | solution.py:69
  24.6 6.3 %collective-permute-start.8 = (bf16[2,8,10,128]{3,2,1,0:T(8,128)(2,1)S(1)}, bf16[2,8,10,128]{3,2,1,0:T(8,128)(2,1)S(1)}, u32[]{:S(2)}, u32[]{:S(2)}) collective-permute-start(bf16[2,8,10,128]{3,2,1,0:T(8,128)(2,1)S(1)} %pad_maximum_fusion.5), channel_id=1, source_target_pairs={{0,1},{1,2},{2,3},{4,5},{5,6},{6,7},{8,9},{9,10},{10,11},{12,13},{... | collective-permute-start | bytes 122888 | tf_op jit(solution)/shard_map/ppermute | solution.py:69
  28.4 5.3 %collective-permute-start.9 = (bf16[2,8,10,128]{3,2,1,0:T(8,128)(2,1)S(1)}, bf16[2,8,10,128]{3,2,1,0:T(8,128)(2,1)S(1)}, u32[]{:S(2)}, u32[]{:S(2)}) collective-permute-start(bf16[2,8,10,128]{3,2,1,0:T(8,128)(2,1)S(1)} %pad_maximum_fusion.6), channel_id=1, source_target_pairs={{1,0},{2,1},{3,2},{5,4},{6,5},{7,6},{9,8},{10,9},{11,10},{13,12},{... | collective-permute-start | bytes 122888 | tf_op jit(solution)/shard_map/ppermute | solution.py:69
  30.9 20.6 %copy-start.1 = (f32[2]{0:T(128)S(1)}, f32[2]{0:T(128)}, u32[]{:S(2)}) copy-start(f32[2]{0:T(128)} %constant.91.clone) | copy-start | bytes 28
  33.7 12.7 %collective-permute-start.13 = (bf16[4,2,2,3,16,512]{5,4,3,2,1,0:T(8,128)(2,1)S(1)}, bf16[4,2,2,3,16,512]{5,4,3,2,1,0:T(8,128)(2,1)S(1)}, u32[]{:S(2)}, u32[]{:S(2)}) collective-permute-start(bf16[4,2,2,3,16,512]{5,4,3,2,1,0:T(8,128)(2,1)S(1)} %pad_maximum_fusion.p0), channel_id=1, source_target_pairs={{0,16},{1,17},{2,18},{3,19},{4,20},{5,21},{6,22},{7,23},{8,24},{9,... | collective-permute-start | bytes 2359304 | tf_op jit(solution)/shard_map/ppermute | solution.py:69
  36.6 6.5 %collective-permute-start.12 = (bf16[800,128]{1,0:T(8,128)(2,1)S(1)}, bf16[800,128]{1,0:T(8,128)(2,1)S(1)}, u32[]{:S(2)}, u32[]{:S(2)}) collective-permute-start(bf16[800,128]{1,0:T(8,128)(2,1)S(1)} %get-tuple-element.23), channel_id=1, source_target_pairs={{0,64},{1,65},{2,66},{3,67},{4,68},{5,69},{6,70},{7,71},{8,72},{9,... | collective-permute-start | bytes 614408 | tf_op jit(solution)/shard_map/ppermute | solution.py:69
  39.0 15.7 %collective-permute-start.17 = (bf16[4,2,2,3,16,512]{5,4,3,2,1,0:T(8,128)(2,1)S(1)}, bf16[4,2,2,3,16,512]{5,4,3,2,1,0:T(8,128)(2,1)S(1)}, u32[]{:S(2)}, u32[]{:S(2)}) collective-permute-start(bf16[4,2,2,3,16,512]{5,4,3,2,1,0:T(8,128)(2,1)S(1)} %pad_maximum_fusion.p0), channel_id=1, source_target_pairs={{0,24},{1,25},{2,26},{3,27},{4,28},{5,29},{6,30},{7,31},{8,0},{9,1... | collective-permute-start | bytes 2359304 | tf_op jit(solution)/shard_map/ppermute | solution.py:69
  39.8 15.0 %collective-permute-start.18 = (bf16[4,2,2,3,16,512]{5,4,3,2,1,0:T(8,128)(2,1)S(1)}, bf16[4,2,2,3,16,512]{5,4,3,2,1,0:T(8,128)(2,1)S(1)}, u32[]{:S(2)}, u32[]{:S(2)}) collective-permute-start(bf16[4,2,2,3,16,512]{5,4,3,2,1,0:T(8,128)(2,1)S(1)} %pad_maximum_fusion.p0), channel_id=1, source_target_pairs={{0,8},{1,9},{2,10},{3,11},{4,12},{5,13},{6,14},{7,15},{8,16},{9,17... | collective-permute-start | bytes 2359304 | tf_op jit(solution)/shard_map/ppermute | solution.py:69
  46.4 6.7 %collective-permute-start.14 = (bf16[2560,128]{1,0:T(8,128)(2,1)S(1)}, bf16[2560,128]{1,0:T(8,128)(2,1)S(1)}, u32[]{:S(2)}, u32[]{:S(2)}) collective-permute-start(bf16[2560,128]{1,0:T(8,128)(2,1)S(1)} %collective-permute-done.11.m2), channel_id=1, source_target_pairs={{0,32},{1,33},{2,34},{3,35},{4,36},{5,37},{6,38},{7,39},{8,40},{9,... | collective-permute-start | bytes 1966088 | tf_op jit(solution)/shard_map/ppermute | solution.py:69
  50.9 1.9 %collective-permute-start.15 = (bf16[800,128]{1,0:T(8,128)(2,1)S(1)}, bf16[800,128]{1,0:T(8,128)(2,1)S(1)}, u32[]{:S(2)}, u32[]{:S(2)}) collective-permute-start(bf16[800,128]{1,0:T(8,128)(2,1)S(1)} %get-tuple-element.26.r0), channel_id=1, source_target_pairs={{0,32},{1,33},{2,34},{3,35},{4,36},{5,37},{6,38},{7,39},{8,40},{9,... | collective-permute-start | bytes 614408 | tf_op jit(solution)/shard_map/ppermute | solution.py:69
  51.0 2.1 %collective-permute-start.16 = (bf16[800,128]{1,0:T(8,128)(2,1)S(1)}, bf16[800,128]{1,0:T(8,128)(2,1)S(1)}, u32[]{:S(2)}, u32[]{:S(2)}) collective-permute-start(bf16[800,128]{1,0:T(8,128)(2,1)S(1)} %collective-permute-done.12.r2), channel_id=1, source_target_pairs={{0,32},{1,33},{2,34},{3,35},{4,36},{5,37},{6,38},{7,39},{8,40},{9,... | collective-permute-start | bytes 614408 | tf_op jit(solution)/shard_map/ppermute | solution.py:69
  85.8 7.4 %collective-permute-start.19 = (bf16[2,2,8,32,512]{4,3,2,1,0:T(8,128)(2,1)S(1)}, bf16[2,2,8,32,512]{4,3,2,1,0:T(8,128)(2,1)S(1)}, u32[]{:S(2)}, u32[]{:S(2)}) collective-permute-start(bf16[2,2,8,32,512]{4,3,2,1,0:T(8,128)(2,1)S(1)} %get-tuple-element.30), channel_id=1, source_target_pairs={{0,32},{1,33},{2,34},{3,35},{4,36},{5,37},{6,38},{7,39},{8,40},{9,... | collective-permute-start | bytes 3145736 | tf_op jit(solution)/shard_map/ppermute | solution.py:69

commit v7 on v6

--- a/solution.py
+++ b/solution.py
@@ -168,7 +168,7 @@
         out_shape=jax.ShapeDtypeStruct((4, 2, 1600, 128), BF16),
         in_specs=[pl.BlockSpec(memory_space=pltpu.SMEM)] + [vmem] * 8,
         out_specs=vmem,
-        scratch_shapes=[pltpu.VMEM((4, 320, 128), F32)],
+        scratch_shapes=[pltpu.VMEM((4, 328, 128), F32)],
         compiler_params=pltpu.CompilerParams(vmem_limit_bytes=16 * 2**20),
         name="pack_cells",
     )(position, *mains, *rims)
@@ -287,7 +287,7 @@
         for u in range(8):
             for slot, out in ((0, kept_ref), (1, sent_ref)):
                 own = u * 8 + slot * 4
-                total = jnp.concatenate([rows[own + v] for v in range(4)], axis=1)
+                total = jnp.concatenate([rows[own + v, 0:32, :] for v in range(4)], axis=1)
                 out[i // 2, i % 2, u] = total.astype(out.dtype)
         return 0
 
@@ -308,7 +308,7 @@
             pltpu.VMEM((4, 6, 10, 32, 128), F32),
             pltpu.VMEM((4, 1024, 256), BF16),
             pltpu.VMEM((2, 1024, 512), F32),
-            pltpu.VMEM((64, 32, 128), F32),
+            pltpu.VMEM((64, 40, 128), F32),
         ],
         compiler_params=pltpu.CompilerParams(vmem_limit_bytes=32 * 2**20),
         name="gated_block",

time: 95.4 us -> 95.4 us (level)
  no operation moved by 1% of the time
where the time goes in v7:
time: 95.4 us; the launch traced here: 95.1 us
  starting transfers between devices  39.4 us (41%)
  Pallas kernels  33.5 us (35%)
  waiting for transfers between devices  12.6 us (13%)
  other arithmetic  4.6 us (5%)
  local copies, waits for them, and re-layouts  4.55 us (5%)
    ppermute x20, starting transfers between devices, send(): return lax.ppermute(value, BOTH, pairs)  39.4 us
    pallas_call x1, Pallas kernels, run_block(): pl.pallas_call(block_kernel, out_shape=[jax.ShapeDtypeStruct((2, 2, 8, 32...  31 us
    ppermute x20, waiting for transfers between devices, send(): return lax.ppermute(value, BOTH, pairs)  12.6 us
  transfers between devices with their start and end apart: 20, of which 6 were waited for; matrix products, arithmetic and copies ran while one was open for 6% of the time, Pallas kernels for 3%

profile of v7, /device:TPU:1, one launch (start us, length us, event | category | flops | bytes accessed | tf_op | source)
XLA Modules:
  0.0 95.1 jit_solution(4980524387640058587)
XLA Ops:
  0.0 0.0 copy-start
  0.0 0.8 copy_multiply_fusion
  0.8 0.7 fusion.5
  1.5 2.1 %collective-permute-start = (bf16[3,16,512]{2,1,0:T(8,128)(2,1)S(1)}, bf16[3,16,512]{2,1,0:T(8,128)(2,1)S(1)}, u32[]{:S(2)}, u32[]{:S(2)}) collective-permute-start(bf16[3,16,512]{2,1,0:T(8,128)(2,1)S(1)} %get-tuple-element.54), channel_id=1, source_target_pairs={{0,4},{1,5},{2,6},{3,7},{4,0},{5,1},{6,2},{7,3},{8,12},{9,13},{10,... | collective-permute-start | bytes 147464 | tf_op jit(solution)/shard_map/ppermute | solution.py:69
  3.7 1.8 %collective-permute-start.2 = (bf16[3,16,512]{2,1,0:T(8,128)(2,1)S(1)}, bf16[3,16,512]{2,1,0:T(8,128)(2,1)S(1)}, u32[]{:S(2)}, u32[]{:S(2)}) collective-permute-start(bf16[3,16,512]{2,1,0:T(8,128)(2,1)S(1)} %get-tuple-element.54), channel_id=1, source_target_pairs={{0,68},{1,69},{2,70},{3,71},{4,64},{5,65},{6,66},{7,67},{8,76},{9,... | collective-permute-start | bytes 147464 | tf_op jit(solution)/shard_map/ppermute | solution.py:69
  5.5 1.0 %fusion.2 = bf16[3,9,2,512]{3,2,1,0:T(2,128)(2,1)S(1)} fusion(f32[3,9,2,512]{3,2,1,0:T(2,128)} %bitcast.60, pred[]{:T(512)S(6)} %eq.8), kind=kLoop, calls=%fused_computation.20 | loop fusion | flops 27648 | bytes 165889 | tf_op jit(solution)/shard_map/convert_element_type | solution.py:329
  6.6 0.7 collective-permute-start.1
  7.3 1.4 %copy.28 = bf16[2,8,1,8,30,128]{5,4,1,0,3,2:T(8,128)(2,1)S(1)} copy(bf16[2,8,1,8,30,128]{5,3,4,2,1,0:T(8,128)(2,1)} %param.5) | data formatting | bytes 1966080 | tf_op args[0]
  8.7 0.7 slice_bitcast_fusion.1
  9.4 2.7 %collective-permute-start.6 = (bf16[2,8,30,128]{3,2,1,0:T(8,128)(2,1)}, bf16[2,8,30,128]{3,2,1,0:T(8,128)(2,1)S(1)}, u32[]{:S(2)}, u32[]{:S(2)}) collective-permute-start(bf16[2,8,30,128]{3,2,1,0:T(8,128)(2,1)} %get-tuple-element.39), channel_id=1, source_target_pairs={{0,4},{1,5},{2,6},{3,7},{4,8},{5,9},{6,10},{7,11},{8,12},{9,13},{1... | collective-permute-start | bytes 368648 | tf_op jit(solution)/shard_map/ppermute | solution.py:69
  12.1 1.3 %collective-permute-start.7 = (bf16[2,8,30,128]{3,2,1,0:T(8,128)(2,1)S(1)}, bf16[2,8,30,128]{3,2,1,0:T(8,128)(2,1)S(1)}, u32[]{:S(2)}, u32[]{:S(2)}) collective-permute-start(bf16[2,8,30,128]{3,2,1,0:T(8,128)(2,1)S(1)} %get-tuple-element.40), channel_id=1, source_target_pairs={{4,0},{5,1},{6,2},{7,3},{8,4},{9,5},{10,6},{11,7},{12,8},{13,9},{1... | collective-permute-start | bytes 368648 | tf_op jit(solution)/shard_map/ppermute | solution.py:69
  13.4 0.0 copy-done
  13.5 0.1 reshape.45
  13.7 0.1 stack.81.pos_ref
  13.8 0.0 collective-permute-done.1
  13.8 0.0 collective-permute-done
  13.8 0.0 collective-permute-done.2
  13.8 5.0 %collective-permute-start.3 = (bf16[2,2,3,16,512]{4,3,2,1,0:T(8,128)(2,1)S(1)}, bf16[2,2,3,16,512]{4,3,2,1,0:T(8,128)(2,1)S(1)}, u32[]{:S(2)}, u32[]{:S(2)}) collective-permute-start(bf16[2,2,3,16,512]{4,3,2,1,0:T(8,128)(2,1)S(1)} %bitcast.54), channel_id=1, source_target_pairs={{0,3},{1,0},{2,1},{3,2},{4,7},{5,4},{6,5},{7,6},{8,11},{9,8},{10,9... | collective-permute-start | bytes 589832 | tf_op jit(solution)/shard_map/ppermute | solution.py:69
  18.8 0.3 collective-permute-start.4
  19.1 0.7 collective-permute-start.5
  19.8 0.1 fusion.8
  20.0 0.4 pad_dynamic-slice_fusion
  20.4 0.1 copy.19
  20.5 0.1 copy.22
  20.6 0.1 add_add_fusion.2
  20.6 0.0 collective-permute-done.6.above
  20.6 1.2 %collective-permute-start.10 = (bf16[2560,128]{1,0:T(8,128)(2,1)S(1)}, bf16[2560,128]{1,0:T(8,128)(2,1)S(1)}, u32[]{:S(2)}, u32[]{:S(2)}) collective-permute-start(bf16[2560,128]{1,0:T(8,128)(2,1)S(1)} %bitcast.48), channel_id=1, source_target_pairs={{0,32},{1,33},{2,34},{3,35},{4,36},{5,37},{6,38},{7,39},{8,40},{9,... | collective-permute-start | bytes 1966088 | tf_op jit(solution)/shard_map/ppermute | solution.py:69
  21.9 0.0 collective-permute-done.7.below
  21.9 2.5 %collective-permute-start.11 = (bf16[2560,128]{1,0:T(8,128)(2,1)S(1)}, bf16[2560,128]{1,0:T(8,128)(2,1)S(1)}, u32[]{:S(2)}, u32[]{:S(2)}) collective-permute-start(bf16[2560,128]{1,0:T(8,128)(2,1)S(1)} %bitcast.59), channel_id=1, source_target_pairs={{0,64},{1,65},{2,66},{3,67},{4,68},{5,69},{6,70},{7,71},{8,72},{9,... | collective-permute-start | bytes 1966088 | tf_op jit(solution)/shard_map/ppermute | solution.py:69
  24.5 0.0 collective-permute-done.3
  24.6 3.9 %collective-permute-start.8 = (bf16[2,8,10,128]{3,2,1,0:T(8,128)(2,1)S(1)}, bf16[2,8,10,128]{3,2,1,0:T(8,128)(2,1)S(1)}, u32[]{:S(2)}, u32[]{:S(2)}) collective-permute-start(bf16[2,8,10,128]{3,2,1,0:T(8,128)(2,1)S(1)} %pad_maximum_fusion.5), channel_id=1, source_target_pairs={{0,1},{1,2},{2,3},{4,5},{5,6},{6,7},{8,9},{9,10},{10,11},{12,13},{... | collective-permute-start | bytes 122888 | tf_op jit(solution)/shard_map/ppermute | solution.py:69
  28.4 0.0 collective-permute-done.4
  28.4 1.3 %collective-permute-start.9 = (bf16[2,8,10,128]{3,2,1,0:T(8,128)(2,1)S(1)}, bf16[2,8,10,128]{3,2,1,0:T(8,128)(2,1)S(1)}, u32[]{:S(2)}, u32[]{:S(2)}) collective-permute-start(bf16[2,8,10,128]{3,2,1,0:T(8,128)(2,1)S(1)} %pad_maximum_fusion.6), channel_id=1, source_target_pairs={{1,0},{2,1},{3,2},{5,4},{6,5},{7,6},{9,8},{10,9},{11,10},{13,12},{... | collective-permute-start | bytes 122888 | tf_op jit(solution)/shard_map/ppermute | solution.py:69
  29.7 0.0 collective-permute-done.5
  29.7 1.1 %pad_maximum_fusion.p0 = bf16[4,2,2,3,16,512]{5,4,3,2,1,0:T(8,128)(2,1)S(1)} fusion(bf16[1,2,2,3,16,512]{5,4,3,2,1,0:T(8,128)(2,1)} %bitcast.21, bf16[1,2,2,3,16,512]{5,4,3,2,1,0:T(8,128)(2,1)} %bitcast.20, bf16[1,2,2,3,16,512]{5,4,3,2,1,0:T(8,128)(2,1)S(1)} %bitcast.67, bf16[1,2,2,3,16,512]{5,4,3,2,1,0:T(8,128)(2,1)S(1)} %bitcast.57), kind=kLoop, calls=%fused_computation.6 | loop fusion | flops 1179648 | bytes 1572864 | tf_op jit(solution)/shard_map/stack | solution.py:350
  30.9 0.0 copy-start.1
  30.9 0.0 collective-permute-done.8.left
  30.9 2.8 %collective-permute-done.9.right = bf16[2,8,10,128]{3,2,1,0:T(8,128)(2,1)S(1)} collective-permute-done((bf16[2,8,10,128]{3,2,1,0:T(8,128)(2,1)S(1)}, bf16[2,8,10,128]{3,2,1,0:T(8,128)(2,1)S(1)}, u32[]{:S(2)}, u32[]{:S(2)}) %collective-permute-start.9) | collective-permute-done | bytes 40992 | tf_op jit(solution)/shard_map/ppermute | solution.py:69
  33.7 0.0 collective-permute-done.10.m1
  33.7 2.0 %collective-permute-start.13 = (bf16[4,2,2,3,16,512]{5,4,3,2,1,0:T(8,128)(2,1)S(1)}, bf16[4,2,2,3,16,512]{5,4,3,2,1,0:T(8,128)(2,1)S(1)}, u32[]{:S(2)}, u32[]{:S(2)}) collective-permute-start(bf16[4,2,2,3,16,512]{5,4,3,2,1,0:T(8,128)(2,1)S(1)} %pad_maximum_fusion.p0), channel_id=1, source_target_pairs={{0,16},{1,17},{2,18},{3,19},{4,20},{5,21},{6,22},{7,23},{8,24},{9,... | collective-permute-start | bytes 2359304 | tf_op jit(solution)/shard_map/ppermute | solution.py:69
  35.8 0.8 pack_rims.1
  36.6 2.4 %collective-permute-start.12 = (bf16[800,128]{1,0:T(8,128)(2,1)S(1)}, bf16[800,128]{1,0:T(8,128)(2,1)S(1)}, u32[]{:S(2)}, u32[]{:S(2)}) collective-permute-start(bf16[800,128]{1,0:T(8,128)(2,1)S(1)} %get-tuple-element.23), channel_id=1, source_target_pairs={{0,64},{1,65},{2,66},{3,67},{4,68},{5,69},{6,70},{7,71},{8,72},{9,... | collective-permute-start | bytes 614408 | tf_op jit(solution)/shard_map/ppermute | solution.py:69
  39.0 0.7 collective-permute-start.17
  39.8 0.7 collective-permute-start.18
  40.5 0.0 collective-permute-done.11.m2
  40.5 2.6 %collective-permute-done.12.r2 = bf16[800,128]{1,0:T(8,128)(2,1)S(1)} collective-permute-done((bf16[800,128]{1,0:T(8,128)(2,1)S(1)}, bf16[800,128]{1,0:T(8,128)(2,1)S(1)}, u32[]{:S(2)}, u32[]{:S(2)}) %collective-permute-start.12) | collective-permute-done | bytes 204832 | tf_op jit(solution)/shard_map/ppermute | solution.py:69
  43.1 3.3 %collective-permute-done.13.p2 = bf16[4,2,2,3,16,512]{5,4,3,2,1,0:T(8,128)(2,1)S(1)} collective-permute-done((bf16[4,2,2,3,16,512]{5,4,3,2,1,0:T(8,128)(2,1)S(1)}, bf16[4,2,2,3,16,512]{5,4,3,2,1,0:T(8,128)(2,1)S(1)}, u32[]{:S(2)}, u32[]{:S(2)}) %collective-permute-start.13) | collective-permute-done | bytes 786464 | tf_op jit(solution)/shard_map/ppermute | solution.py:69
  46.4 4.4 %collective-permute-start.14 = (bf16[2560,128]{1,0:T(8,128)(2,1)S(1)}, bf16[2560,128]{1,0:T(8,128)(2,1)S(1)}, u32[]{:S(2)}, u32[]{:S(2)}) collective-permute-start(bf16[2560,128]{1,0:T(8,128)(2,1)S(1)} %collective-permute-done.11.m2), channel_id=1, source_target_pairs={{0,32},{1,33},{2,34},{3,35},{4,36},{5,37},{6,38},{7,39},{8,40},{9,... | collective-permute-start | bytes 1966088 | tf_op jit(solution)/shard_map/ppermute | solution.py:69
  50.9 0.1 collective-permute-start.15
  51.0 0.5 collective-permute-start.16
  51.5 0.0 copy-done.1
  51.5 0.1 broadcast_multiply_fusion.k_ref
  51.6 1.2 %collective-permute-done.15.r1 = bf16[800,128]{1,0:T(8,128)(2,1)S(1)} collective-permute-done((bf16[800,128]{1,0:T(8,128)(2,1)S(1)}, bf16[800,128]{1,0:T(8,128)(2,1)S(1)}, u32[]{:S(2)}, u32[]{:S(2)}) %collective-permute-start.15) | collective-permute-done | bytes 204832 | tf_op jit(solution)/shard_map/ppermute | solution.py:69
  52.8 0.3 collective-permute-done.16.r3
  53.1 0.0 collective-permute-done.14.m3
  53.1 1.7 %pack_cells.1.x_ref = bf16[4,2,1600,128]{3,2,1,0:T(8,128)(2,1)S(1)} custom-call(s32[5]{0:T(128)S(1)} %stack.81.pos_ref, bf16[2560,128]{1,0:T(8,128)(2,1)S(1)} %bitcast.49, bf16[2560,128]{1,0:T(8,128)(2,1)S(1)} %collective-permute-done.10.m1, bf16[2560,128]{1,0:T(8,128)(2,1)S(1)} %collective-permute-done.11.m2, ...), custom_call_target="tpu_custom_call" | custom-call | tf_op jit(solution)/shard_map/pack_cells/pallas_call | solution.py:166
  54.8 0.0 collective-permute-done.17.p1
  54.8 0.0 collective-permute-done.18.p3
  54.8 31.0 %gated_block.1 = (f32[2,2,8,32,512]{4,3,2,1,0:T(8,128)S(1)}, bf16[2,2,8,32,512]{4,3,2,1,0:T(8,128)(2,1)S(1)}) custom-call(s32[5]{0:T(128)S(1)} %stack.81.pos_ref, bf16[4,2,1600,128]{3,2,1,0:T(8,128)(2,1)S(1)} %pack_cells.1.x_ref, bf16[4,2,2,3,16,512]{5,4,3,2,1,0:T(8,128)(2,1)S(1)} %pad_maximum_fusion.p0, ...), custom_call_target="tpu_custom_call" | custom-call | tf_op jit(solution)/shard_map/gated_block/pallas_call | solution.py:299
  85.8 5.1 %collective-permute-start.19 = (bf16[2,2,8,32,512]{4,3,2,1,0:T(8,128)(2,1)S(1)}, bf16[2,2,8,32,512]{4,3,2,1,0:T(8,128)(2,1)S(1)}, u32[]{:S(2)}, u32[]{:S(2)}) collective-permute-start(bf16[2,2,8,32,512]{4,3,2,1,0:T(8,128)(2,1)S(1)} %get-tuple-element.30), channel_id=1, source_target_pairs={{0,32},{1,33},{2,34},{3,35},{4,36},{5,37},{6,38},{7,39},{8,40},{9,... | collective-permute-start | bytes 3145736 | tf_op jit(solution)/shard_map/ppermute | solution.py:69
  90.9 2.3 %collective-permute-done.19 = bf16[2,2,8,32,512]{4,3,2,1,0:T(8,128)(2,1)S(1)} collective-permute-done((bf16[2,2,8,32,512]{4,3,2,1,0:T(8,128)(2,1)S(1)}, bf16[2,2,8,32,512]{4,3,2,1,0:T(8,128)(2,1)S(1)}, u32[]{:S(2)}, u32[]{:S(2)}) %collective-permute-start.19) | collective-permute-done | bytes 1048608 | tf_op jit(solution)/shard_map/ppermute | solution.py:69
  93.2 0.4 fusion.1
  93.6 1.5 %copy.23 = bf16[2,2,1,8,30,512]{5,3,4,2,1,0:T(8,128)(2,1)} copy(bf16[2,2,1,8,30,512]{5,4,3,1,0,2:T(8,128)(2,1)S(1)} %fusion.1) | data formatting | bytes 1966080 | tf_op jit(solution)/shard_map/convert_element_type | solution.py:365
  (23 shorter events, 0.5 us)
Async XLA Ops:
  0.0 13.4 %copy-start = (f32[3,3,3,2,512]{4,3,2,1,0:T(2,128)S(1)}, f32[3,3,3,2,512]{4,3,2,1,0:T(2,128)}, u32[]{:S(2)}) copy-start(f32[3,3,3,2,512]{4,3,2,1,0:T(2,128)} %param.7) | copy-start | bytes 331780
  1.5 12.2 %collective-permute-start = (bf16[3,16,512]{2,1,0:T(8,128)(2,1)S(1)}, bf16[3,16,512]{2,1,0:T(8,128)(2,1)S(1)}, u32[]{:S(2)}, u32[]{:S(2)}) collective-permute-start(bf16[3,16,512]{2,1,0:T(8,128)(2,1)S(1)} %get-tuple-element.54), channel_id=1, source_target_pairs={{0,4},{1,5},{2,6},{3,7},{4,0},{5,1},{6,2},{7,3},{8,12},{9,13},{10,... | collective-permute-start | bytes 147464 | tf_op jit(solution)/shard_map/ppermute | solution.py:69
  3.7 10.1 %collective-permute-start.2 = (bf16[3,16,512]{2,1,0:T(8,128)(2,1)S(1)}, bf16[3,16,512]{2,1,0:T(8,128)(2,1)S(1)}, u32[]{:S(2)}, u32[]{:S(2)}) collective-permute-start(bf16[3,16,512]{2,1,0:T(8,128)(2,1)S(1)} %get-tuple-element.54), channel_id=1, source_target_pairs={{0,68},{1,69},{2,70},{3,71},{4,64},{5,65},{6,66},{7,67},{8,76},{9,... | collective-permute-start | bytes 147464 | tf_op jit(solution)/shard_map/ppermute | solution.py:69
  6.6 7.2 %collective-permute-start.1 = (bf16[102,512]{1,0:T(8,128)(2,1)S(1)}, bf16[102,512]{1,0:T(8,128)(2,1)S(1)}, u32[]{:S(2)}, u32[]{:S(2)}) collective-permute-start(bf16[102,512]{1,0:T(8,128)(2,1)S(1)} %pad_maximum_fusion.3), channel_id=1, source_target_pairs={{0,64},{1,65},{2,66},{3,67},{4,68},{5,69},{6,70},{7,71},{8,72},{9,... | collective-permute-start | bytes 313352 | tf_op jit(solution)/shard_map/ppermute | solution.py:69
  9.4 11.3 %collective-permute-start.6 = (bf16[2,8,30,128]{3,2,1,0:T(8,128)(2,1)}, bf16[2,8,30,128]{3,2,1,0:T(8,128)(2,1)S(1)}, u32[]{:S(2)}, u32[]{:S(2)}) collective-permute-start(bf16[2,8,30,128]{3,2,1,0:T(8,128)(2,1)} %get-tuple-element.39), channel_id=1, source_target_pairs={{0,4},{1,5},{2,6},{3,7},{4,8},{5,9},{6,10},{7,11},{8,12},{9,13},{1... | collective-permute-start | bytes 368648 | tf_op jit(solution)/shard_map/ppermute | solution.py:69
  12.1 9.8 %collective-permute-start.7 = (bf16[2,8,30,128]{3,2,1,0:T(8,128)(2,1)S(1)}, bf16[2,8,30,128]{3,2,1,0:T(8,128)(2,1)S(1)}, u32[]{:S(2)}, u32[]{:S(2)}) collective-permute-start(bf16[2,8,30,128]{3,2,1,0:T(8,128)(2,1)S(1)} %get-tuple-element.40), channel_id=1, source_target_pairs={{4,0},{5,1},{6,2},{7,3},{8,4},{9,5},{10,6},{11,7},{12,8},{13,9},{1... | collective-permute-start | bytes 368648 | tf_op jit(solution)/shard_map/ppermute | solution.py:69
  13.8 10.7 %collective-permute-start.3 = (bf16[2,2,3,16,512]{4,3,2,1,0:T(8,128)(2,1)S(1)}, bf16[2,2,3,16,512]{4,3,2,1,0:T(8,128)(2,1)S(1)}, u32[]{:S(2)}, u32[]{:S(2)}) collective-permute-start(bf16[2,2,3,16,512]{4,3,2,1,0:T(8,128)(2,1)S(1)} %bitcast.54), channel_id=1, source_target_pairs={{0,3},{1,0},{2,1},{3,2},{4,7},{5,4},{6,5},{7,6},{8,11},{9,8},{10,9... | collective-permute-start | bytes 589832 | tf_op jit(solution)/shard_map/ppermute | solution.py:69
  18.8 9.6 %collective-permute-start.4 = (bf16[2,2,3,16,512]{4,3,2,1,0:T(8,128)(2,1)S(1)}, bf16[2,2,3,16,512]{4,3,2,1,0:T(8,128)(2,1)}, u32[]{:S(2)}, u32[]{:S(2)}) collective-permute-start(bf16[2,2,3,16,512]{4,3,2,1,0:T(8,128)(2,1)S(1)} %bitcast.55), channel_id=1, source_target_pairs={{0,2},{1,3},{2,0},{3,1},{4,6},{5,7},{6,4},{7,5},{8,10},{9,11},{10,... | collective-permute-start | bytes 589832 | tf_op jit(solution)/shard_map/ppermute | solution.py:69
  19.1 10.6 %collective-permute-start.5 = (bf16[2,2,3,16,512]{4,3,2,1,0:T(8,128)(2,1)S(1)}, bf16[2,2,3,16,512]{4,3,2,1,0:T(8,128)(2,1)}, u32[]{:S(2)}, u32[]{:S(2)}) collective-permute-start(bf16[2,2,3,16,512]{4,3,2,1,0:T(8,128)(2,1)S(1)} %bitcast.56), channel_id=1, source_target_pairs={{0,1},{1,2},{2,3},{3,0},{4,5},{5,6},{6,7},{7,4},{8,9},{9,10},{10,1... | collective-permute-start | bytes 589832 | tf_op jit(solution)/shard_map/ppermute | solution.py:69
  20.6 13.1 %collective-permute-start.10 = (bf16[2560,128]{1,0:T(8,128)(2,1)S(1)}, bf16[2560,128]{1,0:T(8,128)(2,1)S(1)}, u32[]{:S(2)}, u32[]{:S(2)}) collective-permute-start(bf16[2560,128]{1,0:T(8,128)(2,1)S(1)} %bitcast.48), channel_id=1, source_target_pairs={{0,32},{1,33},{2,34},{3,35},{4,36},{5,37},{6,38},{7,39},{8,40},{9,... | collective-permute-start | bytes 1966088 | tf_op jit(solution)/shard_map/ppermute | solution.py:69
  21.9 18.6 %collective-permute-start.11 = (bf16[2560,128]{1,0:T(8,128)(2,1)S(1)}, bf16[2560,128]{1,0:T(8,128)(2,1)S(1)}, u32[]{:S(2)}, u32[]{:S(2)}) collective-permute-start(bf16[2560,128]{1,0:T(8,128)(2,1)S(1)} %bitcast.59), channel_id=1, source_target_pairs={{0,64},{1,65},{2,66},{3,67},{4,68},{5,69},{6,70},{7,71},{8,72},{9,... | collective-permute-start | bytes 1966088 | tf_op jit(solution)/shard_map/ppermute | solution.py:69
  24.6 6.3 %collective-permute-start.8 = (bf16[2,8,10,128]{3,2,1,0:T(8,128)(2,1)S(1)}, bf16[2,8,10,128]{3,2,1,0:T(8,128)(2,1)S(1)}, u32[]{:S(2)}, u32[]{:S(2)}) collective-permute-start(bf16[2,8,10,128]{3,2,1,0:T(8,128)(2,1)S(1)} %pad_maximum_fusion.5), channel_id=1, source_target_pairs={{0,1},{1,2},{2,3},{4,5},{5,6},{6,7},{8,9},{9,10},{10,11},{12,13},{... | collective-permute-start | bytes 122888 | tf_op jit(solution)/shard_map/ppermute | solution.py:69
  28.4 5.3 %collective-permute-start.9 = (bf16[2,8,10,128]{3,2,1,0:T(8,128)(2,1)S(1)}, bf16[2,8,10,128]{3,2,1,0:T(8,128)(2,1)S(1)}, u32[]{:S(2)}, u32[]{:S(2)}) collective-permute-start(bf16[2,8,10,128]{3,2,1,0:T(8,128)(2,1)S(1)} %pad_maximum_fusion.6), channel_id=1, source_target_pairs={{1,0},{2,1},{3,2},{5,4},{6,5},{7,6},{9,8},{10,9},{11,10},{13,12},{... | collective-permute-start | bytes 122888 | tf_op jit(solution)/shard_map/ppermute | solution.py:69
  30.9 20.6 %copy-start.1 = (f32[2]{0:T(128)S(1)}, f32[2]{0:T(128)}, u32[]{:S(2)}) copy-start(f32[2]{0:T(128)} %constant.91.clone) | copy-start | bytes 28
  33.7 12.7 %collective-permute-start.13 = (bf16[4,2,2,3,16,512]{5,4,3,2,1,0:T(8,128)(2,1)S(1)}, bf16[4,2,2,3,16,512]{5,4,3,2,1,0:T(8,128)(2,1)S(1)}, u32[]{:S(2)}, u32[]{:S(2)}) collective-permute-start(bf16[4,2,2,3,16,512]{5,4,3,2,1,0:T(8,128)(2,1)S(1)} %pad_maximum_fusion.p0), channel_id=1, source_target_pairs={{0,16},{1,17},{2,18},{3,19},{4,20},{5,21},{6,22},{7,23},{8,24},{9,... | collective-permute-start | bytes 2359304 | tf_op jit(solution)/shard_map/ppermute | solution.py:69
  36.6 6.5 %collective-permute-start.12 = (bf16[800,128]{1,0:T(8,128)(2,1)S(1)}, bf16[800,128]{1,0:T(8,128)(2,1)S(1)}, u32[]{:S(2)}, u32[]{:S(2)}) collective-permute-start(bf16[800,128]{1,0:T(8,128)(2,1)S(1)} %get-tuple-element.23), channel_id=1, source_target_pairs={{0,64},{1,65},{2,66},{3,67},{4,68},{5,69},{6,70},{7,71},{8,72},{9,... | collective-permute-start | bytes 614408 | tf_op jit(solution)/shard_map/ppermute | solution.py:69
  39.0 15.7 %collective-permute-start.17 = (bf16[4,2,2,3,16,512]{5,4,3,2,1,0:T(8,128)(2,1)S(1)}, bf16[4,2,2,3,16,512]{5,4,3,2,1,0:T(8,128)(2,1)S(1)}, u32[]{:S(2)}, u32[]{:S(2)}) collective-permute-start(bf16[4,2,2,3,16,512]{5,4,3,2,1,0:T(8,128)(2,1)S(1)} %pad_maximum_fusion.p0), channel_id=1, source_target_pairs={{0,24},{1,25},{2,26},{3,27},{4,28},{5,29},{6,30},{7,31},{8,0},{9,1... | collective-permute-start | bytes 2359304 | tf_op jit(solution)/shard_map/ppermute | solution.py:69
  39.8 15.0 %collective-permute-start.18 = (bf16[4,2,2,3,16,512]{5,4,3,2,1,0:T(8,128)(2,1)S(1)}, bf16[4,2,2,3,16,512]{5,4,3,2,1,0:T(8,128)(2,1)S(1)}, u32[]{:S(2)}, u32[]{:S(2)}) collective-permute-start(bf16[4,2,2,3,16,512]{5,4,3,2,1,0:T(8,128)(2,1)S(1)} %pad_maximum_fusion.p0), channel_id=1, source_target_pairs={{0,8},{1,9},{2,10},{3,11},{4,12},{5,13},{6,14},{7,15},{8,16},{9,17... | collective-permute-start | bytes 2359304 | tf_op jit(solution)/shard_map/ppermute | solution.py:69
  46.4 6.7 %collective-permute-start.14 = (bf16[2560,128]{1,0:T(8,128)(2,1)S(1)}, bf16[2560,128]{1,0:T(8,128)(2,1)S(1)}, u32[]{:S(2)}, u32[]{:S(2)}) collective-permute-start(bf16[2560,128]{1,0:T(8,128)(2,1)S(1)} %collective-permute-done.11.m2), channel_id=1, source_target_pairs={{0,32},{1,33},{2,34},{3,35},{4,36},{5,37},{6,38},{7,39},{8,40},{9,... | collective-permute-start | bytes 1966088 | tf_op jit(solution)/shard_map/ppermute | solution.py:69
  50.9 1.9 %collective-permute-start.15 = (bf16[800,128]{1,0:T(8,128)(2,1)S(1)}, bf16[800,128]{1,0:T(8,128)(2,1)S(1)}, u32[]{:S(2)}, u32[]{:S(2)}) collective-permute-start(bf16[800,128]{1,0:T(8,128)(2,1)S(1)} %get-tuple-element.26.r0), channel_id=1, source_target_pairs={{0,32},{1,33},{2,34},{3,35},{4,36},{5,37},{6,38},{7,39},{8,40},{9,... | collective-permute-start | bytes 614408 | tf_op jit(solution)/shard_map/ppermute | solution.py:69
  51.0 2.1 %collective-permute-start.16 = (bf16[800,128]{1,0:T(8,128)(2,1)S(1)}, bf16[800,128]{1,0:T(8,128)(2,1)S(1)}, u32[]{:S(2)}, u32[]{:S(2)}) collective-permute-start(bf16[800,128]{1,0:T(8,128)(2,1)S(1)} %collective-permute-done.12.r2), channel_id=1, source_target_pairs={{0,32},{1,33},{2,34},{3,35},{4,36},{5,37},{6,38},{7,39},{8,40},{9,... | collective-permute-start | bytes 614408 | tf_op jit(solution)/shard_map/ppermute | solution.py:69
  85.8 7.4 %collective-permute-start.19 = (bf16[2,2,8,32,512]{4,3,2,1,0:T(8,128)(2,1)S(1)}, bf16[2,2,8,32,512]{4,3,2,1,0:T(8,128)(2,1)S(1)}, u32[]{:S(2)}, u32[]{:S(2)}) collective-permute-start(bf16[2,2,8,32,512]{4,3,2,1,0:T(8,128)(2,1)S(1)} %get-tuple-element.30), channel_id=1, source_target_pairs={{0,32},{1,33},{2,34},{3,35},{4,36},{5,37},{6,38},{7,39},{8,40},{9,... | collective-permute-start | bytes 3145736 | tf_op jit(solution)/shard_map/ppermute | solution.py:69
